TPU v7x, 32 devices: a whole 2x2x4 slice. The times are simulated.
32 devices in a mesh: groups: 2 (over y), seq: 4 (over z), head: 2 (over x), sub: 2 (over core).
Axes of the slice: x: 2, y: 2, z: 4, core: 2. Of those that a mesh axis runs over, the one named last changes fastest.
Arguments:
- hidden: bfloat16 [8, 4, 8192], P('groups', None, ('head', 'sub')), parts along dimension 0, may hold values from -2.5 to 2.5
- query: bfloat16 [8, 4, 64, 128], P('groups', None, ('head', 'sub')), parts along dimension 0, may hold values from -4096 to 4096
- key_new: bfloat16 [8, 4, 8, 128], P('groups', None, ('head', 'sub')), parts along dimension 0, may hold values from -16 to 16
- value_new: bfloat16 [8, 4, 8, 128], P('groups', None, ('head', 'sub')), parts along dimension 0, may hold values from -12 to 12
- kv_cache: bfloat16 [2, 8, 1024, 8, 128], P(None, 'groups', 'seq', ('head', 'sub')), parts along dimension 1, may hold values from -127 to 127, as said below
- kv_scale: float32 [2, 8, 8, 8], P(None, 'groups', ('head', 'sub'), 'seq'), parts along dimension 1, may hold values from 0.004 to 0.032
- context_len: int32 [8], P('groups'), parts along dimension 0, may hold values from 128 to 1024
- attn_out_weight: bfloat16 [8192, 8192], P('seq', ('head', 'sub')), may hold values from -0.0625 to 0.0625
- norm_gain: float32 [8192], P(('head', 'sub')), may hold values from 0.5 to 1.5
- in_weight: bfloat16 [2, 8192, 16384], P(None, ('head', 'sub'), 'seq'), may hold values from -0.0625 to 0.0625
- conv_weight: bfloat16 [16384, 4], P(('seq', 'head', 'sub')), may hold values from -3 to 3
- conv_bias: float32 [16384], P(('seq', 'head', 'sub')), may hold values from -3 to 3
- conv_state: bfloat16 [8, 3, 16384], P('groups', None, ('seq', 'head', 'sub')), parts along dimension 0, may hold values from -6 to 6
- xproj_weight: bfloat16 [16384, 544], P(('seq', 'head', 'sub')), may hold values from -0.046875 to 0.046875
- dt_weight: bfloat16 [512, 16384], P(None, ('seq', 'head', 'sub')), may hold values from -0.25 to 0.25
- dt_bias: float32 [16384], P(('seq', 'head', 'sub')), may hold values from -3 to 0
- decay_rate: float32 [16384, 16], P(('seq', 'head', 'sub')), may hold values from 0.05 to 8
- skip_gain: float32 [16384], P(('seq', 'head', 'sub')), may hold values from 0.5 to 1.5
- ssm_state: float32 [8, 16384, 16], P('groups', ('seq', 'head', 'sub')), parts along dimension 0, may hold values from -6 to 6
- mamba_out_weight: bfloat16 [16384, 8192], P('seq', ('head', 'sub')), may hold values from -0.046875 to 0.046875
Outputs:
- layer_out: bfloat16 [8, 4, 8192], P('groups', None, ('head', 'sub')), parts along dimension 0
- ssm_next: float32 [8, 16384, 16], P('groups', ('seq', 'head', 'sub')), parts along dimension 0
There are 2 independent parts, one for each index of `groups`. A program takes and returns all parts, laid end to end along the dimension named above; an argument that names none is the same for every part. Nothing has to cross between parts.
Inputs may be any that keep to these rules, and one draw needn't show every extreme that they name: `kv_cache`: whole numbers.
All inputs are finite; a program needn't handle non-finite values.
Results may differ from a plain program's by a relative error of at most 0.015.
Values may be sent and summed in bfloat16 or wider, within the bound.
No kernel may reach another device: no remote copies, remote signals or barrier semaphores. Data moves between devices by JAX's collectives and lax.ppermute only.
A program may use at most 128 MiB of HBM per device.

v0:
```python
import math

import jax
import jax.numpy as jnp
from jax import lax
from jax.sharding import PartitionSpec as P

BLOCK = 128
D = 8192


epsilon = 1e-06


def combined_all(value, axis, combine):
    everything = jax.tree.map(lambda part: lax.all_gather(part, axis), value)
    leading = jax.tree.map(lambda part: part[0], everything)

    def hop(k, so_far):
        return combine(so_far, jax.tree.map(lambda part: part[k], everything))

    return lax.fori_loop(1, lax.axis_size(axis), hop, leading)


def rms_unit(values):
    return values * lax.rsqrt(jnp.mean(values * values, axis=-1, keepdims=True) + epsilon)


def combine_parts(first_part, second_part):
    top_first, sum_first, mix_first = first_part
    top_second, sum_second, mix_second = second_part
    merged_top = jnp.maximum(top_first, top_second)
    factor_first = jnp.exp(top_first - merged_top)
    factor_second = jnp.exp(top_second - merged_top)
    merged_sum = sum_first * factor_first + sum_second * factor_second
    merged_mix = mix_first * factor_first[..., None] + mix_second * factor_second[..., None]
    return (merged_top, merged_sum, merged_mix)


def local(
    hidden,
    query,
    key_new,
    value_new,
    kv_cache,
    kv_scale,
    context_len,
    attn_out_weight,
    norm_gain,
    in_weight,
    conv_weight,
    conv_bias,
    conv_state,
    xproj_weight,
    dt_weight,
    dt_bias,
    decay_rate,
    skip_gain,
    ssm_state,
    mamba_out_weight,
):
    requests = hidden.shape[0]
    steps_new = hidden.shape[1]
    row_count = requests * steps_new
    local_heads = key_new.shape[2]
    head_dim = query.shape[3]
    group_size = query.shape[2] // local_heads
    cache_len = kv_cache.shape[2]
    inv_root = 1.0 / math.sqrt(head_dim)
    queries = query.reshape(requests, steps_new, local_heads, group_size, head_dim)
    scores = jnp.einsum(
        "rtkgd,rpkd->rtkgp", queries, kv_cache[0], preferred_element_type=jnp.float32
    )
    key_scale = jnp.repeat(kv_scale[0], BLOCK, axis=2)
    value_scale = jnp.repeat(kv_scale[1], BLOCK, axis=2)
    scores = scores * key_scale[:, None, :, None, :] * inv_root
    position = lax.axis_index("seq") * cache_len + jnp.arange(cache_len, dtype=jnp.int32)
    is_live = (position[None, :] < context_len[:, None])[:, None, None, None, :]
    scores = jnp.where(is_live, scores, -1e30)
    local_top = jnp.max(scores, axis=-1)
    weights = jnp.where(is_live, jnp.exp(scores - local_top[..., None]), 0.0)
    local_total = jnp.sum(weights, axis=-1)
    weights = (weights * value_scale[:, None, :, None, :]).astype(jnp.bfloat16)
    partial_value = jnp.einsum(
        "rtkgp,rpkd->rtkgd", weights, kv_cache[1], preferred_element_type=jnp.float32
    )
    cache_top, cache_total, cache_mix = combined_all(
        (local_top, local_total, partial_value), "seq", combine_parts
    )
    recent = (
        jnp.einsum("rtkgd,rjkd->rtkgj", queries, key_new, preferred_element_type=jnp.float32)
        * inv_root
    )
    order_new = jnp.arange(steps_new, dtype=jnp.int32)
    causal = (order_new[None, :] <= order_new[:, None])[None, :, None, None, :]
    recent = jnp.where(causal, recent, -1e30)
    recent_top = jnp.max(recent, axis=-1)
    joint_top = jnp.maximum(cache_top, recent_top)
    recent_weight = jnp.where(causal, jnp.exp(recent - joint_top[..., None]), 0.0)
    recent_total = jnp.sum(recent_weight, axis=-1)
    recent_mix = jnp.einsum(
        "rtkgj,rjkd->rtkgd",
        recent_weight.astype(jnp.bfloat16),
        value_new,
        preferred_element_type=jnp.float32,
    )
    factor_cache = jnp.exp(cache_top - joint_top)
    blended = cache_mix * factor_cache[..., None] + recent_mix
    denominator = cache_total * factor_cache + recent_total
    head_rows = (
        (blended / denominator[..., None])
        .astype(jnp.bfloat16)
        .reshape(row_count, local_heads * group_size * head_dim)
    )
    every_head = lax.all_gather(head_rows, ("head", "sub"), axis=1, tiled=True)
    width_in = attn_out_weight.shape[0]
    chosen = lax.dynamic_slice_in_dim(every_head, lax.axis_index("seq") * width_in, width_in, 1)
    attended = lax.psum(jnp.dot(chosen, attn_out_weight, preferred_element_type=jnp.float32), "seq")
    residual = hidden.astype(jnp.float32).reshape(row_count, -1) + attended
    squares = lax.psum(jnp.sum(residual * residual, axis=-1), ("head", "sub"))
    normed = (residual * lax.rsqrt(squares[:, None] / D + epsilon) * norm_gain).astype(jnp.bfloat16)
    projected = jnp.einsum("nd,cde->cne", normed, in_weight, preferred_element_type=jnp.float32)
    own_width = conv_weight.shape[0]
    summed = lax.psum(projected, ("head", "sub"))
    channels = lax.dynamic_slice_in_dim(
        summed, lax.axis_index(("head", "sub")) * own_width, own_width, 2
    )
    conv_in = channels[0].astype(jnp.bfloat16)
    gate_in = channels[1].astype(jnp.bfloat16)
    window = jnp.concatenate(
        [
            conv_state.astype(jnp.float32),
            conv_in.astype(jnp.float32).reshape(requests, steps_new, own_width),
        ],
        axis=1,
    )
    taps_count = conv_weight.shape[1]
    conv_sum = jnp.zeros((requests, steps_new, own_width), jnp.float32) + conv_bias
    for tap in range(taps_count):
        conv_sum = (
            conv_sum + conv_weight[:, tap].astype(jnp.float32) * window[:, tap : tap + steps_new, :]
        )
    conv_out = jax.nn.silu(conv_sum).astype(jnp.bfloat16).reshape(row_count, own_width)
    mixing = lax.psum(
        jnp.dot(conv_out, xproj_weight, preferred_element_type=jnp.float32), ("seq", "head", "sub")
    )
    low_width = dt_weight.shape[0]
    state_width = decay_rate.shape[1]
    low_rank = rms_unit(mixing[:, :low_width]).astype(jnp.bfloat16)
    input_mat = rms_unit(mixing[:, low_width : low_width + state_width]).reshape(
        requests, steps_new, state_width
    )
    output_mat = rms_unit(mixing[:, low_width + state_width :]).reshape(
        requests, steps_new, state_width
    )
    delta = jax.nn.softplus(
        jnp.dot(low_rank, dt_weight, preferred_element_type=jnp.float32) + dt_bias
    ).reshape(requests, steps_new, own_width)
    signal = conv_out.astype(jnp.float32).reshape(requests, steps_new, own_width)
    memory = ssm_state
    outputs = []
    for moment in range(steps_new):
        step_now = delta[:, moment]
        memory = (
            jnp.exp(-step_now[..., None] * decay_rate) * memory
            + (step_now * signal[:, moment])[..., None] * input_mat[:, moment][:, None, :]
        )
        outputs.append(
            jnp.sum(memory * output_mat[:, moment][:, None, :], axis=-1)
            + skip_gain * signal[:, moment]
        )
    stacked = jnp.stack(outputs, axis=1).reshape(row_count, own_width)
    gated_out = (stacked * jax.nn.silu(gate_in.astype(jnp.float32))).astype(jnp.bfloat16)
    gated_block = lax.all_gather(gated_out, ("head", "sub"), axis=1, tiled=True)
    mamba_part = lax.psum(
        jnp.dot(gated_block, mamba_out_weight, preferred_element_type=jnp.float32), "seq"
    )
    final = (residual + mamba_part).astype(jnp.bfloat16).reshape(requests, steps_new, -1)
    return (final, memory)


def solution(mesh):
    return jax.shard_map(
        local,
        mesh=mesh,
        in_specs=(
            P("groups", None, ("head", "sub")),
            P("groups", None, ("head", "sub"), None),
            P("groups", None, ("head", "sub"), None),
            P("groups", None, ("head", "sub"), None),
            P(None, "groups", "seq", ("head", "sub"), None),
            P(None, "groups", ("head", "sub"), "seq"),
            P("groups"),
            P("seq", ("head", "sub")),
            P(("head", "sub")),
            P(None, ("head", "sub"), "seq"),
            P(("seq", "head", "sub"), None),
            P(("seq", "head", "sub")),
            P("groups", None, ("seq", "head", "sub")),
            P(("seq", "head", "sub"), None),
            P(None, ("seq", "head", "sub")),
            P(("seq", "head", "sub")),
            P(("seq", "head", "sub"), None),
            P(("seq", "head", "sub")),
            P("groups", ("seq", "head", "sub"), None),
            P("seq", ("head", "sub")),
        ),
        out_specs=(P("groups", None, ("head", "sub")), P("groups", ("seq", "head", "sub"), None)),
        check_vma=False,
    )
```

profile of v0, /device:TPU:0, one launch (start us, length us, event | category | flops | bytes accessed | tf_op | source)
XLA Modules:
  0.0 263.2 jit_solution(12783281778043170904)
XLA Ops:
  7.3 2.0 fusion.56
  11.1 1.2 fusion.59
  12.3 14.9 %all-gather = f32[16,4,2,8]{3,1,2,0:T(4,128)S(1)} all-gather(f32[4,4,2,8]{3,1,2,0:T(4,128)S(1)} %get-tuple-element.269), channel_id=2, replica_groups=mesh['groups'=2,'seq'=4,'head'=2,'sub'=2] {'seq'}, dimensions={0}, use_global_device_ids=true | all-gather | bytes 5120 | tf_op jit(solution)/shard_map/all_gather | solution.py:16
  27.7 16.2 %all-gather.2 = f32[16,4,2,8,128]{4,3,2,1,0:T(8,128)S(1)} all-gather(f32[4,4,2,8,128]{4,3,2,1,0:T(8,128)S(1)} %copy.76), channel_id=4, replica_groups=mesh['groups'=2,'seq'=4,'head'=2,'sub'=2] {'seq'}, dimensions={0}, use_global_device_ids=true | all-gather | bytes 655360 | tf_op jit(solution)/shard_map/all_gather | solution.py:16
  43.9 13.1 %all-gather.1 = f32[16,4,2,8]{3,1,2,0:T(4,128)S(1)} all-gather(f32[4,4,2,8]{3,1,2,0:T(4,128)S(1)} %fusion.12), channel_id=3, replica_groups=mesh['groups'=2,'seq'=4,'head'=2,'sub'=2] {'seq'}, dimensions={0}, use_global_device_ids=true | all-gather | bytes 5120 | tf_op jit(solution)/shard_map/all_gather | solution.py:16
  57.1 0.8 while.19
  57.9 1.3 fusion.60
  59.3 1.0 fusion.9
  60.4 5.8 %all_gather.30 = bf16[16,8192]{1,0:T(8,128)(2,1)S(1)} all-gather(bf16[16,2048]{1,0:T(8,128)(2,1)S(1)} %reshape.247), channel_id=1, replica_groups=mesh['groups'=2,'seq'=4,'head'=2,'sub'=2] {'head','sub'}, dimensions={1}, use_global_device_ids=true | all-gather | bytes 327680 | tf_op jit(solution)/shard_map/all_gather | solution.py:115
  66.2 5.2 %fusion.34 = f32[16,2048]{1,0:T(8,128)} fusion(bf16[2048,2048]{1,0:T(8,128)(2,1)} %param.29, bf16[16,8192]{1,0:T(8,128)(2,1)S(1)} %all_gather.30, s32[]{:T(128)S(6)} %select_n.44), kind=kOutput, calls=%fused_computation.73 | convolution fusion | flops 134217728 | bytes 8585220 | tf_op jit(solution)/shard_map/dot_general | solution.py:118
  71.6 34.6 %all-reduce.4.cloned.1.call-done = f32[16,2048]{1,0:T(8,128)} async-done(((f32[16,2048]{1,0:T(8,128)}), f32[16,2048]{1,0:T(8,128)}) %all-reduce.4.cloned.1.call-update) | async-done | bytes 131088 | tf_op jit(solution)/shard_map/psum | solution.py:118
  106.2 1.0 multiply_reduce_fusion.4
  107.3 5.7 %psum.36 = f32[16]{0:T(128)S(1)} all-reduce(f32[16]{0:T(128)S(1)} %get-tuple-element.231), channel_id=1, replica_groups=mesh['groups'=2,'seq'=4,'head'=2,'sub'=2] {'head','sub'}, use_global_device_ids=true, to_apply=%region_8.9 | all-reduce | flops 16 | bytes 128 | tf_op jit(solution)/shard_map/psum | solution.py:120
  112.9 13.0 %convolution_bitcast_fusion = f32[2,16,4096]{2,1,0:T(8,128)S(1)} fusion(bf16[2,2048,4096]{2,1,0:T(8,128)(2,1)} %param.31, f32[16,2048]{1,0:T(8,128)S(1)} %get-tuple-element.232, f32[2048]{0:T(1024)S(1)} %copy-done.4, f32[16]{0:T(128)S(1)} %add_rsqrt_fusion.3), kind=kOutput, calls=%fused_computation.11 | convolution fusion | flops 536969216 | bytes 34218048 | tf_op jit(solution)/shard_map/nd,cde->cne/dot_general | solution.py:122
  125.9 16.9 %all-reduce.7 = bf16[2,16,4096]{2,1,0:T(8,128)(2,1)S(1)} all-reduce(f32[2,16,4096]{2,1,0:T(8,128)S(1)} %convolution_bitcast_fusion), channel_id=1, replica_groups=mesh['groups'=2,'seq'=4,'head'=2,'sub'=2] {'head','sub'}, use_global_device_ids=true, to_apply=%region_9.10 | all-reduce | flops 131072 | bytes 786432 | tf_op jit(solution)/shard_map/psum | solution.py:124
  142.8 0.8 fusion.54
  144.1 59.7 %psum.38 = f32[16,544]{1,0:T(8,128)S(1)} all-reduce(f32[16,544]{1,0:T(8,128)S(1)} %fusion.61), channel_id=1, replica_groups=mesh['groups'=2,'seq'=4,'head'=2,'sub'=2] {'seq','head','sub'}, use_global_device_ids=true, to_apply=%region_10.11 | all-reduce | flops 8704 | bytes 69632 | tf_op jit(solution)/shard_map/psum | solution.py:144
  204.1 1.0 compare_select_fusion
  205.5 2.0 multiply_reduce_fusion.2
  207.5 0.8 multiply_add_fusion.7
  208.4 5.6 %all_gather.31 = bf16[16,4096]{1,0:T(8,128)(2,1)S(1)} all-gather(bf16[16,1024]{1,0:T(8,128)(2,1)S(1)} %fusion.36), channel_id=1, replica_groups=mesh['groups'=2,'seq'=4,'head'=2,'sub'=2] {'head','sub'}, dimensions={1}, use_global_device_ids=true | all-gather | bytes 163840 | tf_op jit(solution)/shard_map/all_gather | solution.py:174
  214.0 8.7 %fusion.62 = f32[16,2048]{1,0:T(8,128)} fusion(bf16[16,4096]{1,0:T(8,128)(2,1)S(1)} %all_gather.31, bf16[4096,2048]{1,0:T(8,128)(2,1)} %param.41), kind=kOutput, calls=%fused_computation.143 | convolution fusion | flops 268435456 | bytes 17039360 | tf_op jit(solution)/shard_map/dot_general | solution.py:176
  222.8 32.0 %all-reduce.6.cloned.1.call-done = f32[16,2048]{1,0:T(8,128)} async-done(((f32[16,2048]{1,0:T(8,128)}), f32[16,2048]{1,0:T(8,128)}) %all-reduce.6.cloned.1.call-update) | async-done | bytes 131088 | tf_op jit(solution)/shard_map/psum | solution.py:175
  254.7 0.9 add_convert_fusion
  (76 shorter events, 5.2 us)
Async XLA Ops:
  7.2 136.5 %copy-start = (bf16[1024,544]{0,1:T(8,128)(2,1)S(1)}, bf16[1024,544]{0,1:T(8,128)(2,1)}, u32[]{:S(2)}) copy-start(bf16[1024,544]{0,1:T(8,128)(2,1)} %param.35) | copy-start | bytes 3342340
  7.2 64.3 %copy-start.3 = (bf16[4,4,2048]{2,1,0:T(4,128)(2,1)S(1)}, bf16[4,4,2048]{2,1,0:T(4,128)(2,1)}, u32[]{:S(2)}) copy-start(bf16[4,4,2048]{2,1,0:T(4,128)(2,1)} %param.22) | copy-start | bytes 196612
  7.2 64.3 %copy-start.6 = (bf16[4,3,1024]{2,0,1:T(4,128)(2,1)S(1)}, bf16[4,3,1024]{2,0,1:T(4,128)(2,1)}, u32[]{:S(2)}) copy-start(bf16[4,3,1024]{2,0,1:T(4,128)(2,1)} %param.34) | copy-start | bytes 73732
  7.2 64.3 %copy-start.5 = (bf16[1024,4]{0,1:T(4,128)(2,1)S(1)}, bf16[1024,4]{0,1:T(4,128)(2,1)}, u32[]{:S(2)}) copy-start(bf16[1024,4]{0,1:T(4,128)(2,1)} %param.32) | copy-start | bytes 24580
  7.2 105.7 %copy-start.4 = (f32[2048]{0:T(1024)S(1)}, f32[2048]{0:T(1024)}, u32[]{:S(2)}) copy-start(f32[2048]{0:T(1024)} %param.30) | copy-start | bytes 24580
  7.2 99.0 %all-reduce.4.cloned.1.call-start = ((), (), s32[]{:S(2)}) async-start(), calls=%async_computation | async-start | bytes 262144 | tf_op jit(solution)/shard_map/psum | solution.py:118
  71.4 183.3 %all-reduce.6.cloned.1.call-start = ((), (), s32[]{:S(2)}) async-start(), calls=%async_computation.1 | async-start | bytes 262144 | tf_op jit(solution)/shard_map/psum | solution.py:175
  112.9 91.2 %copy-start.1 = (bf16[512,1024]{1,0:T(8,128)(2,1)S(1)}, bf16[512,1024]{1,0:T(8,128)(2,1)}, u32[]{:S(2)}) copy-start(bf16[512,1024]{1,0:T(8,128)(2,1)} %param.36) | copy-start | bytes 3145732
  112.9 92.6 %copy-start.2 = (f32[4,1024,16]{1,2,0:T(8,128)S(1)}, f32[4,1024,16]{1,2,0:T(8,128)}, u32[]{:S(2)}) copy-start(f32[4,1024,16]{1,2,0:T(8,128)} %param.40) | copy-start | bytes 786436
Sparse Core Ops, SparseCore 0:
  71.5 34.6 all-reduce.3
  222.9 31.8 all-reduce.5
where the time goes:
time: 264 us; the launch traced here: 263 us
  blocking collectives  138 us (52%)
  waiting for transfers between devices  66.6 us (25%)
  matrix products  32 us (12%)
  between operations  14.4 us (5%)
  other arithmetic  7.95 us (3%)
  local copies, waits for them, and re-layouts  4.11 us (2%)
    psum x1, blocking collectives, local(): lax.psum(jnp.dot(conv_out, xproj_weight, preferred_element_type=jnp.float...  59.7 us
    all_gather x3, blocking collectives, combined_all(): everything = jax.tree.map(lambda part: lax.all_gather(part, axis), value)  44.2 us
    psum x1, waiting for transfers between devices, local(): lax.psum(jnp.dot(chosen, attn_out_weight, preferred_element_type=jnp.floa...  34.6 us
    psum x1, waiting for transfers between devices, local(): lax.psum(jnp.dot(gated_block, mamba_out_weight, preferred_element_type=jn...  32 us
    psum x1, blocking collectives, local(): summed = lax.psum(projected, ('head', 'sub'))  16.9 us
    dot_general x1, matrix products, local(): jnp.einsum('nd,cde->cne', normed, in_weight, preferred_element_type=jnp.f...  13 us
    dot_general x1, matrix products, local(): jnp.dot(gated_block, mamba_out_weight, preferred_element_type=jnp.float32)  8.7 us
    all_gather x1, blocking collectives, local(): every_head = lax.all_gather(head_rows, ('head', 'sub'), axis=1, tiled=True)  5.79 us
  transfers between devices with their start and end apart: 2, of which 2 were waited for; matrix products, arithmetic and copies ran while one was open for 0% of the time, Pallas kernels for 0%

commit v1 on v0

v1 whole, which is shorter than its diff:
```python
import math

import jax
import jax.numpy as jnp
from jax import lax
from jax.sharding import PartitionSpec as P

BLOCK = 128
EPS = 1e-06
HS = ("head", "sub")
DIRECT = 8


def shifted(value, axes, hop):
    count = lax.axis_size(axes)
    return lax.ppermute(value, axes, [(i, (i + hop) % count) for i in range(count)])


def paired_sum(terms):
    if len(terms) == 1:
        return terms[0]
    return paired_sum(terms[::2]) + paired_sum(terms[1::2])


def everyone(value, axes):
    return [value] + [shifted(value, axes, hop) for hop in range(1, lax.axis_size(axes))]


def sum_over(value, axes, kind=None):
    if lax.axis_size(axes) > DIRECT:
        return lax.psum(value, axes)
    if kind is not None:
        value = lax.optimization_barrier(value.astype(kind))
    return paired_sum([part.astype(jnp.float32) for part in everyone(value, axes)])


def split_pair(value):
    upper = lax.reduce_precision(value, 8, 7)
    return upper, lax.reduce_precision(value - upper, 8, 7)


def split_three(value):
    upper, middle = split_pair(value)
    return upper, middle, lax.reduce_precision(value - upper - middle, 8, 7)


def rms_unit(values):
    return values * lax.rsqrt(jnp.mean(values * values, axis=-1, keepdims=True) + EPS)


def attention(query, key_new, value_new, kv_cache, kv_scale, context_len):
    requests, steps, heads, dim = query.shape
    kv_heads = key_new.shape[2]
    group = heads // kv_heads
    cache_len = kv_cache.shape[2]
    width = cache_len * kv_heads
    inv_root = 1.0 / math.sqrt(dim)
    first = lax.axis_index("seq") == 0
    flat_query = query.reshape(requests, steps * heads, dim)
    flat_cache = kv_cache.reshape(2, requests, width, dim)
    column = jnp.arange(width, dtype=jnp.int32)
    row = jnp.arange(steps * heads, dtype=jnp.int32)
    row_kv = (row % heads) // group
    same = row_kv[:, None] == (column % kv_heads)[None, :]
    place = lax.axis_index("seq") * cache_len + column // kv_heads
    live = same[None] & (place[None, :] < context_len[:, None])[:, None, :]
    spread = jnp.repeat(kv_scale.transpose(0, 1, 3, 2), BLOCK, axis=2).reshape(2, requests, width)
    scores = jnp.einsum("rqd,rpd->rqp", flat_query, flat_cache[0], preferred_element_type=jnp.float32)
    scores = jnp.where(live, scores * spread[0][:, None, :] * inv_root, -1e30)
    flat_new_k = key_new.reshape(requests, steps * kv_heads, dim)
    flat_new_v = value_new.reshape(requests, steps * kv_heads, dim)
    new_column = jnp.arange(steps * kv_heads, dtype=jnp.int32)
    new_live = (
        (row_kv[:, None] == (new_column % kv_heads)[None, :])
        & ((new_column // kv_heads)[None, :] <= (row // heads)[:, None])
        & first
    )[None]
    recent = jnp.einsum("rqd,rjd->rqj", flat_query, flat_new_k, preferred_element_type=jnp.float32)
    recent = jnp.where(new_live, recent * inv_root, -1e30)
    top = jnp.maximum(jnp.max(scores, axis=-1), jnp.max(recent, axis=-1))
    weight = jnp.where(live, jnp.exp(scores - top[..., None]), 0.0)
    new_weight = jnp.where(new_live, jnp.exp(recent - top[..., None]), 0.0)
    total = jnp.sum(weight, axis=-1) + jnp.sum(new_weight, axis=-1)
    scaled = (weight * spread[1][:, None, :]).astype(jnp.bfloat16)
    mix = jnp.einsum("rqp,rpd->rqd", scaled, flat_cache[1], preferred_element_type=jnp.float32)
    mix = mix + jnp.einsum(
        "rqj,rjd->rqd", new_weight.astype(jnp.bfloat16), flat_new_v, preferred_element_type=jnp.float32
    )
    rows = requests * steps
    return mix.reshape(rows, heads, dim), top.reshape(rows, heads), total.reshape(rows, heads)


def merge(mixes, tops, totals):
    best = tops[0]
    for top in tops[1:]:
        best = jnp.maximum(best, top)
    factors = [jnp.exp(top - best) for top in tops]
    summed = paired_sum([total * factor for total, factor in zip(totals, factors)])
    mixed = paired_sum(
        [mix.astype(jnp.float32) * factor[..., None] for mix, factor in zip(mixes, factors)]
    )
    return (mixed / summed[..., None]).astype(jnp.bfloat16)


def local(
    hidden,
    query,
    key_new,
    value_new,
    kv_cache,
    kv_scale,
    context_len,
    attn_out_weight,
    norm_gain,
    in_weight,
    conv_weight,
    conv_bias,
    conv_state,
    xproj_weight,
    dt_weight,
    dt_bias,
    decay_rate,
    skip_gain,
    ssm_state,
    mamba_out_weight,
):
    requests, steps = hidden.shape[:2]
    rows = requests * steps
    seq_count = lax.axis_size("seq")
    hs_count = lax.axis_size(HS)
    hs_index = lax.axis_index(HS)
    heads = query.shape[2]
    dim = query.shape[3]
    mix, top, total = attention(query, key_new, value_new, kv_cache, kv_scale, context_len)
    if seq_count == hs_count:
        packed = jnp.concatenate(
            [mix.reshape(rows, heads * dim)] + list(split_three(top)) + list(split_three(total)), axis=1
        ).astype(jnp.bfloat16)
        swap = [(s * hs_count + j, j * hs_count + s) for s in range(seq_count) for j in range(hs_count)]
        swapped = lax.ppermute(packed, ("seq",) + HS, swap)
        parts = everyone(lax.optimization_barrier(swapped), HS)
        base = heads * dim
        piece = lambda part, k: part[:, base + k * heads : base + (k + 1) * heads].astype(jnp.float32)
        three = lambda part, k: piece(part, k) + piece(part, k + 1) + piece(part, k + 2)
        chosen = merge(
            [part[:, :base].reshape(rows, heads, dim) for part in parts],
            [three(part, 0) for part in parts],
            [three(part, 3) for part in parts],
        ).reshape(rows, base)
    else:
        mixes, tops, totals = (lax.all_gather(part, "seq") for part in (mix, top, total))
        every = range(seq_count)
        own_heads = merge([mixes[k] for k in every], [tops[k] for k in every], [totals[k] for k in every])
        every_head = lax.all_gather(own_heads.reshape(rows, heads * dim), HS, axis=1, tiled=True)
        width_in = attn_out_weight.shape[0]
        chosen = lax.dynamic_slice_in_dim(every_head, lax.axis_index("seq") * width_in, width_in, 1)
    attended = sum_over(
        jnp.dot(chosen, attn_out_weight, preferred_element_type=jnp.float32), "seq", jnp.bfloat16
    )
    residual = hidden.astype(jnp.float32).reshape(rows, -1) + attended
    features = residual.shape[1] * hs_count
    squares = jnp.sum(residual * residual, axis=-1, keepdims=True)
    gained = (residual * norm_gain).astype(jnp.bfloat16)
    projected = jnp.einsum("nd,cde->nce", gained, in_weight, preferred_element_type=jnp.float32)
    own_width = conv_weight.shape[0]
    upper, lower = split_pair(squares)

    def block_for(index):
        block = lax.dynamic_slice_in_dim(projected, index * own_width, own_width, 2)
        return block.reshape(rows, 2 * own_width)

    channels = block_for(hs_index)
    for hop in range(1, hs_count):
        block = jnp.concatenate([block_for((hs_index + hop) % hs_count), upper, lower], axis=1)
        part = shifted(block.astype(jnp.bfloat16), HS, hop).astype(jnp.float32)
        channels = channels + part[:, : 2 * own_width]
        squares = squares + part[:, 2 * own_width : 2 * own_width + 1] + part[:, 2 * own_width + 1 :]
    channels = channels * lax.rsqrt(squares / features + EPS)
    conv_in = channels[:, :own_width].astype(jnp.bfloat16)
    gate_in = channels[:, own_width:].astype(jnp.bfloat16)
    window = jnp.concatenate(
        [
            conv_state.astype(jnp.float32),
            conv_in.astype(jnp.float32).reshape(requests, steps, own_width),
        ],
        axis=1,
    )
    conv_sum = jnp.zeros((requests, steps, own_width), jnp.float32) + conv_bias
    for tap in range(conv_weight.shape[1]):
        conv_sum = conv_sum + conv_weight[:, tap].astype(jnp.float32) * window[:, tap : tap + steps, :]
    conv_out = jax.nn.silu(conv_sum).astype(jnp.bfloat16).reshape(rows, own_width)
    mixing = jnp.dot(conv_out, xproj_weight, preferred_element_type=jnp.float32)
    mixing = sum_over(sum_over(mixing, HS), "seq")
    low_width = dt_weight.shape[0]
    state_width = decay_rate.shape[1]
    low_rank = rms_unit(mixing[:, :low_width]).astype(jnp.bfloat16)
    input_mat = rms_unit(mixing[:, low_width : low_width + state_width]).reshape(
        requests, steps, state_width
    )
    output_mat = rms_unit(mixing[:, low_width + state_width :]).reshape(requests, steps, state_width)
    delta = jax.nn.softplus(
        jnp.dot(low_rank, dt_weight, preferred_element_type=jnp.float32) + dt_bias
    ).reshape(requests, steps, own_width)
    signal = conv_out.astype(jnp.float32).reshape(requests, steps, own_width)
    memory = ssm_state
    outputs = []
    for moment in range(steps):
        step_now = delta[:, moment]
        memory = (
            jnp.exp(-step_now[..., None] * decay_rate) * memory
            + (step_now * signal[:, moment])[..., None] * input_mat[:, moment][:, None, :]
        )
        outputs.append(
            jnp.sum(memory * output_mat[:, moment][:, None, :], axis=-1)
            + skip_gain * signal[:, moment]
        )
    stacked = jnp.stack(outputs, axis=1).reshape(rows, own_width)
    gated_out = (stacked * jax.nn.silu(gate_in.astype(jnp.float32))).astype(jnp.bfloat16)
    gated_block = lax.all_gather(gated_out, HS, axis=1, tiled=True)
    mamba_part = sum_over(
        jnp.dot(gated_block, mamba_out_weight, preferred_element_type=jnp.float32), "seq", jnp.bfloat16
    )
    final = (residual + mamba_part).astype(jnp.bfloat16).reshape(requests, steps, -1)
    return (final, memory)


def solution(mesh):
    return jax.shard_map(
        local,
        mesh=mesh,
        in_specs=(
            P("groups", None, HS),
            P("groups", None, HS, None),
            P("groups", None, HS, None),
            P("groups", None, HS, None),
            P(None, "groups", "seq", HS, None),
            P(None, "groups", HS, "seq"),
            P("groups"),
            P("seq", HS),
            P(HS),
            P(None, HS, "seq"),
            P(("seq",) + HS, None),
            P(("seq",) + HS),
            P("groups", None, ("seq",) + HS),
            P(("seq",) + HS, None),
            P(None, ("seq",) + HS),
            P(("seq",) + HS),
            P(("seq",) + HS, None),
            P(("seq",) + HS),
            P("groups", ("seq",) + HS, None),
            P("seq", HS),
        ),
        out_specs=(P("groups", None, HS), P("groups", ("seq",) + HS, None)),
        check_vma=False,
    )
```

time: 264 us -> 105 us (0.40)
  blocking collectives: 138 us -> 5.61 us
  waiting for transfers between devices: 66.6 us -> 16.3 us
  starting transfers between devices: 0.08 us -> 34.1 us
  between operations: 14.4 us -> 1.2 us
  local copies, waits for them, and re-layouts: 4.11 us -> 7.9 us
    psum x3 -> x0, blocking collectives: 82.2 us -> none  [the longest x1 59.7 us: local(): lax.psum(jnp.dot(conv_out, xproj_weight, preferred_element_type=jnp.float...]
    psum x2 -> x0, waiting for transfers between devices: 66.6 us -> none  [the longest x1 34.6 us: local(): lax.psum(jnp.dot(chosen, attn_out_weight, preferred_element_type=jnp.floa...]
    all_gather x5 -> x1, blocking collectives: 55.6 us -> 5.61 us  [local(): gated_block = lax.all_gather(gated_out, HS, axis=1, tiled=True)]
    ppermute x0 -> x19, starting transfers between devices: none -> 34.1 us  [the longest x18 33.4 us: shifted(): lax.ppermute(value, axes, [(i, (i + hop) % count) for i in range(count)])]
    ppermute x0 -> x19, waiting for transfers between devices: none -> 16.3 us  [the longest x18 16.3 us: shifted(): lax.ppermute(value, axes, [(i, (i + hop) % count) for i in range(count)])]
  transfers between devices with their start and end apart: 2 -> 19, of which waited for: 2 -> 11; matrix products, arithmetic and copies ran while one was open for 0% -> 4% of each run, Pallas kernels for 0% -> 0%
where the time goes in v1:
time: 105 us; the launch traced here: 104 us
  starting transfers between devices  34.1 us (32%)
  matrix products  30.6 us (29%)
  waiting for transfers between devices  16.3 us (16%)
  other arithmetic  8.51 us (8%)
  local copies, waits for them, and re-layouts  7.9 us (8%)
  blocking collectives  5.61 us (5%)
  between operations  1.2 us (1%)
    ppermute x18, starting transfers between devices, shifted(): lax.ppermute(value, axes, [(i, (i + hop) % count) for i in range(count)])  33.4 us
    ppermute x18, waiting for transfers between devices, shifted(): lax.ppermute(value, axes, [(i, (i + hop) % count) for i in range(count)])  16.3 us
    dot_general x1, matrix products, local(): jnp.einsum('nd,cde->nce', gained, in_weight, preferred_element_type=jnp.f...  12.9 us
    dot_general x1, matrix products, local(): jnp.dot(gated_block, mamba_out_weight, preferred_element_type=jnp.float32)  8.04 us
    all_gather x1, blocking collectives, local(): gated_block = lax.all_gather(gated_out, HS, axis=1, tiled=True)  5.61 us
    dot_general x1, matrix products, local(): jnp.dot(chosen, attn_out_weight, preferred_element_type=jnp.float32)  4.8 us
  transfers between devices with their start and end apart: 19, of which 11 were waited for; matrix products, arithmetic and copies ran while one was open for 4% of the time, Pallas kernels for 0%

profile of v1, /device:TPU:0, one launch (start us, length us, event | category | flops | bytes accessed | tf_op | source)
XLA Modules:
  0.0 104.3 jit_solution(7035117390074417062)
XLA Ops:
  1.7 1.9 %fusion.71 = (bf16[1,4,256,2,128]{4,3,2,1,0:T(2,128)(2,1)S(1)}, bf16[1,4,256,2,128]{4,3,2,1,0:T(2,128)(2,1)S(1)}) fusion(bf16[2,4,256,2,128]{4,3,2,1,0:T(2,128)(2,1)} %param.24), kind=kLoop, calls=%fused_computation.196 | loop fusion | bytes 2097152 | tf_op jit(solution)/shard_map/slice | solution.py:85
  5.5 1.2 %fusion.75 = (f32[4,64]{1,0:T(4,128)S(1)}, f32[4,64,512]{2,1,0:T(8,128)S(1)}) fusion(f32[4,512]{1,0:T(4,128)S(1)} %copy.79, bf16[4,64,128]{2,1,0:T(8,128)(2,1)} %bitcast.144, bf16[4,512,128]{2,1,0:T(8,128)(2,1)S(1)} %bitcast.133, pred[4,512]{1,0:T(4,128)(4,1)S(1)} %broadcast_compare_fusion.1, pred[64,512]{1,0:T(8,128)(4,1)S(1)} %broadcast_compare_fusion), kind=kOutput, calls=%fused_computation.200 | convolution fusion | flops 34209536 | bytes 1158144 | tf_op jit(solution)/shard_map/rqd,rpd->rqp/dot_general | solution.py:68
  9.6 6.4 %collective-permute-start.1 = (bf16[16,2144]{1,0:T(8,128)(2,1)S(1)}, bf16[16,2144]{1,0:T(8,128)(2,1)S(1)}, u32[]{:S(2)}, u32[]{:S(2)}) collective-permute-start(bf16[16,2144]{1,0:T(8,128)(2,1)S(1)} %collective-permute-done), channel_id=1, source_target_pairs={{0,1},{1,2},{2,3},{3,0},{4,5},{5,6},{6,7},{7,4},{8,9},{9,10},{10,1... | collective-permute-start | bytes 205832 | tf_op jit(solution)/shard_map/ppermute | solution.py:16
  15.9 5.7 %collective-permute-start.2 = (bf16[16,2144]{1,0:T(8,128)(2,1)S(1)}, bf16[16,2144]{1,0:T(8,128)(2,1)S(1)}, u32[]{:S(2)}, u32[]{:S(2)}) collective-permute-start(bf16[16,2144]{1,0:T(8,128)(2,1)S(1)} %collective-permute-done), channel_id=1, source_target_pairs={{0,2},{1,3},{2,0},{3,1},{4,6},{5,7},{6,4},{7,5},{8,10},{9,11},{10,... | collective-permute-start | bytes 205832 | tf_op jit(solution)/shard_map/ppermute | solution.py:16
  21.6 1.4 %collective-permute-start.3 = (bf16[16,2144]{1,0:T(8,128)(2,1)S(1)}, bf16[16,2144]{1,0:T(8,128)(2,1)S(1)}, u32[]{:S(2)}, u32[]{:S(2)}) collective-permute-start(bf16[16,2144]{1,0:T(8,128)(2,1)S(1)} %collective-permute-done), channel_id=1, source_target_pairs={{0,3},{1,0},{2,1},{3,2},{4,7},{5,4},{6,5},{7,6},{8,11},{9,8},{10,9... | collective-permute-start | bytes 205832 | tf_op jit(solution)/shard_map/ppermute | solution.py:16
  25.7 4.8 %convolution_convert_fusion.1 = bf16[16,2048]{1,0:T(8,128)(2,1)S(1)} fusion(bf16[2048,2048]{1,0:T(8,128)(2,1)} %param.27, f32[2,8,16,128]{3,2,1,0:T(8,128)S(1)} %bitcast.138, f32[2,8,16,128]{3,2,1,0:T(8,128)S(1)} %bitcast.137, f32[2,8,16,128]{3,2,1,0:T(8,128)S(1)} %bitcast.136, f32[2,8,16,128]{3,2,1,0:T(8,128)S(1)} %bitcast.135, ...), kind=kOutput, calls=%fused_computation.1 | convolution fusion | flops 134676480 | bytes 9371648 | tf_op jit(solution)/shard_map/dot_general | solution.py:158
  30.5 1.3 %collective-permute-start.4 = (bf16[16,2048]{1,0:T(8,128)(2,1)S(1)}, bf16[16,2048]{1,0:T(8,128)(2,1)S(1)}, u32[]{:S(2)}, u32[]{:S(2)}) collective-permute-start(bf16[16,2048]{1,0:T(8,128)(2,1)S(1)} %convolution_convert_fusion.1), channel_id=1, source_target_pairs={{0,8},{4,12},{8,0},{12,4},{1,9},{5,13},{9,1},{13,5},{2,10},{6,14},... | collective-permute-start | bytes 196616 | tf_op jit(solution)/shard_map/ppermute | solution.py:16
  31.8 1.8 %collective-permute-start.5 = (bf16[16,2048]{1,0:T(8,128)(2,1)S(1)}, bf16[16,2048]{1,0:T(8,128)(2,1)S(1)}, u32[]{:S(2)}, u32[]{:S(2)}) collective-permute-start(bf16[16,2048]{1,0:T(8,128)(2,1)S(1)} %convolution_convert_fusion.1), channel_id=1, source_target_pairs={{0,4},{4,8},{8,12},{12,0},{1,5},{5,9},{9,13},{13,1},{2,6},{6,10},{... | collective-permute-start | bytes 196616 | tf_op jit(solution)/shard_map/ppermute | solution.py:16
  33.6 2.0 %collective-permute-start.6 = (bf16[16,2048]{1,0:T(8,128)(2,1)S(1)}, bf16[16,2048]{1,0:T(8,128)(2,1)S(1)}, u32[]{:S(2)}, u32[]{:S(2)}) collective-permute-start(bf16[16,2048]{1,0:T(8,128)(2,1)S(1)} %convolution_convert_fusion.1), channel_id=1, source_target_pairs={{0,12},{4,0},{8,4},{12,8},{1,13},{5,1},{9,5},{13,9},{2,14},{6,2},{... | collective-permute-start | bytes 196616 | tf_op jit(solution)/shard_map/ppermute | solution.py:16
  36.3 2.7 %collective-permute-done.4 = bf16[16,2048]{1,0:T(8,128)(2,1)S(1)} collective-permute-done((bf16[16,2048]{1,0:T(8,128)(2,1)S(1)}, bf16[16,2048]{1,0:T(8,128)(2,1)S(1)}, u32[]{:S(2)}, u32[]{:S(2)}) %collective-permute-start.4) | collective-permute-done | bytes 65568 | tf_op jit(solution)/shard_map/ppermute | solution.py:16
  39.0 1.2 %collective-permute-done.6 = bf16[16,2048]{1,0:T(8,128)(2,1)S(1)} collective-permute-done((bf16[16,2048]{1,0:T(8,128)(2,1)S(1)}, bf16[16,2048]{1,0:T(8,128)(2,1)S(1)}, u32[]{:S(2)}, u32[]{:S(2)}) %collective-permute-start.6) | collective-permute-done | bytes 65568 | tf_op jit(solution)/shard_map/ppermute | solution.py:16
  40.3 12.9 %fusion.21 = f32[16,2,4096]{2,0,1:T(8,128)S(1)} fusion(bf16[2,2048,4096]{2,1,0:T(8,128)(2,1)} %param.29, f32[16,2048]{1,0:T(8,128)S(1)} %get-tuple-element.12, f32[2048]{0:T(1024)S(1)} %copy-done.5), kind=kOutput, calls=%fused_computation.61 | convolution fusion | flops 536936448 | bytes 34217984 | tf_op jit(solution)/shard_map/nd,cde->nce/dot_general | solution.py:164
  56.5 1.5 %collective-permute-start.9 = (bf16[16,2050]{1,0:T(8,128)(2,1)S(1)}, bf16[16,2050]{1,0:T(8,128)(2,1)}, u32[]{:S(2)}, u32[]{:S(2)}) collective-permute-start(bf16[16,2050]{1,0:T(8,128)(2,1)S(1)} %concatenate.22), channel_id=1, source_target_pairs={{0,3},{1,0},{2,1},{3,2},{4,7},{5,4},{6,5},{7,6},{8,11},{9,8},{10,9... | collective-permute-start | bytes 196808 | tf_op jit(solution)/shard_map/ppermute | solution.py:16
  58.7 1.3 %collective-permute-done.8 = bf16[16,2050]{1,0:T(8,128)(2,1)} collective-permute-done((bf16[16,2050]{1,0:T(8,128)(2,1)S(1)}, bf16[16,2050]{1,0:T(8,128)(2,1)}, u32[]{:S(2)}, u32[]{:S(2)}) %collective-permute-start.8) | collective-permute-done | bytes 65632 | tf_op jit(solution)/shard_map/ppermute | solution.py:16
  64.4 1.2 %collective-permute-start.12 = (f32[16,544]{1,0:T(8,128)S(1)}, f32[16,544]{1,0:T(8,128)S(1)}, u32[]{:S(2)}, u32[]{:S(2)}) collective-permute-start(f32[16,544]{1,0:T(8,128)S(1)} %fusion.77), channel_id=1, source_target_pairs={{0,3},{1,0},{2,1},{3,2},{4,7},{5,4},{6,5},{7,6},{8,11},{9,8},{10,9... | collective-permute-start | bytes 104456 | tf_op jit(solution)/shard_map/ppermute | solution.py:16
  65.7 2.1 %collective-permute-done.10 = f32[16,544]{1,0:T(8,128)S(1)} collective-permute-done((f32[16,544]{1,0:T(8,128)S(1)}, f32[16,544]{1,0:T(8,128)S(1)}, u32[]{:S(2)}, u32[]{:S(2)}) %collective-permute-start.10) | collective-permute-done | bytes 34848 | tf_op jit(solution)/shard_map/ppermute | solution.py:16
  67.9 1.6 %collective-permute-start.13 = (f32[16,544]{1,0:T(8,128)S(1)}, f32[16,544]{1,0:T(8,128)S(1)}, u32[]{:S(2)}, u32[]{:S(2)}) collective-permute-start(f32[16,544]{1,0:T(8,128)S(1)} %add_add_fusion.2), channel_id=1, source_target_pairs={{0,8},{4,12},{8,0},{12,4},{1,9},{5,13},{9,1},{13,5},{2,10},{6,14},... | collective-permute-start | bytes 104456 | tf_op jit(solution)/shard_map/ppermute | solution.py:16
  70.2 3.2 %collective-permute-start.15 = (f32[16,544]{1,0:T(8,128)S(1)}, f32[16,544]{1,0:T(8,128)S(1)}, u32[]{:S(2)}, u32[]{:S(2)}) collective-permute-start(f32[16,544]{1,0:T(8,128)S(1)} %add_add_fusion.2), channel_id=1, source_target_pairs={{0,12},{4,0},{8,4},{12,8},{1,13},{5,1},{9,5},{13,9},{2,14},{6,2},{... | collective-permute-start | bytes 104456 | tf_op jit(solution)/shard_map/ppermute | solution.py:16
  74.2 1.6 %collective-permute-done.14 = f32[16,544]{1,0:T(8,128)S(1)} collective-permute-done((f32[16,544]{1,0:T(8,128)S(1)}, f32[16,544]{1,0:T(8,128)S(1)}, u32[]{:S(2)}, u32[]{:S(2)}) %collective-permute-start.14) | collective-permute-done | bytes 34848 | tf_op jit(solution)/shard_map/ppermute | solution.py:16
  77.5 2.0 %multiply_reduce_fusion.2 = (f32[4,1024]{1,0:T(4,128)S(1)}, f32[4,1024]{1,0:T(4,128)S(1)}, f32[4,1024]{1,0:T(4,128)S(1)}, f32[4,1024]{1,0:T(4,128)S(1)}, f32[4,1024,16]{1,2,0:T(8,128)}) fusion(f32[4,16]{1,0:T(4,128)S(1)} %bitcast.168, f32[4,16]{1,0:T(4,128)S(1)} %bitcast.164, f32[4,1024]{1,0:T(4,128)S(1)} %bitcast.152, f32[4,16]{1,0:T(4,128)S(1)} %bitcast.162, ...), kind=kLoop, calls=%fused_computation.17 | loop fusion | flops 1556480 | bytes 788480 | tf_op jit(solution)/shard_map/reduce_sum | solution.py:214
  80.4 5.6 %all_gather.3 = bf16[16,4096]{1,0:T(8,128)(2,1)S(1)} all-gather(bf16[16,1024]{1,0:T(8,128)(2,1)S(1)} %fusion.41), channel_id=1, replica_groups=mesh['groups'=2,'seq'=4,'head'=2,'sub'=2] {'head','sub'}, dimensions={1}, use_global_device_ids=true | all-gather | bytes 163840 | tf_op jit(solution)/shard_map/all_gather | solution.py:219
  86.0 8.0 %convolution_convert_fusion = bf16[16,2048]{1,0:T(8,128)(2,1)S(1)} fusion(bf16[16,4096]{1,0:T(8,128)(2,1)S(1)} %all_gather.3, bf16[4096,2048]{1,0:T(8,128)(2,1)} %param.39), kind=kOutput, calls=%fused_computation | convolution fusion | flops 268468224 | bytes 16973824 | tf_op jit(solution)/shard_map/dot_general | solution.py:221
  95.3 2.8 %collective-permute-start.17 = (bf16[16,2048]{1,0:T(8,128)(2,1)S(1)}, bf16[16,2048]{1,0:T(8,128)(2,1)S(1)}, u32[]{:S(2)}, u32[]{:S(2)}) collective-permute-start(bf16[16,2048]{1,0:T(8,128)(2,1)S(1)} %convolution_convert_fusion), channel_id=1, source_target_pairs={{0,4},{4,8},{8,12},{12,0},{1,5},{5,9},{9,13},{13,1},{2,6},{6,10},{... | collective-permute-start | bytes 196616 | tf_op jit(solution)/shard_map/ppermute | solution.py:16
  99.1 3.6 %collective-permute-done.16 = bf16[16,2048]{1,0:T(8,128)(2,1)S(1)} collective-permute-done((bf16[16,2048]{1,0:T(8,128)(2,1)S(1)}, bf16[16,2048]{1,0:T(8,128)(2,1)S(1)}, u32[]{:S(2)}, u32[]{:S(2)}) %collective-permute-start.16) | collective-permute-done | bytes 65568 | tf_op jit(solution)/shard_map/ppermute | solution.py:16
  (125 shorter events, 25.1 us)
Async XLA Ops:
  0.6 62.4 %copy-start = (bf16[1024,544]{0,1:T(8,128)(2,1)S(1)}, bf16[1024,544]{0,1:T(8,128)(2,1)}, u32[]{:S(2)}) copy-start(bf16[1024,544]{0,1:T(8,128)(2,1)} %param.33) | copy-start | bytes 3342340
  0.7 35.6 %copy-start.7 = (bf16[4,3,1024]{2,0,1:T(4,128)(2,1)S(1)}, bf16[4,3,1024]{2,0,1:T(4,128)(2,1)}, u32[]{:S(2)}) copy-start(bf16[4,3,1024]{2,0,1:T(4,128)(2,1)} %param.32) | copy-start | bytes 73732
  0.7 39.6 %copy-start.5 = (f32[2048]{0:T(1024)S(1)}, f32[2048]{0:T(1024)}, u32[]{:S(2)}) copy-start(f32[2048]{0:T(1024)} %param.28) | copy-start | bytes 24580
  8.9 0.7 collective-permute-start
  9.6 13.5 %collective-permute-start.1 = (bf16[16,2144]{1,0:T(8,128)(2,1)S(1)}, bf16[16,2144]{1,0:T(8,128)(2,1)S(1)}, u32[]{:S(2)}, u32[]{:S(2)}) collective-permute-start(bf16[16,2144]{1,0:T(8,128)(2,1)S(1)} %collective-permute-done), channel_id=1, source_target_pairs={{0,1},{1,2},{2,3},{3,0},{4,5},{5,6},{6,7},{7,4},{8,9},{9,10},{10,1... | collective-permute-start | bytes 205832 | tf_op jit(solution)/shard_map/ppermute | solution.py:16
  15.9 8.2 %collective-permute-start.2 = (bf16[16,2144]{1,0:T(8,128)(2,1)S(1)}, bf16[16,2144]{1,0:T(8,128)(2,1)S(1)}, u32[]{:S(2)}, u32[]{:S(2)}) collective-permute-start(bf16[16,2144]{1,0:T(8,128)(2,1)S(1)} %collective-permute-done), channel_id=1, source_target_pairs={{0,2},{1,3},{2,0},{3,1},{4,6},{5,7},{6,4},{7,5},{8,10},{9,11},{10,... | collective-permute-start | bytes 205832 | tf_op jit(solution)/shard_map/ppermute | solution.py:16
  21.6 3.5 %collective-permute-start.3 = (bf16[16,2144]{1,0:T(8,128)(2,1)S(1)}, bf16[16,2144]{1,0:T(8,128)(2,1)S(1)}, u32[]{:S(2)}, u32[]{:S(2)}) collective-permute-start(bf16[16,2144]{1,0:T(8,128)(2,1)S(1)} %collective-permute-done), channel_id=1, source_target_pairs={{0,3},{1,0},{2,1},{3,2},{4,7},{5,4},{6,5},{7,6},{8,11},{9,8},{10,9... | collective-permute-start | bytes 205832 | tf_op jit(solution)/shard_map/ppermute | solution.py:16
  30.5 8.5 %collective-permute-start.4 = (bf16[16,2048]{1,0:T(8,128)(2,1)S(1)}, bf16[16,2048]{1,0:T(8,128)(2,1)S(1)}, u32[]{:S(2)}, u32[]{:S(2)}) collective-permute-start(bf16[16,2048]{1,0:T(8,128)(2,1)S(1)} %convolution_convert_fusion.1), channel_id=1, source_target_pairs={{0,8},{4,12},{8,0},{12,4},{1,9},{5,13},{9,1},{13,5},{2,10},{6,14},... | collective-permute-start | bytes 196616 | tf_op jit(solution)/shard_map/ppermute | solution.py:16
  31.8 7.2 %collective-permute-start.5 = (bf16[16,2048]{1,0:T(8,128)(2,1)S(1)}, bf16[16,2048]{1,0:T(8,128)(2,1)S(1)}, u32[]{:S(2)}, u32[]{:S(2)}) collective-permute-start(bf16[16,2048]{1,0:T(8,128)(2,1)S(1)} %convolution_convert_fusion.1), channel_id=1, source_target_pairs={{0,4},{4,8},{8,12},{12,0},{1,5},{5,9},{9,13},{13,1},{2,6},{6,10},{... | collective-permute-start | bytes 196616 | tf_op jit(solution)/shard_map/ppermute | solution.py:16
  33.6 6.5 %collective-permute-start.6 = (bf16[16,2048]{1,0:T(8,128)(2,1)S(1)}, bf16[16,2048]{1,0:T(8,128)(2,1)S(1)}, u32[]{:S(2)}, u32[]{:S(2)}) collective-permute-start(bf16[16,2048]{1,0:T(8,128)(2,1)S(1)} %convolution_convert_fusion.1), channel_id=1, source_target_pairs={{0,12},{4,0},{8,4},{12,8},{1,13},{5,1},{9,5},{13,9},{2,14},{6,2},{... | collective-permute-start | bytes 196616 | tf_op jit(solution)/shard_map/ppermute | solution.py:16
  40.3 35.8 %copy-start.1 = (bf16[512,1024]{1,0:T(8,128)(2,1)S(1)}, bf16[512,1024]{1,0:T(8,128)(2,1)}, u32[]{:S(2)}) copy-start(bf16[512,1024]{1,0:T(8,128)(2,1)} %param.34) | copy-start | bytes 3145732
  40.3 37.2 %copy-start.2 = (f32[4,1024,16]{1,2,0:T(8,128)S(1)}, f32[4,1024,16]{1,2,0:T(8,128)}, u32[]{:S(2)}) copy-start(f32[4,1024,16]{1,2,0:T(8,128)} %param.38) | copy-start | bytes 786436
  54.2 4.5 %collective-permute-start.7 = (bf16[16,2050]{1,0:T(8,128)(2,1)S(1)}, bf16[16,2050]{1,0:T(8,128)(2,1)S(1)}, u32[]{:S(2)}, u32[]{:S(2)}) collective-permute-start(bf16[16,2050]{1,0:T(8,128)(2,1)S(1)} %concatenate.20), channel_id=1, source_target_pairs={{0,1},{1,2},{2,3},{3,0},{4,5},{5,6},{6,7},{7,4},{8,9},{9,10},{10,1... | collective-permute-start | bytes 196808 | tf_op jit(solution)/shard_map/ppermute | solution.py:16
  55.0 5.0 %collective-permute-start.8 = (bf16[16,2050]{1,0:T(8,128)(2,1)S(1)}, bf16[16,2050]{1,0:T(8,128)(2,1)}, u32[]{:S(2)}, u32[]{:S(2)}) collective-permute-start(bf16[16,2050]{1,0:T(8,128)(2,1)S(1)} %concatenate.21), channel_id=1, source_target_pairs={{0,2},{1,3},{2,0},{3,1},{4,6},{5,7},{6,4},{7,5},{8,10},{9,11},{10,... | collective-permute-start | bytes 196808 | tf_op jit(solution)/shard_map/ppermute | solution.py:16
  56.5 4.4 %collective-permute-start.9 = (bf16[16,2050]{1,0:T(8,128)(2,1)S(1)}, bf16[16,2050]{1,0:T(8,128)(2,1)}, u32[]{:S(2)}, u32[]{:S(2)}) collective-permute-start(bf16[16,2050]{1,0:T(8,128)(2,1)S(1)} %concatenate.22), channel_id=1, source_target_pairs={{0,3},{1,0},{2,1},{3,2},{4,7},{5,4},{6,5},{7,6},{8,11},{9,8},{10,9... | collective-permute-start | bytes 196808 | tf_op jit(solution)/shard_map/ppermute | solution.py:16
  63.4 4.4 %collective-permute-start.10 = (f32[16,544]{1,0:T(8,128)S(1)}, f32[16,544]{1,0:T(8,128)S(1)}, u32[]{:S(2)}, u32[]{:S(2)}) collective-permute-start(f32[16,544]{1,0:T(8,128)S(1)} %fusion.77), channel_id=1, source_target_pairs={{0,2},{1,3},{2,0},{3,1},{4,6},{5,7},{6,4},{7,5},{8,10},{9,11},{10,... | collective-permute-start | bytes 104456 | tf_op jit(solution)/shard_map/ppermute | solution.py:16
  63.9 4.0 %collective-permute-start.11 = (f32[16,544]{1,0:T(8,128)S(1)}, f32[16,544]{1,0:T(8,128)S(1)}, u32[]{:S(2)}, u32[]{:S(2)}) collective-permute-start(f32[16,544]{1,0:T(8,128)S(1)} %fusion.77), channel_id=1, source_target_pairs={{0,1},{1,2},{2,3},{3,0},{4,5},{5,6},{6,7},{7,4},{8,9},{9,10},{10,1... | collective-permute-start | bytes 104456 | tf_op jit(solution)/shard_map/ppermute | solution.py:16
  64.4 3.5 %collective-permute-start.12 = (f32[16,544]{1,0:T(8,128)S(1)}, f32[16,544]{1,0:T(8,128)S(1)}, u32[]{:S(2)}, u32[]{:S(2)}) collective-permute-start(f32[16,544]{1,0:T(8,128)S(1)} %fusion.77), channel_id=1, source_target_pairs={{0,3},{1,0},{2,1},{3,2},{4,7},{5,4},{6,5},{7,6},{8,11},{9,8},{10,9... | collective-permute-start | bytes 104456 | tf_op jit(solution)/shard_map/ppermute | solution.py:16
  67.9 6.2 %collective-permute-start.13 = (f32[16,544]{1,0:T(8,128)S(1)}, f32[16,544]{1,0:T(8,128)S(1)}, u32[]{:S(2)}, u32[]{:S(2)}) collective-permute-start(f32[16,544]{1,0:T(8,128)S(1)} %add_add_fusion.2), channel_id=1, source_target_pairs={{0,8},{4,12},{8,0},{12,4},{1,9},{5,13},{9,1},{13,5},{2,10},{6,14},... | collective-permute-start | bytes 104456 | tf_op jit(solution)/shard_map/ppermute | solution.py:16
  69.5 6.2 %collective-permute-start.14 = (f32[16,544]{1,0:T(8,128)S(1)}, f32[16,544]{1,0:T(8,128)S(1)}, u32[]{:S(2)}, u32[]{:S(2)}) collective-permute-start(f32[16,544]{1,0:T(8,128)S(1)} %add_add_fusion.2), channel_id=1, source_target_pairs={{0,4},{4,8},{8,12},{12,0},{1,5},{5,9},{9,13},{13,1},{2,6},{6,10},{... | collective-permute-start | bytes 104456 | tf_op jit(solution)/shard_map/ppermute | solution.py:16
  70.2 5.6 %collective-permute-start.15 = (f32[16,544]{1,0:T(8,128)S(1)}, f32[16,544]{1,0:T(8,128)S(1)}, u32[]{:S(2)}, u32[]{:S(2)}) collective-permute-start(f32[16,544]{1,0:T(8,128)S(1)} %add_add_fusion.2), channel_id=1, source_target_pairs={{0,12},{4,0},{8,4},{12,8},{1,13},{5,1},{9,5},{13,9},{2,14},{6,2},{... | collective-permute-start | bytes 104456 | tf_op jit(solution)/shard_map/ppermute | solution.py:16
  94.1 8.6 %collective-permute-start.16 = (bf16[16,2048]{1,0:T(8,128)(2,1)S(1)}, bf16[16,2048]{1,0:T(8,128)(2,1)S(1)}, u32[]{:S(2)}, u32[]{:S(2)}) collective-permute-start(bf16[16,2048]{1,0:T(8,128)(2,1)S(1)} %convolution_convert_fusion), channel_id=1, source_target_pairs={{0,8},{4,12},{8,0},{12,4},{1,9},{5,13},{9,1},{13,5},{2,10},{6,14},... | collective-permute-start | bytes 196616 | tf_op jit(solution)/shard_map/ppermute | solution.py:16
  95.3 7.5 %collective-permute-start.17 = (bf16[16,2048]{1,0:T(8,128)(2,1)S(1)}, bf16[16,2048]{1,0:T(8,128)(2,1)S(1)}, u32[]{:S(2)}, u32[]{:S(2)}) collective-permute-start(bf16[16,2048]{1,0:T(8,128)(2,1)S(1)} %convolution_convert_fusion), channel_id=1, source_target_pairs={{0,4},{4,8},{8,12},{12,0},{1,5},{5,9},{9,13},{13,1},{2,6},{6,10},{... | collective-permute-start | bytes 196616 | tf_op jit(solution)/shard_map/ppermute | solution.py:16
  98.0 5.5 %collective-permute-start.18 = (bf16[16,2048]{1,0:T(8,128)(2,1)S(1)}, bf16[16,2048]{1,0:T(8,128)(2,1)S(1)}, u32[]{:S(2)}, u32[]{:S(2)}) collective-permute-start(bf16[16,2048]{1,0:T(8,128)(2,1)S(1)} %convolution_convert_fusion), channel_id=1, source_target_pairs={{0,12},{4,0},{8,4},{12,8},{1,13},{5,1},{9,5},{13,9},{2,14},{6,2},{... | collective-permute-start | bytes 196616 | tf_op jit(solution)/shard_map/ppermute | solution.py:16
  (4 other events, 84.1 us)

commit v2 on v1

--- a/solution.py
+++ b/solution.py
@@ -3,12 +3,17 @@
 import jax
 import jax.numpy as jnp
 from jax import lax
+from jax.experimental import pallas as pl
+from jax.experimental.pallas import tpu as pltpu
 from jax.sharding import PartitionSpec as P
 
 BLOCK = 128
 EPS = 1e-06
 HS = ("head", "sub")
 DIRECT = 8
+LANES = 128
+MIB = 1024 * 1024
+FLOPS_AHEAD = 20_000_000_000
 
 
 def shifted(value, axes, hop):
@@ -39,16 +44,397 @@
     return upper, lax.reduce_precision(value - upper, 8, 7)
 
 
-def split_three(value):
-    upper, middle = split_pair(value)
-    return upper, middle, lax.reduce_precision(value - upper - middle, 8, 7)
-
-
 def rms_unit(values):
     return values * lax.rsqrt(jnp.mean(values * values, axis=-1, keepdims=True) + EPS)
 
 
+def tile_of(width, limit):
+    tile = width
+    while tile > limit and tile % 2 == 0 and (tile // 2) % 128 == 0:
+        tile //= 2
+    return tile
+
+
+def whole(count):
+    return [pl.BlockSpec(memory_space=pltpu.VMEM)] * count
+
+
 def attention(query, key_new, value_new, kv_cache, kv_scale, context_len):
+    requests, steps, heads, dim = query.shape
+    kv_heads = key_new.shape[2]
+    group = heads // kv_heads
+    cache_len = kv_cache.shape[2]
+    width = cache_len * kv_heads
+    blocks = kv_scale.shape[3]
+    inv_root = 1.0 / math.sqrt(dim)
+    lines = steps * heads
+    total_rows = requests * lines
+    news = steps * kv_heads
+
+    def kernel(length_ref, scale_ref, query_ref, cache_ref, key_ref, value_ref, out_ref):
+        shard = lax.axis_index("seq")
+        row = lax.broadcasted_iota(jnp.int32, (lines, width), 0)
+        column = lax.broadcasted_iota(jnp.int32, (lines, width), 1)
+        same = (row % heads) // group == column % kv_heads
+        place = shard * cache_len + column // kv_heads
+        new_row = lax.broadcasted_iota(jnp.int32, (lines, news), 0)
+        new_column = lax.broadcasted_iota(jnp.int32, (lines, news), 1)
+        new_live = (
+            ((new_row % heads) // group == new_column % kv_heads)
+            & (new_column // kv_heads <= new_row // heads)
+            & (shard == 0)
+        )
+        parity = lax.broadcasted_iota(jnp.int32, (1, kv_heads * BLOCK), 1) % kv_heads
+
+        def spread(which, request):
+            pieces = []
+            for block in range(blocks):
+                piece = jnp.full((1, kv_heads * BLOCK), scale_ref[which, request, 0, block])
+                for head in range(1, kv_heads):
+                    piece = jnp.where(parity == head, scale_ref[which, request, head, block], piece)
+                pieces.append(piece)
+            return jnp.concatenate(pieces, axis=1)
+
+        tops, totals = [], []
+        for request in range(requests):
+            asked = query_ref[request]
+            live = same & (place < length_ref[request])
+            scores = lax.dot_general(
+                asked, cache_ref[0, request], (((1,), (1,)), ((), ())), preferred_element_type=jnp.float32
+            )
+            scores = jnp.where(live, scores * spread(0, request) * inv_root, -1e30)
+            recent = lax.dot_general(
+                asked, key_ref[request], (((1,), (1,)), ((), ())), preferred_element_type=jnp.float32
+            )
+            recent = jnp.where(new_live, recent * inv_root, -1e30)
+            top = jnp.maximum(
+                jnp.max(scores, axis=1, keepdims=True), jnp.max(recent, axis=1, keepdims=True)
+            )
+            weight = jnp.where(live, jnp.exp(scores - top), 0.0)
+            new_weight = jnp.where(new_live, jnp.exp(recent - top), 0.0)
+            total = jnp.sum(weight, axis=1, keepdims=True) + jnp.sum(new_weight, axis=1, keepdims=True)
+            mix = jnp.dot(
+                (weight * spread(1, request)).astype(jnp.bfloat16),
+                cache_ref[1, request],
+                preferred_element_type=jnp.float32,
+            ) + jnp.dot(
+                new_weight.astype(jnp.bfloat16), value_ref[request], preferred_element_type=jnp.float32
+            )
+            for step in range(steps):
+                start = (step * requests + request) * heads
+                out_ref[start : start + heads, :] = mix[step * heads : (step + 1) * heads].astype(jnp.bfloat16)
+            tops.append(top)
+            totals.append(total)
+
+        def by_step(values):
+            return jnp.concatenate(
+                [value[step * heads : (step + 1) * heads] for step in range(steps) for value in values], axis=0
+            )
+
+        lane = lax.broadcasted_iota(jnp.int32, (total_rows, LANES), 1)
+        table = jnp.zeros((total_rows, LANES), jnp.float32)
+        for start, value in ((0, by_step(tops)), (3, by_step(totals))):
+            for k in range(3):
+                piece = value.astype(jnp.bfloat16).astype(jnp.float32)
+                table = jnp.where(lane == start + k, piece, table)
+                value = value - piece
+        turned = jnp.transpose(table)[:8]
+        out_ref[total_rows:, :] = jnp.concatenate(
+            [turned[:, k * LANES : (k + 1) * LANES] for k in range(total_rows // LANES)], axis=0
+        ).astype(jnp.bfloat16)
+
+    return pl.pallas_call(
+        kernel,
+        out_shape=jax.ShapeDtypeStruct((total_rows + total_rows // 16, dim), jnp.bfloat16),
+        in_specs=[pl.BlockSpec(memory_space=pltpu.SMEM)] * 2 + whole(4),
+        out_specs=whole(1)[0],
+        compiler_params=pltpu.CompilerParams(vmem_limit_bytes=6 * 1024 * 1024),
+        cost_estimate=pl.CostEstimate(flops=FLOPS_AHEAD, bytes_accessed=0, transcendentals=0),
+    )(
+        context_len,
+        kv_scale,
+        query.reshape(requests, lines, dim),
+        kv_cache.reshape(2, requests, width, dim),
+        key_new.reshape(requests, news, dim),
+        value_new.reshape(requests, news, dim),
+    )
+
+
+def cost(flops):
+    return pl.CostEstimate(flops=flops, bytes_accessed=0, transcendentals=0)
+
+
+def merge_project(parts, weight, rows, heads, dim):
+    lines = rows * heads
+    count = len(parts)
+    depth, width = weight.shape
+    tile = tile_of(width, 512)
+
+    def kernel(*refs):
+        part_refs, weight_ref, out_ref, mixed, chosen = refs[:count], refs[count], refs[-3], refs[-2], refs[-1]
+        tops, totals = [], []
+        for ref in part_refs:
+            stats = ref[lines:, :].astype(jnp.float32)
+            wide = jnp.concatenate([stats[k * 8 : (k + 1) * 8] for k in range(lines // LANES)], axis=1)
+            table = jnp.transpose(jnp.concatenate([wide, jnp.zeros((LANES - 8, lines), jnp.float32)], axis=0))
+            tops.append(table[:, 0:1] + table[:, 1:2] + table[:, 2:3])
+            totals.append(table[:, 3:4] + table[:, 4:5] + table[:, 5:6])
+        best = tops[0]
+        for top in tops[1:]:
+            best = jnp.maximum(best, top)
+        factors = [jnp.exp(top - best) for top in tops]
+        summed = paired_sum([total * factor for total, factor in zip(totals, factors)])
+        mixed[...] = (
+            paired_sum([ref[:lines, :].astype(jnp.float32) * factor for ref, factor in zip(part_refs, factors)])
+            / summed
+        )
+        for head in range(heads):
+            chosen[:, head * dim : (head + 1) * dim] = mixed[pl.ds(head, rows, stride=heads), :].astype(
+                jnp.bfloat16
+            )
+        for start in range(0, width, tile):
+            out_ref[:, start : start + tile] = jnp.dot(
+                chosen[...], weight_ref[:, start : start + tile], preferred_element_type=jnp.float32
+            ).astype(out_ref.dtype)
+
+    return pl.pallas_call(
+        kernel,
+        out_shape=jax.ShapeDtypeStruct((rows, width), jnp.bfloat16),
+        in_specs=whole(count + 1),
+        out_specs=whole(1)[0],
+        scratch_shapes=[pltpu.VMEM((lines, dim), jnp.float32), pltpu.VMEM((rows, heads * dim), jnp.bfloat16)],
+        compiler_params=pltpu.CompilerParams(vmem_limit_bytes=4 * MIB),
+        cost_estimate=cost(FLOPS_AHEAD),
+    )(*parts, weight)
+
+
+def add_residual(hidden, parts, gain):
+    rows, width = hidden.shape
+
+    def kernel(hidden_ref, gain_ref, *refs):
+        part_refs, (residual_ref, gained_ref, stats_ref) = refs[:-3], refs[-3:]
+        residual = hidden_ref[...].astype(jnp.float32) + paired_sum(
+            [ref[...].astype(jnp.float32) for ref in part_refs]
+        )
+        residual_ref[...] = residual
+        gained_ref[...] = (residual * gain_ref[...]).astype(jnp.bfloat16)
+        left = jnp.sum(residual * residual, axis=1, keepdims=True)
+        lane = lax.broadcasted_iota(jnp.int32, (rows, LANES), 1)
+        table = jnp.zeros((rows, LANES), jnp.float32)
+        for k in range(3):
+            piece = left.astype(jnp.bfloat16).astype(jnp.float32)
+            table = jnp.where(lane == k, piece, table)
+            left = left - piece
+        stats_ref[...] = table.astype(jnp.bfloat16)
+
+    return pl.pallas_call(
+        kernel,
+        out_shape=(
+            jax.ShapeDtypeStruct((rows, width), jnp.float32),
+            jax.ShapeDtypeStruct((rows, width), jnp.bfloat16),
+            jax.ShapeDtypeStruct((rows, LANES), jnp.bfloat16),
+        ),
+        in_specs=whole(2 + len(parts)),
+        out_specs=tuple(whole(3)),
+        compiler_params=pltpu.CompilerParams(vmem_limit_bytes=4 * MIB),
+        cost_estimate=cost(rows * width * 8),
+    )(hidden, gain.reshape(1, width), *parts)
+
+
+def hs_position():
+    return lax.axis_index("head") * lax.axis_size("sub") + lax.axis_index("sub")
+
+
+def project_block(gained, weight, stats, own_width, hop):
+    rows, depth = gained.shape
+    count = lax.axis_size(HS)
+    width = 2 * own_width
+    tile = tile_of(own_width, 512)
+    kind = jnp.bfloat16 if hop else jnp.float32
+
+    def kernel(gained_ref, weight_ref, stats_ref, out_ref):
+        base = ((hs_position() + hop) % count) * own_width
+        for part in range(2):
+            for start in range(0, own_width, tile):
+                columns = pl.ds(pl.multiple_of(base + start, tile), tile)
+                out_ref[:, part * own_width + start : part * own_width + start + tile] = jnp.dot(
+                    gained_ref[...], weight_ref[part, :, columns], preferred_element_type=jnp.float32
+                ).astype(kind)
+        if hop:
+            out_ref[:, width:] = stats_ref[...]
+
+    return pl.pallas_call(
+        kernel,
+        out_shape=jax.ShapeDtypeStruct((rows, width + (LANES if hop else 0)), kind),
+        in_specs=whole(3),
+        out_specs=whole(1)[0],
+        compiler_params=pltpu.CompilerParams(vmem_limit_bytes=4 * MIB),
+        cost_estimate=cost(2 * rows * depth * width),
+    )(gained, weight, stats)
+
+
+def convolve(own, received, stats, state, taps, bias, weight, features):
+    rows, width = own.shape
+    own_width = width // 2
+    requests = state.shape[1]
+    taps_count = taps.shape[0]
+    mixed_width = weight.shape[0]
+    count = len(received)
+
+    def kernel(own_ref, stats_ref, state_ref, taps_ref, bias_ref, weight_ref, *refs):
+        received_refs, (conv_ref, gate_ref, mixing_ref) = refs[:count], refs[count:]
+        pieces = stats_ref[...].astype(jnp.float32)
+        channels = own_ref[...]
+        for ref in received_refs:
+            channels = channels + ref[:, :width].astype(jnp.float32)
+            pieces = pieces + ref[:, width:].astype(jnp.float32)
+        squares = jnp.sum(pieces, axis=1, keepdims=True)
+        channels = (channels * lax.rsqrt(squares / features + EPS)).astype(jnp.bfloat16)
+        gate_ref[...] = channels[:, own_width:]
+        window = jnp.concatenate(
+            [state_ref[k].astype(jnp.float32) for k in range(taps_count - 1)]
+            + [channels[:, :own_width].astype(jnp.float32)],
+            axis=0,
+        )
+        total = bias_ref[...]
+        for tap in range(taps_count):
+            total = total + taps_ref[tap : tap + 1, :].astype(jnp.float32) * window[
+                tap * requests : tap * requests + rows
+            ]
+        conv = (total * jax.nn.sigmoid(total)).astype(jnp.bfloat16)
+        conv_ref[...] = conv
+        mixing_ref[...] = lax.dot_general(
+            conv, weight_ref[...], (((1,), (1,)), ((), ())), preferred_element_type=jnp.float32
+        )
+
+    return pl.pallas_call(
+        kernel,
+        out_shape=(
+            jax.ShapeDtypeStruct((rows, own_width), jnp.bfloat16),
+            jax.ShapeDtypeStruct((rows, own_width), jnp.bfloat16),
+            jax.ShapeDtypeStruct((rows, mixed_width), jnp.float32),
+        ),
+        in_specs=whole(6 + count),
+        out_specs=tuple(whole(3)),
+        compiler_params=pltpu.CompilerParams(vmem_limit_bytes=8 * MIB),
+        cost_estimate=cost(FLOPS_AHEAD),
+    )(own, stats, state, taps, bias, weight, *received)
+
+
+def scan_states(mixing, conv, gate, dt_weight, dt_bias, decay, skip, state):
+    rows, own_width = conv.shape
+    requests, state_width = state.shape[:2]
+    low_width = dt_weight.shape[0]
+
+    def kernel(mixing_ref, conv_ref, gate_ref, dt_ref, bias_ref, decay_ref, skip_ref, state_ref, *refs):
+        gated_ref, next_ref, out = refs
+        low = mixing_ref[:, :low_width]
+        low_rank = (low * lax.rsqrt(jnp.mean(low * low, axis=1, keepdims=True) + EPS)).astype(jnp.bfloat16)
+        step_size = jnp.dot(low_rank, dt_ref[...], preferred_element_type=jnp.float32) + bias_ref[...]
+        step_size = jnp.maximum(step_size, 0.0) + jnp.log1p(jnp.exp(-jnp.abs(step_size)))
+        mats = mixing_ref[:, low_width : low_width + 2 * state_width]
+        lane = lax.broadcasted_iota(jnp.int32, mats.shape, 1)
+        power = mats * mats
+        first = jnp.sum(jnp.where(lane < state_width, power, 0.0), axis=1, keepdims=True)
+        second = jnp.sum(jnp.where(lane < state_width, 0.0, power), axis=1, keepdims=True)
+        mats = mats * lax.rsqrt(jnp.where(lane < state_width, first, second) / state_width + EPS)
+        mats = jnp.concatenate([mats, jnp.zeros((rows, LANES - 2 * state_width), jnp.float32)], axis=1)
+        turned = jnp.transpose(jnp.concatenate([mats, jnp.zeros((LANES - rows, LANES), jnp.float32)], axis=0))
+        signal = conv_ref[...].astype(jnp.float32)
+        drive = step_size * signal
+        decay = decay_ref[...]
+        for request in range(requests):
+            memory = state_ref[request]
+            for row in range(request, rows, requests):
+                memory = (
+                    jnp.exp(-step_size[row : row + 1] * decay) * memory
+                    + drive[row : row + 1] * turned[:state_width, row : row + 1]
+                )
+                out[row : row + 1, :] = jnp.sum(
+                    memory * turned[state_width : 2 * state_width, row : row + 1], axis=0, keepdims=True
+                )
+            next_ref[request] = memory
+        gate = gate_ref[...].astype(jnp.float32)
+        gated_ref[...] = ((out[...] + skip_ref[...] * signal) * (gate * jax.nn.sigmoid(gate))).astype(
+            jnp.bfloat16
+        )
+
+    return pl.pallas_call(
+        kernel,
+        out_shape=(
+            jax.ShapeDtypeStruct((rows, own_width), jnp.bfloat16),
+            jax.ShapeDtypeStruct(state.shape, jnp.float32),
+        ),
+        in_specs=whole(8),
+        out_specs=tuple(whole(2)),
+        scratch_shapes=[pltpu.VMEM((rows, own_width), jnp.float32)],
+        compiler_params=pltpu.CompilerParams(vmem_limit_bytes=8 * MIB),
+        cost_estimate=cost(FLOPS_AHEAD // 4),
+    )(mixing, conv, gate, dt_weight, dt_bias, decay, skip, state)
+
+
+def project_out(blocks, hops, weight, before):
+    rows, own_width = blocks[0].shape
+    count = lax.axis_size(HS)
+    width = weight.shape[1]
+    tile = tile_of(width, 512)
+    kind = jnp.float32 if before is None else jnp.bfloat16
+
+    def kernel(*refs):
+        block_refs, weight_ref, out_ref = refs[: len(hops)], refs[len(hops)], refs[-1]
+        for start in range(0, width, tile):
+            columns = slice(start, start + tile)
+            terms = []
+            for ref, hop in zip(block_refs, hops):
+                base = pl.multiple_of(((hs_position() + count - hop) % count) * own_width, own_width)
+                terms.append(
+                    jnp.dot(
+                        ref[...], weight_ref[pl.ds(base, own_width), columns], preferred_element_type=jnp.float32
+                    )
+                )
+            total = terms[0]
+            for term in terms[1:]:
+                total = total + term
+            if before is not None:
+                total = total + refs[len(hops) + 1][:, columns]
+            out_ref[:, columns] = total.astype(kind)
+
+    extra = () if before is None else (before,)
+    return pl.pallas_call(
+        kernel,
+        out_shape=jax.ShapeDtypeStruct((rows, width), kind),
+        in_specs=whole(len(blocks) + 1 + len(extra)),
+        out_specs=whole(1)[0],
+        compiler_params=pltpu.CompilerParams(vmem_limit_bytes=4 * MIB),
+        cost_estimate=cost(2 * rows * own_width * width * len(hops)),
+    )(*blocks, weight, *extra)
+
+
+def finish(residual, parts, requests):
+    rows, width = residual.shape
+    steps = rows // requests
+
+    def kernel(residual_ref, *refs):
+        part_refs, out_ref, total = refs[:-2], refs[-2], refs[-1]
+        total[...] = residual_ref[...] + paired_sum([ref[...].astype(jnp.float32) for ref in part_refs])
+        for request in range(requests):
+            out_ref[request] = jnp.concatenate(
+                [total[step * requests + request : step * requests + request + 1, :] for step in range(steps)],
+                axis=0,
+            ).astype(jnp.bfloat16)
+
+    return pl.pallas_call(
+        kernel,
+        out_shape=jax.ShapeDtypeStruct((requests, steps, width), jnp.bfloat16),
+        in_specs=whole(1 + len(parts)),
+        out_specs=whole(1)[0],
+        scratch_shapes=[pltpu.VMEM((rows, width), jnp.float32)],
+        compiler_params=pltpu.CompilerParams(vmem_limit_bytes=4 * MIB),
+        cost_estimate=cost(rows * width * 8),
+    )(residual, *parts)
+
+
+def plain_attention(query, key_new, value_new, kv_cache, kv_scale, context_len):
     requests, steps, heads, dim = query.shape
     kv_heads = key_new.shape[2]
     group = heads // kv_heads
@@ -102,7 +488,7 @@
     return (mixed / summed[..., None]).astype(jnp.bfloat16)
 
 
-def local(
+def plain(
     hidden,
     query,
     key_new,
@@ -131,29 +517,13 @@
     hs_index = lax.axis_index(HS)
     heads = query.shape[2]
     dim = query.shape[3]
-    mix, top, total = attention(query, key_new, value_new, kv_cache, kv_scale, context_len)
-    if seq_count == hs_count:
-        packed = jnp.concatenate(
-            [mix.reshape(rows, heads * dim)] + list(split_three(top)) + list(split_three(total)), axis=1
-        ).astype(jnp.bfloat16)
-        swap = [(s * hs_count + j, j * hs_count + s) for s in range(seq_count) for j in range(hs_count)]
-        swapped = lax.ppermute(packed, ("seq",) + HS, swap)
-        parts = everyone(lax.optimization_barrier(swapped), HS)
-        base = heads * dim
-        piece = lambda part, k: part[:, base + k * heads : base + (k + 1) * heads].astype(jnp.float32)
-        three = lambda part, k: piece(part, k) + piece(part, k + 1) + piece(part, k + 2)
-        chosen = merge(
-            [part[:, :base].reshape(rows, heads, dim) for part in parts],
-            [three(part, 0) for part in parts],
-            [three(part, 3) for part in parts],
-        ).reshape(rows, base)
-    else:
-        mixes, tops, totals = (lax.all_gather(part, "seq") for part in (mix, top, total))
-        every = range(seq_count)
-        own_heads = merge([mixes[k] for k in every], [tops[k] for k in every], [totals[k] for k in every])
-        every_head = lax.all_gather(own_heads.reshape(rows, heads * dim), HS, axis=1, tiled=True)
-        width_in = attn_out_weight.shape[0]
-        chosen = lax.dynamic_slice_in_dim(every_head, lax.axis_index("seq") * width_in, width_in, 1)
+    mix, top, total = plain_attention(query, key_new, value_new, kv_cache, kv_scale, context_len)
+    mixes, tops, totals = (lax.all_gather(part, "seq") for part in (mix, top, total))
+    every = range(seq_count)
+    own_heads = merge([mixes[k] for k in every], [tops[k] for k in every], [totals[k] for k in every])
+    every_head = lax.all_gather(own_heads.reshape(rows, heads * dim), HS, axis=1, tiled=True)
+    width_in = attn_out_weight.shape[0]
+    chosen = lax.dynamic_slice_in_dim(every_head, lax.axis_index("seq") * width_in, width_in, 1)
     attended = sum_over(
         jnp.dot(chosen, attn_out_weight, preferred_element_type=jnp.float32), "seq", jnp.bfloat16
     )
@@ -222,6 +592,115 @@
     )
     final = (residual + mamba_part).astype(jnp.bfloat16).reshape(requests, steps, -1)
     return (final, memory)
+
+
+def local(
+    hidden,
+    query,
+    key_new,
+    value_new,
+    kv_cache,
+    kv_scale,
+    context_len,
+    attn_out_weight,
+    norm_gain,
+    in_weight,
+    conv_weight,
+    conv_bias,
+    conv_state,
+    xproj_weight,
+    dt_weight,
+    dt_bias,
+    decay_rate,
+    skip_gain,
+    ssm_state,
+    mamba_out_weight,
+):
+    requests, steps = hidden.shape[:2]
+    rows = requests * steps
+    seq_count = lax.axis_size("seq")
+    hs_count = lax.axis_size(HS)
+    heads, dim = query.shape[2:]
+    own_width = conv_weight.shape[0]
+    if (
+        seq_count != hs_count
+        or seq_count > DIRECT
+        or own_width % LANES
+        or dim != LANES
+        or (rows * heads) % LANES
+        or rows % 16
+    ):
+        return plain(
+            hidden,
+            query,
+            key_new,
+            value_new,
+            kv_cache,
+            kv_scale,
+            context_len,
+            attn_out_weight,
+            norm_gain,
+            in_weight,
+            conv_weight,
+            conv_bias,
+            conv_state,
+            xproj_weight,
+            dt_weight,
+            dt_bias,
+            decay_rate,
+            skip_gain,
+            ssm_state,
+            mamba_out_weight,
+        )
+    part = attention(query, key_new, value_new, kv_cache, kv_scale, context_len)
+    parts = [
+        lax.ppermute(
+            part,
+            ("seq",) + HS,
+            [
+                (s * hs_count + j, j * hs_count + (s + hop) % hs_count)
+                for s in range(seq_count)
+                for j in range(hs_count)
+            ],
+        )
+        for hop in range(hs_count)
+    ]
+    partial = merge_project(parts, attn_out_weight, rows, heads, dim)
+    step_hidden = hidden.transpose(1, 0, 2).reshape(rows, -1)
+    features = step_hidden.shape[1] * hs_count
+    residual, gained, stats = add_residual(step_hidden, everyone(partial, "seq"), norm_gain)
+    received = []
+    for hop in range(1, hs_count):
+        block = project_block(gained, in_weight, stats, own_width, hop)
+        received.append(shifted(block, HS, hop))
+    own = project_block(gained, in_weight, stats, own_width, 0)
+    conv, gate, mixing = convolve(
+        own,
+        received,
+        stats,
+        conv_state.transpose(1, 0, 2),
+        conv_weight.T,
+        conv_bias.reshape(1, -1),
+        xproj_weight.T,
+        features,
+    )
+    mixing = sum_over(sum_over(mixing, HS), "seq")
+    gated, state = scan_states(
+        mixing,
+        conv,
+        gate,
+        dt_weight,
+        dt_bias.reshape(1, -1),
+        decay_rate.T,
+        skip_gain.reshape(1, -1),
+        ssm_state.transpose(0, 2, 1),
+    )
+    hops = range(1, hs_count)
+    blocks = [shifted(gated, HS, hop) for hop in hops]
+    first = project_out([gated], [0], mamba_out_weight, None)
+    partial = project_out(blocks, hops, mamba_out_weight, first)
+    final = finish(residual, everyone(partial, "seq"), requests)
+    return final, state.transpose(0, 2, 1)
 
 
 def solution(mesh):

time: 105 us -> 86.5 us (0.82)
  matrix products: 30.6 us -> 0 us
  Pallas kernels: 0 us -> 14.2 us
  waiting for transfers between devices: 16.3 us -> 29.6 us
  other arithmetic: 8.51 us -> 0.02 us
  starting transfers between devices: 34.1 us -> 25.8 us
  local copies, waits for them, and re-layouts: 7.9 us -> 15.6 us
  blocking collectives: 5.61 us -> 0 us
    dot_general x9 -> x0, matrix products: 30.6 us -> none  [the longest x1 12.9 us: local(): jnp.einsum('nd,cde->nce', gained, in_weight, preferred_element_type=jnp.f...]
    unnamed x28 -> x45, local copies, waits for them, and re-layouts: 0.72 us -> 15.6 us
    pallas_call x0 -> x12, Pallas kernels: none -> 14.2 us  [the longest x4 4.78 us: project_block(): pl.pallas_call(kernel, out_shape=jax.ShapeDtypeStruct((rows, width + (LAN...]
    ppermute x18, starting transfers between devices: 33.4 us -> 19.5 us  [shifted(): lax.ppermute(value, axes, [(i, (i + hop) % count) for i in range(count)])]
    ppermute x1 -> x4, waiting for transfers between devices: 0.01 us -> 7.25 us  [local(): lax.ppermute(part, ('seq',) + HS, [(s * hs_count + j, j * hs_count + (s +...]
    ppermute x18, waiting for transfers between devices: 16.3 us -> 22.4 us  [shifted(): lax.ppermute(value, axes, [(i, (i + hop) % count) for i in range(count)])]
    ppermute x1 -> x4, starting transfers between devices: 0.66 us -> 6.32 us  [local(): lax.ppermute(part, ('seq',) + HS, [(s * hs_count + j, j * hs_count + (s +...]
    all_gather x1 -> x0, blocking collectives: 5.61 us -> none  [local(): gated_block = lax.all_gather(gated_out, HS, axis=1, tiled=True)]
  transfers between devices with their start and end apart: 19 -> 22, of which waited for: 11 -> 14; matrix products, arithmetic and copies ran while one was open for 4% -> 0% of each run, Pallas kernels for 0% -> 2%
where the time goes in v2:
time: 86.5 us; the launch traced here: 86.2 us
  waiting for transfers between devices  29.6 us (34%)
  starting transfers between devices  25.8 us (30%)
  local copies, waits for them, and re-layouts  15.6 us (18%)
  Pallas kernels  14.2 us (16%)
  between operations  0.87 us (1%)
    ppermute x18, waiting for transfers between devices, shifted(): lax.ppermute(value, axes, [(i, (i + hop) % count) for i in range(count)])  22.4 us
    ppermute x18, starting transfers between devices, shifted(): lax.ppermute(value, axes, [(i, (i + hop) % count) for i in range(count)])  19.5 us
    unnamed x45, local copies, waits for them, and re-layouts  15.6 us
    ppermute x4, waiting for transfers between devices, local(): lax.ppermute(part, ('seq',) + HS, [(s * hs_count + j, j * hs_count + (s +...  7.25 us
    ppermute x4, starting transfers between devices, local(): lax.ppermute(part, ('seq',) + HS, [(s * hs_count + j, j * hs_count + (s +...  6.32 us
    pallas_call x4, Pallas kernels, project_block(): pl.pallas_call(kernel, out_shape=jax.ShapeDtypeStruct((rows, width + (LAN...  4.78 us
    pallas_call x2, Pallas kernels, project_out(): pl.pallas_call(kernel, out_shape=jax.ShapeDtypeStruct((rows, width), kind...  2.39 us
    pallas_call x1, Pallas kernels, attention(): pl.pallas_call(kernel, out_shape=jax.ShapeDtypeStruct((total_rows + total...  2.35 us
  transfers between devices with their start and end apart: 22, of which 14 were waited for; matrix products, arithmetic and copies ran while one was open for 0% of the time, Pallas kernels for 2%

profile of v2, /device:TPU:0, one launch (start us, length us, event | category | flops | bytes accessed | tf_op | source)
XLA Modules:
  0.0 86.2 jit_solution(13003930105739332731)
XLA Ops:
  1.4 1.2 %copy-done.4 = bf16[2,4,256,2,128]{4,3,2,1,0:T(2,128)(2,1)S(1)} copy-done((bf16[2,4,256,2,128]{4,3,2,1,0:T(2,128)(2,1)S(1)}, bf16[2,4,256,2,128]{4,3,2,1,0:T(2,128)(2,1)}, u32[]{:S(2)}) %copy-start.4) | copy-done | bytes 1048600
  5.5 2.4 %shard_map.203 = bf16[272,128]{1,0:T(8,128)(2,1)S(1)} custom-call(s32[4]{0:T(128)S(1)} %copy-done.16, f32[2,4,2,2]{3,2,1,0:T(2,128)S(1)} %copy.23.scale_ref, bf16[4,64,128]{2,1,0:T(8,128)(2,1)S(1)} %bitcast.21, bf16[2,4,512,128]{3,2,1,0:T(8,128)(2,1)S(1)} %bitcast.19, bf16[4,8,128]{2,1,0:T(8,128)(2,1)S(1)} %bitcast.24, bf16[4,8,128]{2,1,0:T(8,128)(2,1)S(1)} %bitcast.25), custom_call_target="tpu_custom_call" | custom-call | flops 20000000000 | tf_op jit(solution)/shard_map/pallas_call | solution.py:146
  7.9 2.4 %collective-permute-start.3 = (bf16[272,128]{1,0:T(8,128)(2,1)S(1)}, bf16[272,128]{1,0:T(8,128)(2,1)S(1)}, u32[]{:S(2)}, u32[]{:S(2)}) collective-permute-start(bf16[272,128]{1,0:T(8,128)(2,1)S(1)} %shard_map.203), channel_id=1, source_target_pairs={{0,3},{1,7},{2,11},{3,15},{4,0},{5,4},{6,8},{7,12},{8,1},{9,5},{10... | collective-permute-start | bytes 208904 | tf_op jit(solution)/shard_map/ppermute | solution.py:657
  10.3 2.6 %collective-permute-start.2 = (bf16[272,128]{1,0:T(8,128)(2,1)S(1)}, bf16[272,128]{1,0:T(8,128)(2,1)S(1)}, u32[]{:S(2)}, u32[]{:S(2)}) collective-permute-start(bf16[272,128]{1,0:T(8,128)(2,1)S(1)} %shard_map.203), channel_id=1, source_target_pairs={{0,2},{1,6},{2,10},{3,14},{4,3},{5,7},{6,11},{7,15},{8,0},{9,4},{1... | collective-permute-start | bytes 208904 | tf_op jit(solution)/shard_map/ppermute | solution.py:657
  14.2 7.2 %collective-permute-done.2.refs_2_ = bf16[272,128]{1,0:T(8,128)(2,1)S(1)} collective-permute-done((bf16[272,128]{1,0:T(8,128)(2,1)S(1)}, bf16[272,128]{1,0:T(8,128)(2,1)S(1)}, u32[]{:S(2)}, u32[]{:S(2)}) %collective-permute-start.2) | collective-permute-done | bytes 69664 | tf_op jit(solution)/shard_map/ppermute | solution.py:657
  21.5 1.9 %shard_map.204.refs_0_ = bf16[16,2048]{1,0:T(8,128)(2,1)S(1)} custom-call(bf16[272,128]{1,0:T(8,128)(2,1)S(1)} %collective-permute-done.refs_0_, bf16[272,128]{1,0:T(8,128)(2,1)S(1)} %collective-permute-done.1.refs_1_, bf16[272,128]{1,0:T(8,128)(2,1)S(1)} %collective-permute-done.2.refs_2_, bf16[272,128]{1,0:T(8,128)(2,1)S(1)} %collective-permute-done.3.refs_3_, ...), custom_call_target="tpu_custom_call" | custom-call | flops 20000000000 | tf_op jit(solution)/shard_map/pallas_call | solution.py:200
  23.4 3.7 %collective-permute-start.6 = (bf16[16,2048]{1,0:T(8,128)(2,1)S(1)}, bf16[16,2048]{1,0:T(8,128)(2,1)S(1)}, u32[]{:S(2)}, u32[]{:S(2)}) collective-permute-start(bf16[16,2048]{1,0:T(8,128)(2,1)S(1)} %shard_map.204.refs_0_), channel_id=1, source_target_pairs={{0,12},{4,0},{8,4},{12,8},{1,13},{5,1},{9,5},{13,9},{2,14},{6,2},{... | collective-permute-start | bytes 196616 | tf_op jit(solution)/shard_map/ppermute | solution.py:21
  27.1 1.9 %collective-permute-start.4 = (bf16[16,2048]{1,0:T(8,128)(2,1)S(1)}, bf16[16,2048]{1,0:T(8,128)(2,1)S(1)}, u32[]{:S(2)}, u32[]{:S(2)}) collective-permute-start(bf16[16,2048]{1,0:T(8,128)(2,1)S(1)} %shard_map.204.refs_0_), channel_id=1, source_target_pairs={{0,4},{4,8},{8,12},{12,0},{1,5},{5,9},{9,13},{13,1},{2,6},{6,10},{... | collective-permute-start | bytes 196616 | tf_op jit(solution)/shard_map/ppermute | solution.py:21
  29.1 5.1 %collective-permute-done.5.refs_2_ = bf16[16,2048]{1,0:T(8,128)(2,1)S(1)} collective-permute-done((bf16[16,2048]{1,0:T(8,128)(2,1)S(1)}, bf16[16,2048]{1,0:T(8,128)(2,1)S(1)}, u32[]{:S(2)}, u32[]{:S(2)}) %collective-permute-start.5) | collective-permute-done | bytes 65568 | tf_op jit(solution)/shard_map/ppermute | solution.py:21
  34.3 10.6 %copy-done = bf16[2,2048,4096]{2,1,0:T(8,128)(2,1)S(1)} copy-done((bf16[2,2048,4096]{2,1,0:T(8,128)(2,1)S(1)}, bf16[2,2048,4096]{2,1,0:T(8,128)(2,1)}, u32[]{:S(2)}) %copy-start) | copy-done | bytes 33554456
  48.5 1.6 %collective-permute-start.7 = (bf16[16,2176]{1,0:T(8,128)(2,1)S(1)}, bf16[16,2176]{1,0:T(8,128)(2,1)S(1)}, u32[]{:S(2)}, u32[]{:S(2)}) collective-permute-start(bf16[16,2176]{1,0:T(8,128)(2,1)S(1)} %shard_map.207), channel_id=1, source_target_pairs={{0,1},{1,2},{2,3},{3,0},{4,5},{5,6},{6,7},{7,4},{8,9},{9,10},{10,1... | collective-permute-start | bytes 208904 | tf_op jit(solution)/shard_map/ppermute | solution.py:21
  50.1 1.3 %collective-permute-start.8 = (bf16[16,2176]{1,0:T(8,128)(2,1)S(1)}, bf16[16,2176]{1,0:T(8,128)(2,1)S(1)}, u32[]{:S(2)}, u32[]{:S(2)}) collective-permute-start(bf16[16,2176]{1,0:T(8,128)(2,1)S(1)} %shard_map.208), channel_id=1, source_target_pairs={{0,2},{1,3},{2,0},{3,1},{4,6},{5,7},{6,4},{7,5},{8,10},{9,11},{10,... | collective-permute-start | bytes 208904 | tf_op jit(solution)/shard_map/ppermute | solution.py:21
  51.4 1.4 %collective-permute-start.9 = (bf16[16,2176]{1,0:T(8,128)(2,1)S(1)}, bf16[16,2176]{1,0:T(8,128)(2,1)S(1)}, u32[]{:S(2)}, u32[]{:S(2)}) collective-permute-start(bf16[16,2176]{1,0:T(8,128)(2,1)S(1)} %shard_map.209), channel_id=1, source_target_pairs={{0,3},{1,0},{2,1},{3,2},{4,7},{5,4},{6,5},{7,6},{8,11},{9,8},{10,9... | collective-permute-start | bytes 208904 | tf_op jit(solution)/shard_map/ppermute | solution.py:21
  55.4 1.9 %collective-permute-start.12 = (f32[16,544]{1,0:T(8,128)S(1)}, f32[16,544]{1,0:T(8,128)S(1)}, u32[]{:S(2)}, u32[]{:S(2)}) collective-permute-start(f32[16,544]{1,0:T(8,128)S(1)} %get-tuple-element.13), channel_id=1, source_target_pairs={{0,3},{1,0},{2,1},{3,2},{4,7},{5,4},{6,5},{7,6},{8,11},{9,8},{10,9... | collective-permute-start | bytes 104456 | tf_op jit(solution)/shard_map/ppermute | solution.py:21
  57.9 1.3 %collective-permute-done.12 = f32[16,544]{1,0:T(8,128)S(1)} collective-permute-done((f32[16,544]{1,0:T(8,128)S(1)}, f32[16,544]{1,0:T(8,128)S(1)}, u32[]{:S(2)}, u32[]{:S(2)}) %collective-permute-start.12) | collective-permute-done | bytes 34848 | tf_op jit(solution)/shard_map/ppermute | solution.py:21
  59.2 1.5 %collective-permute-done.11 = f32[16,544]{1,0:T(8,128)S(1)} collective-permute-done((f32[16,544]{1,0:T(8,128)S(1)}, f32[16,544]{1,0:T(8,128)S(1)}, u32[]{:S(2)}, u32[]{:S(2)}) %collective-permute-start.11) | collective-permute-done | bytes 34848 | tf_op jit(solution)/shard_map/ppermute | solution.py:21
  61.6 1.5 %collective-permute-start.15 = (f32[16,544]{1,0:T(8,128)S(1)}, f32[16,544]{1,0:T(8,128)S(1)}, u32[]{:S(2)}, u32[]{:S(2)}) collective-permute-start(f32[16,544]{1,0:T(8,128)S(1)} %add_add_fusion.1), channel_id=1, source_target_pairs={{0,12},{4,0},{8,4},{12,8},{1,13},{5,1},{9,5},{13,9},{2,14},{6,2},{... | collective-permute-start | bytes 104456 | tf_op jit(solution)/shard_map/ppermute | solution.py:21
  65.7 3.2 %collective-permute-done.14 = f32[16,544]{1,0:T(8,128)S(1)} collective-permute-done((f32[16,544]{1,0:T(8,128)S(1)}, f32[16,544]{1,0:T(8,128)S(1)}, u32[]{:S(2)}, u32[]{:S(2)}) %collective-permute-start.14) | collective-permute-done | bytes 34848 | tf_op jit(solution)/shard_map/ppermute | solution.py:21
  69.5 1.4 %shard_map.211 = (bf16[16,1024]{1,0:T(8,128)(2,1)S(1)}, f32[4,16,1024]{2,1,0:T(8,128)}) custom-call(f32[16,544]{1,0:T(8,128)S(1)} %add_add_fusion.mixing_ref, bf16[16,1024]{1,0:T(8,128)(2,1)S(1)} %get-tuple-element.14.conv_ref, bf16[16,1024]{1,0:T(8,128)(2,1)S(1)} %get-tuple-element.15.gate_ref, bf16[512,1024]{1,0:T(8,128)(2,1)S(1)} %copy-done.5, ...), custom_call_target="tpu_custom_call" | custom-call | flops 5000000000 | tf_op jit(solution)/shard_map/pallas_call | solution.py:362
  72.6 2.6 %collective-permute-done.17.refs_1_ = bf16[16,1024]{1,0:T(8,128)(2,1)S(1)} collective-permute-done((bf16[16,1024]{1,0:T(8,128)(2,1)S(1)}, bf16[16,1024]{1,0:T(8,128)(2,1)S(1)}, u32[]{:S(2)}, u32[]{:S(2)}) %collective-permute-start.17) | collective-permute-done | bytes 32800 | tf_op jit(solution)/shard_map/ppermute | solution.py:21
  75.3 1.7 %shard_map.213.refs_0_ = bf16[16,2048]{1,0:T(8,128)(2,1)S(1)} custom-call(bf16[16,1024]{1,0:T(8,128)(2,1)S(1)} %collective-permute-done.16.refs_0_, bf16[16,1024]{1,0:T(8,128)(2,1)S(1)} %collective-permute-done.17.refs_1_, bf16[16,1024]{1,0:T(8,128)(2,1)S(1)} %collective-permute-done.18.refs_2_, bf16[4096,2048]{1,0:T(8,128)(2,1)S(1)} %bitcast.16, ...), custom_call_target="tpu_custom_call" | custom-call | flops 201326592 | tf_op jit(solution)/shard_map/pallas_call | solution.py:403
  77.0 2.3 %collective-permute-start.21 = (bf16[16,2048]{1,0:T(8,128)(2,1)S(1)}, bf16[16,2048]{1,0:T(8,128)(2,1)S(1)}, u32[]{:S(2)}, u32[]{:S(2)}) collective-permute-start(bf16[16,2048]{1,0:T(8,128)(2,1)S(1)} %shard_map.213.refs_0_), channel_id=1, source_target_pairs={{0,12},{4,0},{8,4},{12,8},{1,13},{5,1},{9,5},{13,9},{2,14},{6,2},{... | collective-permute-start | bytes 196616 | tf_op jit(solution)/shard_map/ppermute | solution.py:21
  79.9 1.4 %collective-permute-done.21.refs_3_ = bf16[16,2048]{1,0:T(8,128)(2,1)S(1)} collective-permute-done((bf16[16,2048]{1,0:T(8,128)(2,1)S(1)}, bf16[16,2048]{1,0:T(8,128)(2,1)S(1)}, u32[]{:S(2)}, u32[]{:S(2)}) %collective-permute-start.21) | collective-permute-done | bytes 65568 | tf_op jit(solution)/shard_map/ppermute | solution.py:21
  81.3 3.3 %collective-permute-done.20.refs_2_ = bf16[16,2048]{1,0:T(8,128)(2,1)S(1)} collective-permute-done((bf16[16,2048]{1,0:T(8,128)(2,1)S(1)}, bf16[16,2048]{1,0:T(8,128)(2,1)S(1)}, u32[]{:S(2)}, u32[]{:S(2)}) %collective-permute-start.20) | collective-permute-done | bytes 65568 | tf_op jit(solution)/shard_map/ppermute | solution.py:21
  (82 shorter events, 19.9 us)
Async XLA Ops:
  7.9 21.1 %copy-start.17 = (bf16[4,4,2048]{2,1,0:T(4,128)(2,1)S(1)}, bf16[4,4,2048]{2,1,0:T(4,128)(2,1)}, u32[]{:S(2)}) copy-start(bf16[4,4,2048]{2,1,0:T(4,128)(2,1)} %param.20) | copy-start | bytes 196612
  7.9 26.3 %copy-start.1 = (f32[2048]{0:T(1024)S(1)}, f32[2048]{0:T(1024)}, u32[]{:S(2)}) copy-start(f32[2048]{0:T(1024)} %param.28) | copy-start | bytes 24580
  7.9 6.3 %collective-permute-start.3 = (bf16[272,128]{1,0:T(8,128)(2,1)S(1)}, bf16[272,128]{1,0:T(8,128)(2,1)S(1)}, u32[]{:S(2)}, u32[]{:S(2)}) collective-permute-start(bf16[272,128]{1,0:T(8,128)(2,1)S(1)} %shard_map.203), channel_id=1, source_target_pairs={{0,3},{1,7},{2,11},{3,15},{4,0},{5,4},{6,8},{7,12},{8,1},{9,5},{10... | collective-permute-start | bytes 208904 | tf_op jit(solution)/shard_map/ppermute | solution.py:657
  10.3 11.2 %collective-permute-start.2 = (bf16[272,128]{1,0:T(8,128)(2,1)S(1)}, bf16[272,128]{1,0:T(8,128)(2,1)S(1)}, u32[]{:S(2)}, u32[]{:S(2)}) collective-permute-start(bf16[272,128]{1,0:T(8,128)(2,1)S(1)} %shard_map.203), channel_id=1, source_target_pairs={{0,2},{1,6},{2,10},{3,14},{4,3},{5,7},{6,11},{7,15},{8,0},{9,4},{1... | collective-permute-start | bytes 208904 | tf_op jit(solution)/shard_map/ppermute | solution.py:657
  12.9 8.6 %collective-permute-start.1 = (bf16[272,128]{1,0:T(8,128)(2,1)S(1)}, bf16[272,128]{1,0:T(8,128)(2,1)S(1)}, u32[]{:S(2)}, u32[]{:S(2)}) collective-permute-start(bf16[272,128]{1,0:T(8,128)(2,1)S(1)} %shard_map.203), channel_id=1, source_target_pairs={{0,1},{1,5},{2,9},{3,13},{4,2},{5,6},{6,10},{7,14},{8,3},{9,7},{10... | collective-permute-start | bytes 208904 | tf_op jit(solution)/shard_map/ppermute | solution.py:657
  13.6 7.9 %collective-permute-start = (bf16[272,128]{1,0:T(8,128)(2,1)S(1)}, bf16[272,128]{1,0:T(8,128)(2,1)S(1)}, u32[]{:S(2)}, u32[]{:S(2)}) collective-permute-start(bf16[272,128]{1,0:T(8,128)(2,1)S(1)} %shard_map.203), channel_id=1, source_target_pairs={{0,0},{1,4},{2,8},{3,12},{4,1},{5,5},{6,9},{7,13},{8,2},{9,6},{10,... | collective-permute-start | bytes 208904 | tf_op jit(solution)/shard_map/ppermute | solution.py:657
  23.4 5.6 %collective-permute-start.6 = (bf16[16,2048]{1,0:T(8,128)(2,1)S(1)}, bf16[16,2048]{1,0:T(8,128)(2,1)S(1)}, u32[]{:S(2)}, u32[]{:S(2)}) collective-permute-start(bf16[16,2048]{1,0:T(8,128)(2,1)S(1)} %shard_map.204.refs_0_), channel_id=1, source_target_pairs={{0,12},{4,0},{8,4},{12,8},{1,13},{5,1},{9,5},{13,9},{2,14},{6,2},{... | collective-permute-start | bytes 196616 | tf_op jit(solution)/shard_map/ppermute | solution.py:21
  27.1 7.1 %collective-permute-start.5 = (bf16[16,2048]{1,0:T(8,128)(2,1)S(1)}, bf16[16,2048]{1,0:T(8,128)(2,1)S(1)}, u32[]{:S(2)}, u32[]{:S(2)}) collective-permute-start(bf16[16,2048]{1,0:T(8,128)(2,1)S(1)} %shard_map.204.refs_0_), channel_id=1, source_target_pairs={{0,8},{4,12},{8,0},{12,4},{1,9},{5,13},{9,1},{13,5},{2,10},{6,14},... | collective-permute-start | bytes 196616 | tf_op jit(solution)/shard_map/ppermute | solution.py:21
  27.1 7.1 %collective-permute-start.4 = (bf16[16,2048]{1,0:T(8,128)(2,1)S(1)}, bf16[16,2048]{1,0:T(8,128)(2,1)S(1)}, u32[]{:S(2)}, u32[]{:S(2)}) collective-permute-start(bf16[16,2048]{1,0:T(8,128)(2,1)S(1)} %shard_map.204.refs_0_), channel_id=1, source_target_pairs={{0,4},{4,8},{8,12},{12,0},{1,5},{5,9},{9,13},{13,1},{2,6},{6,10},{... | collective-permute-start | bytes 196616 | tf_op jit(solution)/shard_map/ppermute | solution.py:21
  48.5 5.5 %collective-permute-start.7 = (bf16[16,2176]{1,0:T(8,128)(2,1)S(1)}, bf16[16,2176]{1,0:T(8,128)(2,1)S(1)}, u32[]{:S(2)}, u32[]{:S(2)}) collective-permute-start(bf16[16,2176]{1,0:T(8,128)(2,1)S(1)} %shard_map.207), channel_id=1, source_target_pairs={{0,1},{1,2},{2,3},{3,0},{4,5},{5,6},{6,7},{7,4},{8,9},{9,10},{10,1... | collective-permute-start | bytes 208904 | tf_op jit(solution)/shard_map/ppermute | solution.py:21
  50.1 4.8 %collective-permute-start.8 = (bf16[16,2176]{1,0:T(8,128)(2,1)S(1)}, bf16[16,2176]{1,0:T(8,128)(2,1)S(1)}, u32[]{:S(2)}, u32[]{:S(2)}) collective-permute-start(bf16[16,2176]{1,0:T(8,128)(2,1)S(1)} %shard_map.208), channel_id=1, source_target_pairs={{0,2},{1,3},{2,0},{3,1},{4,6},{5,7},{6,4},{7,5},{8,10},{9,11},{10,... | collective-permute-start | bytes 208904 | tf_op jit(solution)/shard_map/ppermute | solution.py:21
  51.4 3.5 %collective-permute-start.9 = (bf16[16,2176]{1,0:T(8,128)(2,1)S(1)}, bf16[16,2176]{1,0:T(8,128)(2,1)S(1)}, u32[]{:S(2)}, u32[]{:S(2)}) collective-permute-start(bf16[16,2176]{1,0:T(8,128)(2,1)S(1)} %shard_map.209), channel_id=1, source_target_pairs={{0,3},{1,0},{2,1},{3,2},{4,7},{5,4},{6,5},{7,6},{8,11},{9,8},{10,9... | collective-permute-start | bytes 208904 | tf_op jit(solution)/shard_map/ppermute | solution.py:21
  55.4 3.8 %collective-permute-start.12 = (f32[16,544]{1,0:T(8,128)S(1)}, f32[16,544]{1,0:T(8,128)S(1)}, u32[]{:S(2)}, u32[]{:S(2)}) collective-permute-start(f32[16,544]{1,0:T(8,128)S(1)} %get-tuple-element.13), channel_id=1, source_target_pairs={{0,3},{1,0},{2,1},{3,2},{4,7},{5,4},{6,5},{7,6},{8,11},{9,8},{10,9... | collective-permute-start | bytes 104456 | tf_op jit(solution)/shard_map/ppermute | solution.py:21
  57.3 3.4 %collective-permute-start.11 = (f32[16,544]{1,0:T(8,128)S(1)}, f32[16,544]{1,0:T(8,128)S(1)}, u32[]{:S(2)}, u32[]{:S(2)}) collective-permute-start(f32[16,544]{1,0:T(8,128)S(1)} %get-tuple-element.13), channel_id=1, source_target_pairs={{0,1},{1,2},{2,3},{3,0},{4,5},{5,6},{6,7},{7,4},{8,9},{9,10},{10,1... | collective-permute-start | bytes 104456 | tf_op jit(solution)/shard_map/ppermute | solution.py:21
  57.3 4.3 %collective-permute-start.10 = (f32[16,544]{1,0:T(8,128)S(1)}, f32[16,544]{1,0:T(8,128)S(1)}, u32[]{:S(2)}, u32[]{:S(2)}) collective-permute-start(f32[16,544]{1,0:T(8,128)S(1)} %get-tuple-element.13), channel_id=1, source_target_pairs={{0,2},{1,3},{2,0},{3,1},{4,6},{5,7},{6,4},{7,5},{8,10},{9,11},{10,... | collective-permute-start | bytes 104456 | tf_op jit(solution)/shard_map/ppermute | solution.py:21
  61.6 4.1 %collective-permute-start.15 = (f32[16,544]{1,0:T(8,128)S(1)}, f32[16,544]{1,0:T(8,128)S(1)}, u32[]{:S(2)}, u32[]{:S(2)}) collective-permute-start(f32[16,544]{1,0:T(8,128)S(1)} %add_add_fusion.1), channel_id=1, source_target_pairs={{0,12},{4,0},{8,4},{12,8},{1,13},{5,1},{9,5},{13,9},{2,14},{6,2},{... | collective-permute-start | bytes 104456 | tf_op jit(solution)/shard_map/ppermute | solution.py:21
  63.1 5.8 %collective-permute-start.14 = (f32[16,544]{1,0:T(8,128)S(1)}, f32[16,544]{1,0:T(8,128)S(1)}, u32[]{:S(2)}, u32[]{:S(2)}) collective-permute-start(f32[16,544]{1,0:T(8,128)S(1)} %add_add_fusion.1), channel_id=1, source_target_pairs={{0,4},{4,8},{8,12},{12,0},{1,5},{5,9},{9,13},{13,1},{2,6},{6,10},{... | collective-permute-start | bytes 104456 | tf_op jit(solution)/shard_map/ppermute | solution.py:21
  63.7 5.8 %collective-permute-start.13 = (f32[16,544]{1,0:T(8,128)S(1)}, f32[16,544]{1,0:T(8,128)S(1)}, u32[]{:S(2)}, u32[]{:S(2)}) collective-permute-start(f32[16,544]{1,0:T(8,128)S(1)} %add_add_fusion.1), channel_id=1, source_target_pairs={{0,8},{4,12},{8,0},{12,4},{1,9},{5,13},{9,1},{13,5},{2,10},{6,14},... | collective-permute-start | bytes 104456 | tf_op jit(solution)/shard_map/ppermute | solution.py:21
  71.0 1.6 %collective-permute-start.18 = (bf16[16,1024]{1,0:T(8,128)(2,1)S(1)}, bf16[16,1024]{1,0:T(8,128)(2,1)S(1)}, u32[]{:S(2)}, u32[]{:S(2)}) collective-permute-start(bf16[16,1024]{1,0:T(8,128)(2,1)S(1)} %get-tuple-element.16.refs_0_), channel_id=1, source_target_pairs={{0,3},{1,0},{2,1},{3,2},{4,7},{5,4},{6,5},{7,6},{8,11},{9,8},{10,9... | collective-permute-start | bytes 98312 | tf_op jit(solution)/shard_map/ppermute | solution.py:21
  71.0 4.2 %collective-permute-start.17 = (bf16[16,1024]{1,0:T(8,128)(2,1)S(1)}, bf16[16,1024]{1,0:T(8,128)(2,1)S(1)}, u32[]{:S(2)}, u32[]{:S(2)}) collective-permute-start(bf16[16,1024]{1,0:T(8,128)(2,1)S(1)} %get-tuple-element.16.refs_0_), channel_id=1, source_target_pairs={{0,2},{1,3},{2,0},{3,1},{4,6},{5,7},{6,4},{7,5},{8,10},{9,11},{10,... | collective-permute-start | bytes 98312 | tf_op jit(solution)/shard_map/ppermute | solution.py:21
  71.7 3.6 %collective-permute-start.16 = (bf16[16,1024]{1,0:T(8,128)(2,1)S(1)}, bf16[16,1024]{1,0:T(8,128)(2,1)S(1)}, u32[]{:S(2)}, u32[]{:S(2)}) collective-permute-start(bf16[16,1024]{1,0:T(8,128)(2,1)S(1)} %get-tuple-element.16.refs_0_), channel_id=1, source_target_pairs={{0,1},{1,2},{2,3},{3,0},{4,5},{5,6},{6,7},{7,4},{8,9},{9,10},{10,1... | collective-permute-start | bytes 98312 | tf_op jit(solution)/shard_map/ppermute | solution.py:21
  77.0 4.3 %collective-permute-start.21 = (bf16[16,2048]{1,0:T(8,128)(2,1)S(1)}, bf16[16,2048]{1,0:T(8,128)(2,1)S(1)}, u32[]{:S(2)}, u32[]{:S(2)}) collective-permute-start(bf16[16,2048]{1,0:T(8,128)(2,1)S(1)} %shard_map.213.refs_0_), channel_id=1, source_target_pairs={{0,12},{4,0},{8,4},{12,8},{1,13},{5,1},{9,5},{13,9},{2,14},{6,2},{... | collective-permute-start | bytes 196616 | tf_op jit(solution)/shard_map/ppermute | solution.py:21
  79.3 5.3 %collective-permute-start.20 = (bf16[16,2048]{1,0:T(8,128)(2,1)S(1)}, bf16[16,2048]{1,0:T(8,128)(2,1)S(1)}, u32[]{:S(2)}, u32[]{:S(2)}) collective-permute-start(bf16[16,2048]{1,0:T(8,128)(2,1)S(1)} %shard_map.213.refs_0_), channel_id=1, source_target_pairs={{0,8},{4,12},{8,0},{12,4},{1,9},{5,13},{9,1},{13,5},{2,10},{6,14},... | collective-permute-start | bytes 196616 | tf_op jit(solution)/shard_map/ppermute | solution.py:21
  79.3 6.1 %collective-permute-start.19 = (bf16[16,2048]{1,0:T(8,128)(2,1)S(1)}, bf16[16,2048]{1,0:T(8,128)(2,1)S(1)}, u32[]{:S(2)}, u32[]{:S(2)}) collective-permute-start(bf16[16,2048]{1,0:T(8,128)(2,1)S(1)} %shard_map.213.refs_0_), channel_id=1, source_target_pairs={{0,4},{4,8},{8,12},{12,0},{1,5},{5,9},{9,13},{13,1},{2,6},{6,10},{... | collective-permute-start | bytes 196616 | tf_op jit(solution)/shard_map/ppermute | solution.py:21
  (20 other events, 197.2 us)

commit v3 on v2

--- a/solution.py
+++ b/solution.py
@@ -13,6 +13,9 @@
 DIRECT = 8
 LANES = 128
 MIB = 1024 * 1024
+PIECES = 8
+ATT_LIMIT = 8
+LOAD_LIMIT = 2
 FLOPS_AHEAD = 20_000_000_000
 
 
@@ -25,6 +28,16 @@
     if len(terms) == 1:
         return terms[0]
     return paired_sum(terms[::2]) + paired_sum(terms[1::2])
+
+
+def crossed(value, axes, flip):
+    return lax.ppermute(value, axes, [(i, i ^ flip) for i in range(lax.axis_size(axes))])
+
+
+def crossed_all(value, axes):
+    count = lax.axis_size(axes)
+    far_first = {flip: crossed(value, axes, flip) for flip in range(count - 1, 0, -1)}
+    return [value] + [far_first[flip] for flip in range(1, count)]
 
 
 def everyone(value, axes):
@@ -59,7 +72,40 @@
     return [pl.BlockSpec(memory_space=pltpu.VMEM)] * count
 
 
-def attention(query, key_new, value_new, kv_cache, kv_scale, context_len):
+def pieces_of(source, target, ready):
+    rows = target.shape[0] // PIECES
+    return [
+        pltpu.make_async_copy(
+            source.at[k * rows : (k + 1) * rows], target.at[k * rows : (k + 1) * rows], ready.at[k]
+        )
+        for k in range(PIECES)
+    ]
+
+
+def bring(weight, part, after):
+    shape = weight.shape if part is None else weight.shape[1:]
+
+    def kernel(weight_ref, after_ref, out_ref, ready):
+        copies = pieces_of(weight_ref if part is None else weight_ref.at[part], out_ref, ready)
+        for copy in copies:
+            copy.start()
+        for copy in copies:
+            copy.wait()
+
+    return pl.pallas_call(
+        kernel,
+        out_shape=pltpu.VMEM(shape, weight.dtype),
+        in_specs=[pl.BlockSpec(memory_space=pl.ANY)] * 2,
+        out_specs=whole(1)[0],
+        scratch_shapes=[pltpu.SemaphoreType.DMA((PIECES,))],
+        compiler_params=pltpu.CompilerParams(vmem_limit_bytes=LOAD_LIMIT * MIB),
+        cost_estimate=pl.CostEstimate(
+            flops=0, bytes_accessed=2 * math.prod(shape) * weight.dtype.itemsize, transcendentals=0
+        ),
+    )(pltpu.with_memory_space_constraint(weight, pltpu.HBM), after)
+
+
+def attention(query, key_new, value_new, kv_cache, kv_scale, context_len, weight):
     requests, steps, heads, dim = query.shape
     kv_heads = key_new.shape[2]
     group = heads // kv_heads
@@ -71,7 +117,21 @@
     total_rows = requests * lines
     news = steps * kv_heads
 
-    def kernel(length_ref, scale_ref, query_ref, cache_ref, key_ref, value_ref, out_ref):
+    def kernel(*refs):
+        sources, weight_source, out_ref, weight_ref = refs[:6], refs[6], refs[7], refs[8]
+        held, ready, weight_ready = refs[9:15], refs[15], refs[16]
+        length_ref, scale_ref, query_ref, key_ref, value_ref, cache_ref = held
+        copies = [
+            pltpu.make_async_copy(sources[k], held[k], ready.at[k]) for k in range(5)
+        ] + [
+            pltpu.make_async_copy(sources[5].at[:, k], cache_ref.at[:, k], ready.at[5 + k])
+            for k in range(requests)
+        ]
+        for copy in copies:
+            copy.start()
+        weight_copies = pieces_of(weight_source, weight_ref, weight_ready)
+        for copy in weight_copies:
+            copy.start()
         shard = lax.axis_index("seq")
         row = lax.broadcasted_iota(jnp.int32, (lines, width), 0)
         column = lax.broadcasted_iota(jnp.int32, (lines, width), 1)
@@ -89,16 +149,21 @@
         def spread(which, request):
             pieces = []
             for block in range(blocks):
-                piece = jnp.full((1, kv_heads * BLOCK), scale_ref[which, request, 0, block])
-                for head in range(1, kv_heads):
-                    piece = jnp.where(parity == head, scale_ref[which, request, head, block], piece)
+                piece = jnp.zeros((1, kv_heads * BLOCK), jnp.float32)
+                for head in range(kv_heads):
+                    piece = jnp.where(
+                        parity == head, scale_ref[which, head, block : block + 1, request : request + 1], piece
+                    )
                 pieces.append(piece)
             return jnp.concatenate(pieces, axis=1)
 
         tops, totals = [], []
+        for copy in copies[:5]:
+            copy.wait()
         for request in range(requests):
             asked = query_ref[request]
-            live = same & (place < length_ref[request])
+            live = same & (place < length_ref[:, request : request + 1])
+            copies[5 + request].wait()
             scores = lax.dot_general(
                 asked, cache_ref[0, request], (((1,), (1,)), ((), ())), preferred_element_type=jnp.float32
             )
@@ -142,29 +207,37 @@
         out_ref[total_rows:, :] = jnp.concatenate(
             [turned[:, k * LANES : (k + 1) * LANES] for k in range(total_rows // LANES)], axis=0
         ).astype(jnp.bfloat16)
-
+        for copy in weight_copies:
+            copy.wait()
+
+    given_all = (
+        context_len.reshape(1, requests),
+        kv_scale.transpose(0, 2, 3, 1),
+        query.reshape(requests, lines, dim),
+        key_new.reshape(requests, news, dim),
+        value_new.reshape(requests, news, dim),
+        kv_cache.reshape(2, requests, width, dim),
+    )
     return pl.pallas_call(
         kernel,
-        out_shape=jax.ShapeDtypeStruct((total_rows + total_rows // 16, dim), jnp.bfloat16),
-        in_specs=[pl.BlockSpec(memory_space=pltpu.SMEM)] * 2 + whole(4),
-        out_specs=whole(1)[0],
-        compiler_params=pltpu.CompilerParams(vmem_limit_bytes=6 * 1024 * 1024),
-        cost_estimate=pl.CostEstimate(flops=FLOPS_AHEAD, bytes_accessed=0, transcendentals=0),
-    )(
-        context_len,
-        kv_scale,
-        query.reshape(requests, lines, dim),
-        kv_cache.reshape(2, requests, width, dim),
-        key_new.reshape(requests, news, dim),
-        value_new.reshape(requests, news, dim),
-    )
+        out_shape=(
+            jax.ShapeDtypeStruct((total_rows + total_rows // 16, dim), jnp.bfloat16),
+            pltpu.VMEM(weight.shape, weight.dtype),
+        ),
+        in_specs=[pl.BlockSpec(memory_space=pl.ANY)] * 7,
+        out_specs=tuple(whole(2)),
+        scratch_shapes=[pltpu.VMEM(given.shape, given.dtype) for given in given_all]
+        + [pltpu.SemaphoreType.DMA((5 + requests,)), pltpu.SemaphoreType.DMA((PIECES,))],
+        compiler_params=pltpu.CompilerParams(vmem_limit_bytes=ATT_LIMIT * MIB),
+        cost_estimate=cost(1_000_000_000),
+    )(*[pltpu.with_memory_space_constraint(given, pltpu.HBM) for given in given_all + (weight,)])
 
 
 def cost(flops):
     return pl.CostEstimate(flops=flops, bytes_accessed=0, transcendentals=0)
 
 
-def merge_project(parts, weight, rows, heads, dim):
+def merge_project(parts, weight, rows, heads, dim, brought):
     lines = rows * heads
     count = len(parts)
     depth, width = weight.shape
@@ -200,32 +273,39 @@
     return pl.pallas_call(
         kernel,
         out_shape=jax.ShapeDtypeStruct((rows, width), jnp.bfloat16),
-        in_specs=whole(count + 1),
+        in_specs=whole(count + 1) + [pl.BlockSpec(memory_space=pl.ANY)],
         out_specs=whole(1)[0],
         scratch_shapes=[pltpu.VMEM((lines, dim), jnp.float32), pltpu.VMEM((rows, heads * dim), jnp.bfloat16)],
         compiler_params=pltpu.CompilerParams(vmem_limit_bytes=4 * MIB),
         cost_estimate=cost(FLOPS_AHEAD),
-    )(*parts, weight)
+    )(*parts, weight, brought)
+
+
+def in_three(left):
+    rows = left.shape[0]
+    lane = lax.broadcasted_iota(jnp.int32, (rows, LANES), 1)
+    table = jnp.zeros((rows, LANES), jnp.float32)
+    for k in range(3):
+        piece = left.astype(jnp.bfloat16).astype(jnp.float32)
+        table = jnp.where(lane == k, piece, table)
+        left = left - piece
+    return table.astype(jnp.bfloat16)
 
 
 def add_residual(hidden, parts, gain):
-    rows, width = hidden.shape
+    requests, steps, width = hidden.shape
+    rows = requests * steps
 
     def kernel(hidden_ref, gain_ref, *refs):
         part_refs, (residual_ref, gained_ref, stats_ref) = refs[:-3], refs[-3:]
-        residual = hidden_ref[...].astype(jnp.float32) + paired_sum(
+        wide = [hidden_ref[request].astype(jnp.float32) for request in range(requests)]
+        by_step = jnp.concatenate([part[step : step + 1] for step in range(steps) for part in wide], axis=0)
+        residual = by_step + paired_sum(
             [ref[...].astype(jnp.float32) for ref in part_refs]
         )
         residual_ref[...] = residual
         gained_ref[...] = (residual * gain_ref[...]).astype(jnp.bfloat16)
-        left = jnp.sum(residual * residual, axis=1, keepdims=True)
-        lane = lax.broadcasted_iota(jnp.int32, (rows, LANES), 1)
-        table = jnp.zeros((rows, LANES), jnp.float32)
-        for k in range(3):
-            piece = left.astype(jnp.bfloat16).astype(jnp.float32)
-            table = jnp.where(lane == k, piece, table)
-            left = left - piece
-        stats_ref[...] = table.astype(jnp.bfloat16)
+        stats_ref[...] = in_three(jnp.sum(residual * residual, axis=1, keepdims=True))
 
     return pl.pallas_call(
         kernel,
@@ -245,49 +325,56 @@
     return lax.axis_index("head") * lax.axis_size("sub") + lax.axis_index("sub")
 
 
-def project_block(gained, weight, stats, own_width, hop):
+def project_block(gained, weights, stats, own_width, flip, arrived=None):
     rows, depth = gained.shape
-    count = lax.axis_size(HS)
     width = 2 * own_width
     tile = tile_of(own_width, 512)
-    kind = jnp.bfloat16 if hop else jnp.float32
-
-    def kernel(gained_ref, weight_ref, stats_ref, out_ref):
-        base = ((hs_position() + hop) % count) * own_width
+    kind = jnp.bfloat16 if flip else jnp.float32
+    extra = () if arrived is None else (arrived,)
+
+    def kernel(gained_ref, stats_ref, *refs):
+        weight_refs, refs, out_ref = refs[:2], refs[2:], refs[-1]
+        base = (hs_position() ^ flip) * own_width
         for part in range(2):
             for start in range(0, own_width, tile):
                 columns = pl.ds(pl.multiple_of(base + start, tile), tile)
-                out_ref[:, part * own_width + start : part * own_width + start + tile] = jnp.dot(
-                    gained_ref[...], weight_ref[part, :, columns], preferred_element_type=jnp.float32
-                ).astype(kind)
-        if hop:
+                place = slice(part * own_width + start, part * own_width + start + tile)
+                block = jnp.dot(
+                    gained_ref[...], weight_refs[part][:, columns], preferred_element_type=jnp.float32
+                )
+                if extra:
+                    block = block + refs[0][:, place].astype(jnp.float32)
+                out_ref[:, place] = block.astype(kind)
+        if flip and extra:
+            both = stats_ref[...].astype(jnp.float32) + refs[0][:, width:].astype(jnp.float32)
+            out_ref[:, width:] = in_three(jnp.sum(both, axis=1, keepdims=True))
+        elif flip:
             out_ref[:, width:] = stats_ref[...]
 
     return pl.pallas_call(
         kernel,
-        out_shape=jax.ShapeDtypeStruct((rows, width + (LANES if hop else 0)), kind),
-        in_specs=whole(3),
+        out_shape=jax.ShapeDtypeStruct((rows, width + (LANES if flip else 0)), kind),
+        in_specs=whole(4 + len(extra)),
         out_specs=whole(1)[0],
         compiler_params=pltpu.CompilerParams(vmem_limit_bytes=4 * MIB),
         cost_estimate=cost(2 * rows * depth * width),
-    )(gained, weight, stats)
-
-
-def convolve(own, received, stats, state, taps, bias, weight, features):
+    )(gained, stats, *weights, *extra)
+
+
+def convolve(own, received, squares, state, taps, bias, weight, features):
     rows, width = own.shape
     own_width = width // 2
     requests = state.shape[1]
     taps_count = taps.shape[0]
     mixed_width = weight.shape[0]
-    count = len(received)
-
-    def kernel(own_ref, stats_ref, state_ref, taps_ref, bias_ref, weight_ref, *refs):
-        received_refs, (conv_ref, gate_ref, mixing_ref) = refs[:count], refs[count:]
-        pieces = stats_ref[...].astype(jnp.float32)
-        channels = own_ref[...]
-        for ref in received_refs:
-            channels = channels + ref[:, :width].astype(jnp.float32)
-            pieces = pieces + ref[:, width:].astype(jnp.float32)
+    count = len(squares)
+
+    def kernel(own_ref, received_ref, state_ref, taps_ref, bias_ref, weight_ref, *refs):
+        squares_refs, (conv_ref, gate_ref, mixing_ref) = refs[:count], refs[count:]
+        pieces = received_ref[:, width:].astype(jnp.float32)
+        for ref in squares_refs:
+            pieces = pieces + ref[:, ref.shape[1] - LANES :].astype(jnp.float32)
+        channels = own_ref[...] + received_ref[:, :width].astype(jnp.float32)
         squares = jnp.sum(pieces, axis=1, keepdims=True)
         channels = (channels * lax.rsqrt(squares / features + EPS)).astype(jnp.bfloat16)
         gate_ref[...] = channels[:, own_width:]
@@ -318,15 +405,15 @@
         out_specs=tuple(whole(3)),
         compiler_params=pltpu.CompilerParams(vmem_limit_bytes=8 * MIB),
         cost_estimate=cost(FLOPS_AHEAD),
-    )(own, stats, state, taps, bias, weight, *received)
-
-
-def scan_states(mixing, conv, gate, dt_weight, dt_bias, decay, skip, state):
+    )(own, received, state, taps, bias, weight, *squares)
+
+
+def scan_states(mixing, conv, gate, dt_weight, dt_bias, decay, skip, state, brought):
     rows, own_width = conv.shape
     requests, state_width = state.shape[:2]
     low_width = dt_weight.shape[0]
 
-    def kernel(mixing_ref, conv_ref, gate_ref, dt_ref, bias_ref, decay_ref, skip_ref, state_ref, *refs):
+    def kernel(mixing_ref, conv_ref, gate_ref, dt_ref, bias_ref, decay_ref, skip_ref, state_ref, brought_ref, *refs):
         gated_ref, next_ref, out = refs
         low = mixing_ref[:, :low_width]
         low_rank = (low * lax.rsqrt(jnp.mean(low * low, axis=1, keepdims=True) + EPS)).astype(jnp.bfloat16)
@@ -365,28 +452,27 @@
             jax.ShapeDtypeStruct((rows, own_width), jnp.bfloat16),
             jax.ShapeDtypeStruct(state.shape, jnp.float32),
         ),
-        in_specs=whole(8),
+        in_specs=whole(8) + [pl.BlockSpec(memory_space=pl.ANY)],
         out_specs=tuple(whole(2)),
         scratch_shapes=[pltpu.VMEM((rows, own_width), jnp.float32)],
         compiler_params=pltpu.CompilerParams(vmem_limit_bytes=8 * MIB),
         cost_estimate=cost(FLOPS_AHEAD // 4),
-    )(mixing, conv, gate, dt_weight, dt_bias, decay, skip, state)
-
-
-def project_out(blocks, hops, weight, before):
+    )(mixing, conv, gate, dt_weight, dt_bias, decay, skip, state, brought)
+
+
+def project_out(blocks, flips, weight, before):
     rows, own_width = blocks[0].shape
-    count = lax.axis_size(HS)
     width = weight.shape[1]
     tile = tile_of(width, 512)
     kind = jnp.float32 if before is None else jnp.bfloat16
 
     def kernel(*refs):
-        block_refs, weight_ref, out_ref = refs[: len(hops)], refs[len(hops)], refs[-1]
+        block_refs, weight_ref, out_ref = refs[: len(flips)], refs[len(flips)], refs[-1]
         for start in range(0, width, tile):
             columns = slice(start, start + tile)
             terms = []
-            for ref, hop in zip(block_refs, hops):
-                base = pl.multiple_of(((hs_position() + count - hop) % count) * own_width, own_width)
+            for ref, flip in zip(block_refs, flips):
+                base = pl.multiple_of((hs_position() ^ flip) * own_width, own_width)
                 terms.append(
                     jnp.dot(
                         ref[...], weight_ref[pl.ds(base, own_width), columns], preferred_element_type=jnp.float32
@@ -396,7 +482,7 @@
             for term in terms[1:]:
                 total = total + term
             if before is not None:
-                total = total + refs[len(hops) + 1][:, columns]
+                total = total + refs[len(flips) + 1][:, columns]
             out_ref[:, columns] = total.astype(kind)
 
     extra = () if before is None else (before,)
@@ -406,7 +492,7 @@
         in_specs=whole(len(blocks) + 1 + len(extra)),
         out_specs=whole(1)[0],
         compiler_params=pltpu.CompilerParams(vmem_limit_bytes=4 * MIB),
-        cost_estimate=cost(2 * rows * own_width * width * len(hops)),
+        cost_estimate=cost(2 * rows * own_width * width * len(flips)),
     )(*blocks, weight, *extra)
 
 
@@ -623,8 +709,9 @@
     heads, dim = query.shape[2:]
     own_width = conv_weight.shape[0]
     if (
-        seq_count != hs_count
-        or seq_count > DIRECT
+        lax.axis_size("head") != 2
+        or lax.axis_size("sub") != 2
+        or seq_count != hs_count
         or own_width % LANES
         or dim != LANES
         or (rows * heads) % LANES
@@ -652,39 +739,59 @@
             ssm_state,
             mamba_out_weight,
         )
-    part = attention(query, key_new, value_new, kv_cache, kv_scale, context_len)
+    part, out_rows = attention(
+        query, key_new, value_new, kv_cache, kv_scale, context_len, attn_out_weight
+    )
+    first_in = bring(in_weight, 0, part)
+    place = range(hs_count)
     parts = [
         lax.ppermute(
             part,
             ("seq",) + HS,
             [
-                (s * hs_count + j, j * hs_count + (s + hop) % hs_count)
+                (s * hs_count + j, j * hs_count + ((s // 2 + turn) % 2) * 2 + s % 2)
                 for s in range(seq_count)
-                for j in range(hs_count)
+                for j in place
             ],
         )
-        for hop in range(hs_count)
+        for turn in range(2)
     ]
-    partial = merge_project(parts, attn_out_weight, rows, heads, dim)
-    step_hidden = hidden.transpose(1, 0, 2).reshape(rows, -1)
-    features = step_hidden.shape[1] * hs_count
-    residual, gained, stats = add_residual(step_hidden, everyone(partial, "seq"), norm_gain)
-    received = []
-    for hop in range(1, hs_count):
-        block = project_block(gained, in_weight, stats, own_width, hop)
-        received.append(shifted(block, HS, hop))
-    own = project_block(gained, in_weight, stats, own_width, 0)
+    parts, first_in = lax.optimization_barrier((parts, first_in))
+    parts = parts + [crossed(arrived, "sub", 1) for arrived in parts]
+    partial = merge_project(parts, out_rows, rows, heads, dim, first_in)
+    second_in = bring(in_weight, 1, partial)
+    residual, gained, stats = add_residual(hidden, crossed_all(partial, "seq"), norm_gain)
+    features = residual.shape[1] * hs_count
+    give = lambda flip, arrived=None: project_block(gained, (first_in, second_in), stats, own_width, flip, arrived)
+    for_far = crossed(give(3), "sub", 1)
+    for_near = crossed(give(1), "sub", 1)
+    received = crossed(give(2, for_far), "head", 1)
+    own = give(0, for_near)
     conv, gate, mixing = convolve(
         own,
         received,
-        stats,
+        [stats, for_far],
         conv_state.transpose(1, 0, 2),
         conv_weight.T,
         conv_bias.reshape(1, -1),
         xproj_weight.T,
         features,
     )
-    mixing = sum_over(sum_over(mixing, HS), "seq")
+    mixing = mixing + crossed(mixing, "sub", 1)
+    mamba_rows = bring(mamba_out_weight, None, mixing)
+    base = lambda s, x, c: s * hs_count + x * 2 + c
+    arrived = [
+        lax.ppermute(
+            mixing,
+            ("seq",) + HS,
+            [(base(s, x, 1), base(s ^ flip, x ^ 1, 1)) for s in range(seq_count) for x in range(2)]
+            + [(base(s, x, 0), base(s ^ flip, x, 0)) for s in range(seq_count) for x in range(2) if flip],
+        )
+        for flip in range(seq_count - 1, -1, -1)
+    ]
+    arrived, mamba_rows = lax.optimization_barrier((arrived, mamba_rows))
+    line = jnp.where(lax.axis_index("sub") == 0, mixing, 0.0) + paired_sum(arrived)
+    mixing = line + crossed(line, "sub", 1)
     gated, state = scan_states(
         mixing,
         conv,
@@ -694,12 +801,12 @@
         decay_rate.T,
         skip_gain.reshape(1, -1),
         ssm_state.transpose(0, 2, 1),
-    )
-    hops = range(1, hs_count)
-    blocks = [shifted(gated, HS, hop) for hop in hops]
-    first = project_out([gated], [0], mamba_out_weight, None)
-    partial = project_out(blocks, hops, mamba_out_weight, first)
-    final = finish(residual, everyone(partial, "seq"), requests)
+        mamba_rows,
+    )
+    blocks = crossed_all(gated, HS)
+    first = project_out(blocks[:1], [0], mamba_rows, None)
+    partial = project_out(blocks[1:], list(place)[1:], mamba_rows, first)
+    final = finish(residual, crossed_all(partial, "seq"), requests)
     return final, state.transpose(0, 2, 1)
 
 

time: 86.5 us -> 76 us (0.88)
  Pallas kernels: 14.2 us -> 34.4 us
  waiting for transfers between devices: 29.6 us -> 13 us
  local copies, waits for them, and re-layouts: 15.6 us -> 0.06 us
  starting transfers between devices: 25.8 us -> 27.5 us
    pallas_call x1 -> x4, Pallas kernels: 2.35 us -> 22.4 us  [the longest x3 17.9 us: bring(): pl.pallas_call(kernel, out_shape=pltpu.VMEM(shape, weight.dtype), in_spec...]
    ppermute x22, waiting for transfers between devices: 29.6 us -> 13 us  [the longest x16 12.2 us: crossed(): lax.ppermute(value, axes, [(i, i ^ flip) for i in range(lax.axis_size(axe...]
    unnamed x45 -> x22, local copies, waits for them, and re-layouts: 15.6 us -> 0.06 us
    ppermute x22, starting transfers between devices: 25.8 us -> 27.5 us  [the longest x16 14.8 us: crossed(): lax.ppermute(value, axes, [(i, i ^ flip) for i in range(lax.axis_size(axe...]
  transfers between devices with their start and end apart: 22 -> 22, of which waited for: 14 -> 10; matrix products, arithmetic and copies ran while one was open for 0% -> 0% of each run, Pallas kernels for 2% -> 29%
where the time goes in v3:
time: 76 us; the launch traced here: 75.9 us
  Pallas kernels  34.4 us (45%)
  starting transfers between devices  27.5 us (36%)
  waiting for transfers between devices  13 us (17%)
  between operations  0.9 us (1%)
    pallas_call x3, Pallas kernels, bring(): pl.pallas_call(kernel, out_shape=pltpu.VMEM(shape, weight.dtype), in_spec...  17.9 us
    ppermute x16, starting transfers between devices, crossed(): lax.ppermute(value, axes, [(i, i ^ flip) for i in range(lax.axis_size(axe...  14.8 us
    ppermute x16, waiting for transfers between devices, crossed(): lax.ppermute(value, axes, [(i, i ^ flip) for i in range(lax.axis_size(axe...  12.2 us
    ppermute x2, starting transfers between devices, local(): lax.ppermute(part, ('seq',) + HS, [(s * hs_count + j, j * hs_count + (s /...  7.46 us
    ppermute x4, starting transfers between devices, local(): lax.ppermute(mixing, ('seq',) + HS, [(base(s, x, 1), base(s ^ flip, x ^ 1...  5.22 us
    pallas_call x4, Pallas kernels, project_block(): pl.pallas_call(kernel, out_shape=jax.ShapeDtypeStruct((rows, width + (LAN...  4.79 us
    pallas_call x1, Pallas kernels, attention(): pl.pallas_call(kernel, out_shape=(jax.ShapeDtypeStruct((total_rows + tota...  4.54 us
    pallas_call x2, Pallas kernels, project_out(): pl.pallas_call(kernel, out_shape=jax.ShapeDtypeStruct((rows, width), kind...  2.38 us
  transfers between devices with their start and end apart: 22, of which 10 were waited for; matrix products, arithmetic and copies ran while one was open for 0% of the time, Pallas kernels for 29%

profile of v3, /device:TPU:0, one launch (start us, length us, event | category | flops | bytes accessed | tf_op | source)
XLA Modules:
  0.0 75.9 jit_solution(2293922177572000258)
XLA Ops:
  0.6 4.5 %shard_map.203 = (bf16[272,128]{1,0:T(8,128)(2,1)S(1)}, bf16[2048,2048]{1,0:T(8,128)(2,1)S(1)}) custom-call(s32[1,4]{1,0:T(1,128)} %bitcast.30, f32[2,2,2,4]{3,2,1,0:T(2,128)} %bitcast.29, bf16[4,64,128]{2,1,0:T(8,128)(2,1)} %bitcast.26, bf16[4,8,128]{2,1,0:T(8,128)(2,1)} %bitcast.27, bf16[4,8,128]{2,1,0:T(8,128)(2,1)} %bitcast.28, ...), custom_call_target="tpu_custom_call" | custom-call | flops 1000000000 | tf_op jit(solution)/shard_map/pallas_call | solution.py:221
  5.9 6.8 %collective-permute-start.1 = (bf16[272,128]{1,0:T(8,128)(2,1)S(1)}, bf16[272,128]{1,0:T(8,128)(2,1)S(1)}, u32[]{:S(2)}, u32[]{:S(2)}) collective-permute-start(bf16[272,128]{1,0:T(8,128)(2,1)S(1)} %get-tuple-element.20.after_ref), channel_id=1, source_target_pairs={{0,2},{1,6},{2,10},{3,14},{4,3},{5,7},{6,11},{7,15},{8,0},{9,4},{1... | collective-permute-start | bytes 208904 | tf_op jit(solution)/shard_map/ppermute | solution.py:748
  12.7 5.9 %shard_map.204.refs_5_.refs_0_ = bf16[2048,4096]{1,0:T(8,128)(2,1)S(1)} custom-call(bf16[2,2048,4096]{2,1,0:T(8,128)(2,1)} %weight_ref.4, bf16[272,128]{1,0:T(8,128)(2,1)S(1)} %get-tuple-element.20.after_ref), custom_call_target="tpu_custom_call" | custom-call | bytes 33554432 | tf_op jit(solution)/shard_map/pallas_call | solution.py:95
  20.8 1.9 %shard_map.205.refs_0_.after_ref = bf16[16,2048]{1,0:T(8,128)(2,1)S(1)} custom-call(bf16[272,128]{1,0:T(8,128)(2,1)S(1)} %collective-permute-done.refs_0_, bf16[272,128]{1,0:T(8,128)(2,1)S(1)} %collective-permute-done.1.refs_1_, bf16[272,128]{1,0:T(8,128)(2,1)S(1)} %collective-permute-done.2.refs_2_, bf16[272,128]{1,0:T(8,128)(2,1)S(1)} %collective-permute-done.3.refs_3_, ...), custom_call_target="tpu_custom_call" | custom-call | flops 20000000000 | tf_op jit(solution)/shard_map/pallas_call | solution.py:273
  22.8 1.5 %collective-permute-start.4 = (bf16[16,2048]{1,0:T(8,128)(2,1)S(1)}, bf16[16,2048]{1,0:T(8,128)(2,1)S(1)}, u32[]{:S(2)}, u32[]{:S(2)}) collective-permute-start(bf16[16,2048]{1,0:T(8,128)(2,1)S(1)} %shard_map.205.refs_0_.after_ref), channel_id=1, source_target_pairs={{0,4},{4,0},{8,12},{12,8},{1,5},{5,1},{9,13},{13,9},{2,6},{6,2},{1... | collective-permute-start | bytes 196616 | tf_op jit(solution)/shard_map/ppermute | solution.py:34
  24.3 2.9 %collective-permute-start.6 = (bf16[16,2048]{1,0:T(8,128)(2,1)S(1)}, bf16[16,2048]{1,0:T(8,128)(2,1)S(1)}, u32[]{:S(2)}, u32[]{:S(2)}) collective-permute-start(bf16[16,2048]{1,0:T(8,128)(2,1)S(1)} %shard_map.205.refs_0_.after_ref), channel_id=1, source_target_pairs={{0,12},{4,8},{8,4},{12,0},{1,13},{5,9},{9,5},{13,1},{2,14},{6,10},... | collective-permute-start | bytes 196616 | tf_op jit(solution)/shard_map/ppermute | solution.py:34
  27.2 5.9 %shard_map.207.refs_1_ = bf16[2048,4096]{1,0:T(8,128)(2,1)S(1)} custom-call(bf16[2,2048,4096]{2,1,0:T(8,128)(2,1)} %weight_ref.4, bf16[16,2048]{1,0:T(8,128)(2,1)S(1)} %shard_map.205.refs_0_.after_ref), custom_call_target="tpu_custom_call" | custom-call | bytes 33554432 | tf_op jit(solution)/shard_map/pallas_call | solution.py:95
  33.4 1.2 %shard_map.210 = bf16[16,2176]{1,0:T(8,128)(2,1)S(1)} custom-call(bf16[16,2048]{1,0:T(8,128)(2,1)S(1)} %get-tuple-element.26.gained_ref, bf16[16,128]{1,0:T(8,128)(2,1)S(1)} %get-tuple-element.27.stats_ref.refs_0_, bf16[2048,4096]{1,0:T(8,128)(2,1)S(1)} %shard_map.204.refs_5_.refs_0_, bf16[2048,4096]{1,0:T(8,128)(2,1)S(1)} %shard_map.207.refs_1_), custom_call_target="tpu_custom_call" | custom-call | flops 134217728 | tf_op jit(solution)/shard_map/pallas_call | solution.py:354
  34.6 1.2 %shard_map.208 = bf16[16,2176]{1,0:T(8,128)(2,1)S(1)} custom-call(bf16[16,2048]{1,0:T(8,128)(2,1)S(1)} %get-tuple-element.26.gained_ref, bf16[16,128]{1,0:T(8,128)(2,1)S(1)} %get-tuple-element.27.stats_ref.refs_0_, bf16[2048,4096]{1,0:T(8,128)(2,1)S(1)} %shard_map.204.refs_5_.refs_0_, bf16[2048,4096]{1,0:T(8,128)(2,1)S(1)} %shard_map.207.refs_1_), custom_call_target="tpu_custom_call" | custom-call | flops 134217728 | tf_op jit(solution)/shard_map/pallas_call | solution.py:354
  36.3 1.2 %shard_map.211 = bf16[16,2176]{1,0:T(8,128)(2,1)S(1)} custom-call(bf16[16,2048]{1,0:T(8,128)(2,1)S(1)} %get-tuple-element.26.gained_ref, bf16[16,128]{1,0:T(8,128)(2,1)S(1)} %get-tuple-element.27.stats_ref.refs_0_, bf16[2048,4096]{1,0:T(8,128)(2,1)S(1)} %shard_map.204.refs_5_.refs_0_, bf16[2048,4096]{1,0:T(8,128)(2,1)S(1)} %shard_map.207.refs_1_, ...), custom_call_target="tpu_custom_call" | custom-call | flops 134217728 | tf_op jit(solution)/shard_map/pallas_call | solution.py:354
  38.0 1.2 %shard_map.209.own_ref = f32[16,2048]{1,0:T(8,128)S(1)} custom-call(bf16[16,2048]{1,0:T(8,128)(2,1)S(1)} %get-tuple-element.26.gained_ref, bf16[16,128]{1,0:T(8,128)(2,1)S(1)} %get-tuple-element.27.stats_ref.refs_0_, bf16[2048,4096]{1,0:T(8,128)(2,1)S(1)} %shard_map.204.refs_5_.refs_0_, bf16[2048,4096]{1,0:T(8,128)(2,1)S(1)} %shard_map.207.refs_1_, ...), custom_call_target="tpu_custom_call" | custom-call | flops 134217728 | tf_op jit(solution)/shard_map/pallas_call | solution.py:354
  39.1 2.8 %collective-permute-done.9.received_ref = bf16[16,2176]{1,0:T(8,128)(2,1)S(1)} collective-permute-done((bf16[16,2176]{1,0:T(8,128)(2,1)S(1)}, bf16[16,2176]{1,0:T(8,128)(2,1)S(1)}, u32[]{:S(2)}, u32[]{:S(2)}) %collective-permute-start.9) | collective-permute-done | bytes 69664 | tf_op jit(solution)/shard_map/ppermute | solution.py:34
  42.4 1.2 %collective-permute-done.10 = f32[16,544]{1,0:T(8,128)S(1)} collective-permute-done((f32[16,544]{1,0:T(8,128)S(1)}, f32[16,544]{1,0:T(8,128)S(1)}, u32[]{:S(2)}, u32[]{:S(2)}) %collective-permute-start.10) | collective-permute-done | bytes 34848 | tf_op jit(solution)/shard_map/ppermute | solution.py:34
  44.5 1.4 %collective-permute-start.12 = (f32[16,544]{1,0:T(8,128)S(1)}, f32[16,544]{1,0:T(8,128)S(1)}, u32[]{:S(2)}, u32[]{:S(2)}) collective-permute-start(f32[16,544]{1,0:T(8,128)S(1)} %add.18.after_ref), channel_id=1, source_target_pairs={{1,11},{3,9},{5,15},{7,13},{9,3},{11,1},{13,7},{15,5},{0,8},{2,10}... | collective-permute-start | bytes 104456 | tf_op jit(solution)/shard_map/ppermute | solution.py:784
  45.9 2.1 %collective-permute-start.13 = (f32[16,544]{1,0:T(8,128)S(1)}, f32[16,544]{1,0:T(8,128)S(1)}, u32[]{:S(2)}, u32[]{:S(2)}) collective-permute-start(f32[16,544]{1,0:T(8,128)S(1)} %add.18.after_ref), channel_id=1, source_target_pairs={{1,7},{3,5},{5,3},{7,1},{9,15},{11,13},{13,11},{15,9},{0,4},{2,6},... | collective-permute-start | bytes 104456 | tf_op jit(solution)/shard_map/ppermute | solution.py:784
  48.9 6.0 %shard_map.213.brought_ref.refs_1_.refs_3_ = bf16[4096,2048]{1,0:T(8,128)(2,1)S(1)} custom-call(bf16[4096,2048]{1,0:T(8,128)(2,1)} %weight_ref.5, f32[16,544]{1,0:T(8,128)S(1)} %add.18.after_ref), custom_call_target="tpu_custom_call" | custom-call | bytes 33554432 | tf_op jit(solution)/shard_map/pallas_call | solution.py:95
  55.0 2.7 %collective-permute-start.15 = (f32[16,544]{1,0:T(8,128)S(1)}, f32[16,544]{1,0:T(8,128)S(1)}, u32[]{:S(2)}, u32[]{:S(2)}) collective-permute-start(f32[16,544]{1,0:T(8,128)S(1)} %add_add_fusion), channel_id=1, source_target_pairs={{0,1},{1,0},{2,3},{3,2},{4,5},{5,4},{6,7},{7,6},{8,9},{9,8},{10,11... | collective-permute-start | bytes 104456 | tf_op jit(solution)/shard_map/ppermute | solution.py:34
  58.7 1.4 %shard_map.214 = (bf16[16,1024]{1,0:T(8,128)(2,1)S(1)}, f32[4,16,1024]{2,1,0:T(8,128)}) custom-call(f32[16,544]{1,0:T(8,128)S(1)} %add.23.mixing_ref, bf16[16,1024]{1,0:T(8,128)(2,1)S(1)} %get-tuple-element.33.conv_ref, bf16[16,1024]{1,0:T(8,128)(2,1)S(1)} %get-tuple-element.34.gate_ref, bf16[512,1024]{1,0:T(8,128)(2,1)S(1)} %copy-done.3, ...), custom_call_target="tpu_custom_call" | custom-call | flops 5000000000 | tf_op jit(solution)/shard_map/pallas_call | solution.py:449
  60.8 1.2 %collective-permute-start.18 = (bf16[16,1024]{1,0:T(8,128)(2,1)S(1)}, bf16[16,1024]{1,0:T(8,128)(2,1)S(1)}, u32[]{:S(2)}, u32[]{:S(2)}) collective-permute-start(bf16[16,1024]{1,0:T(8,128)(2,1)S(1)} %get-tuple-element.36.refs_0_), channel_id=1, source_target_pairs={{0,3},{1,2},{2,1},{3,0},{4,7},{5,6},{6,5},{7,4},{8,11},{9,10},{10,... | collective-permute-start | bytes 98312 | tf_op jit(solution)/shard_map/ppermute | solution.py:34
  62.6 1.9 %collective-permute-done.17.refs_1_ = bf16[16,1024]{1,0:T(8,128)(2,1)S(1)} collective-permute-done((bf16[16,1024]{1,0:T(8,128)(2,1)S(1)}, bf16[16,1024]{1,0:T(8,128)(2,1)S(1)}, u32[]{:S(2)}, u32[]{:S(2)}) %collective-permute-start.17) | collective-permute-done | bytes 32800 | tf_op jit(solution)/shard_map/ppermute | solution.py:34
  64.5 1.7 %shard_map.216.refs_0_ = bf16[16,2048]{1,0:T(8,128)(2,1)S(1)} custom-call(bf16[16,1024]{1,0:T(8,128)(2,1)S(1)} %collective-permute-done.16.refs_0_, bf16[16,1024]{1,0:T(8,128)(2,1)S(1)} %collective-permute-done.17.refs_1_, bf16[16,1024]{1,0:T(8,128)(2,1)S(1)} %collective-permute-done.18.refs_2_, ...), custom_call_target="tpu_custom_call" | custom-call | flops 201326592 | tf_op jit(solution)/shard_map/pallas_call | solution.py:489
  66.7 2.3 %collective-permute-start.20 = (bf16[16,2048]{1,0:T(8,128)(2,1)S(1)}, bf16[16,2048]{1,0:T(8,128)(2,1)S(1)}, u32[]{:S(2)}, u32[]{:S(2)}) collective-permute-start(bf16[16,2048]{1,0:T(8,128)(2,1)S(1)} %shard_map.216.refs_0_), channel_id=1, source_target_pairs={{0,8},{4,12},{8,0},{12,4},{1,9},{5,13},{9,1},{13,5},{2,10},{6,14},... | collective-permute-start | bytes 196616 | tf_op jit(solution)/shard_map/ppermute | solution.py:34
  69.0 1.7 %collective-permute-start.21 = (bf16[16,2048]{1,0:T(8,128)(2,1)S(1)}, bf16[16,2048]{1,0:T(8,128)(2,1)S(1)}, u32[]{:S(2)}, u32[]{:S(2)}) collective-permute-start(bf16[16,2048]{1,0:T(8,128)(2,1)S(1)} %shard_map.216.refs_0_), channel_id=1, source_target_pairs={{0,12},{4,8},{8,4},{12,0},{1,13},{5,9},{9,5},{13,1},{2,14},{6,10},... | collective-permute-start | bytes 196616 | tf_op jit(solution)/shard_map/ppermute | solution.py:34
  71.2 3.2 %collective-permute-done.20.refs_2_ = bf16[16,2048]{1,0:T(8,128)(2,1)S(1)} collective-permute-done((bf16[16,2048]{1,0:T(8,128)(2,1)S(1)}, bf16[16,2048]{1,0:T(8,128)(2,1)S(1)}, u32[]{:S(2)}, u32[]{:S(2)}) %collective-permute-start.20) | collective-permute-done | bytes 65568 | tf_op jit(solution)/shard_map/ppermute | solution.py:34
  (60 shorter events, 11.1 us)
Async XLA Ops:
  5.2 13.4 %collective-permute-start = (bf16[272,128]{1,0:T(8,128)(2,1)S(1)}, bf16[272,128]{1,0:T(8,128)(2,1)S(1)}, u32[]{:S(2)}, u32[]{:S(2)}) collective-permute-start(bf16[272,128]{1,0:T(8,128)(2,1)S(1)} %get-tuple-element.20.after_ref), channel_id=1, source_target_pairs={{0,0},{1,4},{2,8},{3,12},{4,1},{5,5},{6,9},{7,13},{8,2},{9,6},{10,... | collective-permute-start | bytes 208904 | tf_op jit(solution)/shard_map/ppermute | solution.py:748
  5.9 13.6 %collective-permute-start.1 = (bf16[272,128]{1,0:T(8,128)(2,1)S(1)}, bf16[272,128]{1,0:T(8,128)(2,1)S(1)}, u32[]{:S(2)}, u32[]{:S(2)}) collective-permute-start(bf16[272,128]{1,0:T(8,128)(2,1)S(1)} %get-tuple-element.20.after_ref), channel_id=1, source_target_pairs={{0,2},{1,6},{2,10},{3,14},{4,3},{5,7},{6,11},{7,15},{8,0},{9,4},{1... | collective-permute-start | bytes 208904 | tf_op jit(solution)/shard_map/ppermute | solution.py:748
  19.4 1.3 %collective-permute-start.2 = (bf16[272,128]{1,0:T(8,128)(2,1)S(1)}, bf16[272,128]{1,0:T(8,128)(2,1)S(1)}, u32[]{:S(2)}, u32[]{:S(2)}) collective-permute-start(bf16[272,128]{1,0:T(8,128)(2,1)S(1)} %collective-permute-done.refs_0_), channel_id=1, source_target_pairs={{0,1},{1,0},{2,3},{3,2},{4,5},{5,4},{6,7},{7,6},{8,9},{9,8},{10,11... | collective-permute-start | bytes 208904 | tf_op jit(solution)/shard_map/ppermute | solution.py:34
  19.4 1.4 %collective-permute-start.3 = (bf16[272,128]{1,0:T(8,128)(2,1)S(1)}, bf16[272,128]{1,0:T(8,128)(2,1)S(1)}, u32[]{:S(2)}, u32[]{:S(2)}) collective-permute-start(bf16[272,128]{1,0:T(8,128)(2,1)S(1)} %collective-permute-done.1.refs_1_), channel_id=1, source_target_pairs={{0,1},{1,0},{2,3},{3,2},{4,5},{5,4},{6,7},{7,6},{8,9},{9,8},{10,11... | collective-permute-start | bytes 208904 | tf_op jit(solution)/shard_map/ppermute | solution.py:34
  22.8 10.4 %copy-start = (bf16[4,4,2048]{2,1,0:T(4,128)(2,1)S(1)}, bf16[4,4,2048]{2,1,0:T(4,128)(2,1)}, u32[]{:S(2)}) copy-start(bf16[4,4,2048]{2,1,0:T(4,128)(2,1)} %hidden_ref.1) | copy-start | bytes 196612
  22.8 10.4 %copy-start.1 = (f32[2048]{0:T(1024)S(1)}, f32[2048]{0:T(1024)}, u32[]{:S(2)}) copy-start(f32[2048]{0:T(1024)} %param.28) | copy-start | bytes 24580
  22.8 10.3 %collective-permute-start.4 = (bf16[16,2048]{1,0:T(8,128)(2,1)S(1)}, bf16[16,2048]{1,0:T(8,128)(2,1)S(1)}, u32[]{:S(2)}, u32[]{:S(2)}) collective-permute-start(bf16[16,2048]{1,0:T(8,128)(2,1)S(1)} %shard_map.205.refs_0_.after_ref), channel_id=1, source_target_pairs={{0,4},{4,0},{8,12},{12,8},{1,5},{5,1},{9,13},{13,9},{2,6},{6,2},{1... | collective-permute-start | bytes 196616 | tf_op jit(solution)/shard_map/ppermute | solution.py:34
  24.3 8.9 %collective-permute-start.5 = (bf16[16,2048]{1,0:T(8,128)(2,1)S(1)}, bf16[16,2048]{1,0:T(8,128)(2,1)S(1)}, u32[]{:S(2)}, u32[]{:S(2)}) collective-permute-start(bf16[16,2048]{1,0:T(8,128)(2,1)S(1)} %shard_map.205.refs_0_.after_ref), channel_id=1, source_target_pairs={{0,8},{4,12},{8,0},{12,4},{1,9},{5,13},{9,1},{13,5},{2,10},{6,14},... | collective-permute-start | bytes 196616 | tf_op jit(solution)/shard_map/ppermute | solution.py:34
  24.3 8.9 %collective-permute-start.6 = (bf16[16,2048]{1,0:T(8,128)(2,1)S(1)}, bf16[16,2048]{1,0:T(8,128)(2,1)S(1)}, u32[]{:S(2)}, u32[]{:S(2)}) collective-permute-start(bf16[16,2048]{1,0:T(8,128)(2,1)S(1)} %shard_map.205.refs_0_.after_ref), channel_id=1, source_target_pairs={{0,12},{4,8},{8,4},{12,0},{1,13},{5,9},{9,5},{13,1},{2,14},{6,10},... | collective-permute-start | bytes 196616 | tf_op jit(solution)/shard_map/ppermute | solution.py:34
  34.6 1.7 %collective-permute-start.8 = (bf16[16,2176]{1,0:T(8,128)(2,1)S(1)}, bf16[16,2176]{1,0:T(8,128)(2,1)S(1)}, u32[]{:S(2)}, u32[]{:S(2)}) collective-permute-start(bf16[16,2176]{1,0:T(8,128)(2,1)S(1)} %shard_map.210), channel_id=1, source_target_pairs={{0,1},{1,0},{2,3},{3,2},{4,5},{5,4},{6,7},{7,6},{8,9},{9,8},{10,11... | collective-permute-start | bytes 208904 | tf_op jit(solution)/shard_map/ppermute | solution.py:34
  35.8 2.2 %collective-permute-start.7 = (bf16[16,2176]{1,0:T(8,128)(2,1)S(1)}, bf16[16,2176]{1,0:T(8,128)(2,1)S(1)}, u32[]{:S(2)}, u32[]{:S(2)}) collective-permute-start(bf16[16,2176]{1,0:T(8,128)(2,1)S(1)} %shard_map.208), channel_id=1, source_target_pairs={{0,1},{1,0},{2,3},{3,2},{4,5},{5,4},{6,7},{7,6},{8,9},{9,8},{10,11... | collective-permute-start | bytes 208904 | tf_op jit(solution)/shard_map/ppermute | solution.py:34
  37.6 4.4 %collective-permute-start.9 = (bf16[16,2176]{1,0:T(8,128)(2,1)S(1)}, bf16[16,2176]{1,0:T(8,128)(2,1)S(1)}, u32[]{:S(2)}, u32[]{:S(2)}) collective-permute-start(bf16[16,2176]{1,0:T(8,128)(2,1)S(1)} %shard_map.211), channel_id=1, source_target_pairs={{0,2},{2,0},{1,3},{3,1},{4,6},{6,4},{5,7},{7,5},{8,10},{10,8},{9,1... | collective-permute-start | bytes 208904 | tf_op jit(solution)/shard_map/ppermute | solution.py:34
  42.4 1.2 %collective-permute-start.10 = (f32[16,544]{1,0:T(8,128)S(1)}, f32[16,544]{1,0:T(8,128)S(1)}, u32[]{:S(2)}, u32[]{:S(2)}) collective-permute-start(f32[16,544]{1,0:T(8,128)S(1)} %get-tuple-element.28), channel_id=1, source_target_pairs={{0,1},{1,0},{2,3},{3,2},{4,5},{5,4},{6,7},{7,6},{8,9},{9,8},{10,11... | collective-permute-start | bytes 104456 | tf_op jit(solution)/shard_map/ppermute | solution.py:34
  43.6 11.3 %collective-permute-start.11 = (f32[16,544]{1,0:T(8,128)S(1)}, f32[16,544]{1,0:T(8,128)S(1)}, u32[]{:S(2)}, u32[]{:S(2)}) collective-permute-start(f32[16,544]{1,0:T(8,128)S(1)} %add.18.after_ref), channel_id=1, source_target_pairs={{1,15},{3,13},{5,11},{7,9},{9,7},{11,5},{13,3},{15,1},{0,12},{2,14... | collective-permute-start | bytes 104456 | tf_op jit(solution)/shard_map/ppermute | solution.py:784
  44.5 10.4 %collective-permute-start.12 = (f32[16,544]{1,0:T(8,128)S(1)}, f32[16,544]{1,0:T(8,128)S(1)}, u32[]{:S(2)}, u32[]{:S(2)}) collective-permute-start(f32[16,544]{1,0:T(8,128)S(1)} %add.18.after_ref), channel_id=1, source_target_pairs={{1,11},{3,9},{5,15},{7,13},{9,3},{11,1},{13,7},{15,5},{0,8},{2,10}... | collective-permute-start | bytes 104456 | tf_op jit(solution)/shard_map/ppermute | solution.py:784
  45.9 9.1 %collective-permute-start.13 = (f32[16,544]{1,0:T(8,128)S(1)}, f32[16,544]{1,0:T(8,128)S(1)}, u32[]{:S(2)}, u32[]{:S(2)}) collective-permute-start(f32[16,544]{1,0:T(8,128)S(1)} %add.18.after_ref), channel_id=1, source_target_pairs={{1,7},{3,5},{5,3},{7,1},{9,15},{11,13},{13,11},{15,9},{0,4},{2,6},... | collective-permute-start | bytes 104456 | tf_op jit(solution)/shard_map/ppermute | solution.py:784
  48.0 7.0 %collective-permute-start.14 = (f32[16,544]{1,0:T(8,128)S(1)}, f32[16,544]{1,0:T(8,128)S(1)}, u32[]{:S(2)}, u32[]{:S(2)}) collective-permute-start(f32[16,544]{1,0:T(8,128)S(1)} %add.18.after_ref), channel_id=1, source_target_pairs={{1,3},{3,1},{5,7},{7,5},{9,11},{11,9},{13,15},{15,13},{17,19},{19,... | collective-permute-start | bytes 104456 | tf_op jit(solution)/shard_map/ppermute | solution.py:784
  55.0 3.6 %collective-permute-start.15 = (f32[16,544]{1,0:T(8,128)S(1)}, f32[16,544]{1,0:T(8,128)S(1)}, u32[]{:S(2)}, u32[]{:S(2)}) collective-permute-start(f32[16,544]{1,0:T(8,128)S(1)} %add_add_fusion), channel_id=1, source_target_pairs={{0,1},{1,0},{2,3},{3,2},{4,5},{5,4},{6,7},{7,6},{8,9},{9,8},{10,11... | collective-permute-start | bytes 104456 | tf_op jit(solution)/shard_map/ppermute | solution.py:34
  60.1 2.5 %collective-permute-start.16 = (bf16[16,1024]{1,0:T(8,128)(2,1)S(1)}, bf16[16,1024]{1,0:T(8,128)(2,1)S(1)}, u32[]{:S(2)}, u32[]{:S(2)}) collective-permute-start(bf16[16,1024]{1,0:T(8,128)(2,1)S(1)} %get-tuple-element.36.refs_0_), channel_id=1, source_target_pairs={{0,1},{1,0},{2,3},{3,2},{4,5},{5,4},{6,7},{7,6},{8,9},{9,8},{10,11... | collective-permute-start | bytes 98312 | tf_op jit(solution)/shard_map/ppermute | solution.py:34
  60.5 4.0 %collective-permute-start.17 = (bf16[16,1024]{1,0:T(8,128)(2,1)S(1)}, bf16[16,1024]{1,0:T(8,128)(2,1)S(1)}, u32[]{:S(2)}, u32[]{:S(2)}) collective-permute-start(bf16[16,1024]{1,0:T(8,128)(2,1)S(1)} %get-tuple-element.36.refs_0_), channel_id=1, source_target_pairs={{0,2},{1,3},{2,0},{3,1},{4,6},{5,7},{6,4},{7,5},{8,10},{9,11},{10,... | collective-permute-start | bytes 98312 | tf_op jit(solution)/shard_map/ppermute | solution.py:34
  60.8 3.7 %collective-permute-start.18 = (bf16[16,1024]{1,0:T(8,128)(2,1)S(1)}, bf16[16,1024]{1,0:T(8,128)(2,1)S(1)}, u32[]{:S(2)}, u32[]{:S(2)}) collective-permute-start(bf16[16,1024]{1,0:T(8,128)(2,1)S(1)} %get-tuple-element.36.refs_0_), channel_id=1, source_target_pairs={{0,3},{1,2},{2,1},{3,0},{4,7},{5,6},{6,5},{7,4},{8,11},{9,10},{10,... | collective-permute-start | bytes 98312 | tf_op jit(solution)/shard_map/ppermute | solution.py:34
  66.2 5.0 %collective-permute-start.19 = (bf16[16,2048]{1,0:T(8,128)(2,1)S(1)}, bf16[16,2048]{1,0:T(8,128)(2,1)S(1)}, u32[]{:S(2)}, u32[]{:S(2)}) collective-permute-start(bf16[16,2048]{1,0:T(8,128)(2,1)S(1)} %shard_map.216.refs_0_), channel_id=1, source_target_pairs={{0,4},{4,0},{8,12},{12,8},{1,5},{5,1},{9,13},{13,9},{2,6},{6,2},{1... | collective-permute-start | bytes 196616 | tf_op jit(solution)/shard_map/ppermute | solution.py:34
  66.7 7.7 %collective-permute-start.20 = (bf16[16,2048]{1,0:T(8,128)(2,1)S(1)}, bf16[16,2048]{1,0:T(8,128)(2,1)S(1)}, u32[]{:S(2)}, u32[]{:S(2)}) collective-permute-start(bf16[16,2048]{1,0:T(8,128)(2,1)S(1)} %shard_map.216.refs_0_), channel_id=1, source_target_pairs={{0,8},{4,12},{8,0},{12,4},{1,9},{5,13},{9,1},{13,5},{2,10},{6,14},... | collective-permute-start | bytes 196616 | tf_op jit(solution)/shard_map/ppermute | solution.py:34
  69.0 6.2 %collective-permute-start.21 = (bf16[16,2048]{1,0:T(8,128)(2,1)S(1)}, bf16[16,2048]{1,0:T(8,128)(2,1)S(1)}, u32[]{:S(2)}, u32[]{:S(2)}) collective-permute-start(bf16[16,2048]{1,0:T(8,128)(2,1)S(1)} %shard_map.216.refs_0_), channel_id=1, source_target_pairs={{0,12},{4,8},{8,4},{12,0},{1,13},{5,9},{9,5},{13,1},{2,14},{6,10},... | collective-permute-start | bytes 196616 | tf_op jit(solution)/shard_map/ppermute | solution.py:34
  (9 other events, 66.3 us)

commit v4 on v3

--- a/solution.py
+++ b/solution.py
@@ -13,9 +13,7 @@
 DIRECT = 8
 LANES = 128
 MIB = 1024 * 1024
-PIECES = 8
-ATT_LIMIT = 8
-LOAD_LIMIT = 2
+PIECES = 4
 FLOPS_AHEAD = 20_000_000_000
 
 
@@ -72,40 +70,90 @@
     return [pl.BlockSpec(memory_space=pltpu.VMEM)] * count
 
 
-def pieces_of(source, target, ready):
+def in_pieces(source, target):
     rows = target.shape[0] // PIECES
-    return [
-        pltpu.make_async_copy(
-            source.at[k * rows : (k + 1) * rows], target.at[k * rows : (k + 1) * rows], ready.at[k]
-        )
-        for k in range(PIECES)
-    ]
-
-
-def bring(weight, part, after):
-    shape = weight.shape if part is None else weight.shape[1:]
-
-    def kernel(weight_ref, after_ref, out_ref, ready):
-        copies = pieces_of(weight_ref if part is None else weight_ref.at[part], out_ref, ready)
-        for copy in copies:
-            copy.start()
-        for copy in copies:
+    return [(source.at[k * rows : (k + 1) * rows], target.at[k * rows : (k + 1) * rows]) for k in range(PIECES)]
+
+
+def hs_position():
+    return lax.axis_index("head") * lax.axis_size("sub") + lax.axis_index("sub")
+
+
+def whole_job(weight):
+    return weight, weight.shape, in_pieces, PIECES
+
+
+def block_job(weight, own_width, flip):
+    def views(source, target):
+        columns = pl.ds(pl.multiple_of((hs_position() ^ flip) * own_width, own_width), own_width)
+        return [
+            pair for part in range(2) for pair in in_pieces(source.at[part, :, columns], target.at[part])
+        ]
+
+    return weight, (2, weight.shape[1], own_width), views, 2 * PIECES
+
+
+def rows_job(weight, own_width, flips):
+    def views(source, target):
+        pairs = []
+        for place, flip in enumerate(flips):
+            base = pl.multiple_of((hs_position() ^ flip) * own_width, own_width)
+            pairs += in_pieces(source.at[pl.ds(base, own_width)], target.at[place])
+        return pairs
+
+    return weight, (len(flips), own_width, weight.shape[1]), views, len(flips) * PIECES
+
+
+def job_shapes(jobs):
+    return [pltpu.VMEM(job[1], job[0].dtype) for job in jobs]
+
+
+def job_inputs(jobs):
+    return [pltpu.with_memory_space_constraint(job[0], pltpu.HBM) for job in jobs]
+
+
+def job_bytes(jobs):
+    return sum(2 * math.prod(job[1]) * job[0].dtype.itemsize for job in jobs)
+
+
+def job_sems(jobs):
+    count = sum(job[3] for job in jobs)
+    return [pltpu.SemaphoreType.DMA((count,))] if jobs else []
+
+
+def start_jobs(jobs, sources, targets, ready):
+    pairs = []
+    for job, source, target in zip(jobs, sources, targets):
+        pairs += job[2](source, target)
+    copies = [pltpu.make_async_copy(source, target, ready.at[k]) for k, (source, target) in enumerate(pairs)]
+    for copy in copies:
+        copy.start()
+    return copies
+
+
+def anywhere(count):
+    return [pl.BlockSpec(memory_space=pl.ANY)] * count
+
+
+def bring(jobs, after):
+    count = len(jobs)
+
+    def kernel(*refs):
+        for copy in start_jobs(jobs, refs[:count], refs[count + 1 : -1], refs[-1]):
             copy.wait()
 
     return pl.pallas_call(
         kernel,
-        out_shape=pltpu.VMEM(shape, weight.dtype),
-        in_specs=[pl.BlockSpec(memory_space=pl.ANY)] * 2,
-        out_specs=whole(1)[0],
-        scratch_shapes=[pltpu.SemaphoreType.DMA((PIECES,))],
-        compiler_params=pltpu.CompilerParams(vmem_limit_bytes=LOAD_LIMIT * MIB),
-        cost_estimate=pl.CostEstimate(
-            flops=0, bytes_accessed=2 * math.prod(shape) * weight.dtype.itemsize, transcendentals=0
-        ),
-    )(pltpu.with_memory_space_constraint(weight, pltpu.HBM), after)
-
-
-def attention(query, key_new, value_new, kv_cache, kv_scale, context_len, weight):
+        out_shape=tuple(job_shapes(jobs)),
+        in_specs=anywhere(count + 1),
+        out_specs=tuple(whole(count)),
+        scratch_shapes=job_sems(jobs),
+        compiler_params=pltpu.CompilerParams(vmem_limit_bytes=2 * MIB),
+        cost_estimate=pl.CostEstimate(flops=0, bytes_accessed=job_bytes(jobs), transcendentals=0),
+    )(*job_inputs(jobs), after)
+
+
+def attention(query, key_new, value_new, kv_cache, kv_scale, context_len, jobs):
     requests, steps, heads, dim = query.shape
     kv_heads = key_new.shape[2]
     group = heads // kv_heads
@@ -118,8 +166,9 @@
     news = steps * kv_heads
 
     def kernel(*refs):
-        sources, weight_source, out_ref, weight_ref = refs[:6], refs[6], refs[7], refs[8]
-        held, ready, weight_ready = refs[9:15], refs[15], refs[16]
+        count = len(jobs)
+        sources, job_sources, refs = refs[:6], refs[6 : 6 + count], refs[6 + count :]
+        out_ref, targets, held, ready = refs[0], refs[1 : 1 + count], refs[1 + count : 7 + count], refs[7 + count]
         length_ref, scale_ref, query_ref, key_ref, value_ref, cache_ref = held
         copies = [
             pltpu.make_async_copy(sources[k], held[k], ready.at[k]) for k in range(5)
@@ -129,9 +178,7 @@
         ]
         for copy in copies:
             copy.start()
-        weight_copies = pieces_of(weight_source, weight_ref, weight_ready)
-        for copy in weight_copies:
-            copy.start()
+        job_copies = start_jobs(jobs, job_sources, targets, refs[-1])
         shard = lax.axis_index("seq")
         row = lax.broadcasted_iota(jnp.int32, (lines, width), 0)
         column = lax.broadcasted_iota(jnp.int32, (lines, width), 1)
@@ -207,7 +254,7 @@
         out_ref[total_rows:, :] = jnp.concatenate(
             [turned[:, k * LANES : (k + 1) * LANES] for k in range(total_rows // LANES)], axis=0
         ).astype(jnp.bfloat16)
-        for copy in weight_copies:
+        for copy in job_copies:
             copy.wait()
 
     given_all = (
@@ -220,24 +267,24 @@
     )
     return pl.pallas_call(
         kernel,
-        out_shape=(
-            jax.ShapeDtypeStruct((total_rows + total_rows // 16, dim), jnp.bfloat16),
-            pltpu.VMEM(weight.shape, weight.dtype),
+        out_shape=tuple(
+            [jax.ShapeDtypeStruct((total_rows + total_rows // 16, dim), jnp.bfloat16)] + job_shapes(jobs)
         ),
-        in_specs=[pl.BlockSpec(memory_space=pl.ANY)] * 7,
-        out_specs=tuple(whole(2)),
+        in_specs=anywhere(6 + len(jobs)),
+        out_specs=tuple(whole(1 + len(jobs))),
         scratch_shapes=[pltpu.VMEM(given.shape, given.dtype) for given in given_all]
-        + [pltpu.SemaphoreType.DMA((5 + requests,)), pltpu.SemaphoreType.DMA((PIECES,))],
-        compiler_params=pltpu.CompilerParams(vmem_limit_bytes=ATT_LIMIT * MIB),
+        + [pltpu.SemaphoreType.DMA((5 + requests,))]
+        + job_sems(jobs),
+        compiler_params=pltpu.CompilerParams(vmem_limit_bytes=8 * MIB),
         cost_estimate=cost(1_000_000_000),
-    )(*[pltpu.with_memory_space_constraint(given, pltpu.HBM) for given in given_all + (weight,)])
+    )(*[pltpu.with_memory_space_constraint(given, pltpu.HBM) for given in given_all], *job_inputs(jobs))
 
 
 def cost(flops):
     return pl.CostEstimate(flops=flops, bytes_accessed=0, transcendentals=0)
 
 
-def merge_project(parts, weight, rows, heads, dim, brought):
+def merge_project(parts, weight, rows, heads, dim):
     lines = rows * heads
     count = len(parts)
     depth, width = weight.shape
@@ -273,12 +320,12 @@
     return pl.pallas_call(
         kernel,
         out_shape=jax.ShapeDtypeStruct((rows, width), jnp.bfloat16),
-        in_specs=whole(count + 1) + [pl.BlockSpec(memory_space=pl.ANY)],
+        in_specs=whole(count + 1),
         out_specs=whole(1)[0],
         scratch_shapes=[pltpu.VMEM((lines, dim), jnp.float32), pltpu.VMEM((rows, heads * dim), jnp.bfloat16)],
         compiler_params=pltpu.CompilerParams(vmem_limit_bytes=4 * MIB),
         cost_estimate=cost(FLOPS_AHEAD),
-    )(*parts, weight, brought)
+    )(*parts, weight)
 
 
 def in_three(left):
@@ -321,47 +368,51 @@
     )(hidden, gain.reshape(1, width), *parts)
 
 
-def hs_position():
-    return lax.axis_index("head") * lax.axis_size("sub") + lax.axis_index("sub")
-
-
-def project_block(gained, weights, stats, own_width, flip, arrived=None):
+def project_block(gained, weight, own_width, kind, stats):
     rows, depth = gained.shape
     width = 2 * own_width
     tile = tile_of(own_width, 512)
-    kind = jnp.bfloat16 if flip else jnp.float32
-    extra = () if arrived is None else (arrived,)
-
-    def kernel(gained_ref, stats_ref, *refs):
-        weight_refs, refs, out_ref = refs[:2], refs[2:], refs[-1]
-        base = (hs_position() ^ flip) * own_width
+    riders = () if stats is None else (stats,)
+
+    def kernel(gained_ref, weight_ref, *refs):
+        out_ref = refs[-1]
         for part in range(2):
             for start in range(0, own_width, tile):
-                columns = pl.ds(pl.multiple_of(base + start, tile), tile)
-                place = slice(part * own_width + start, part * own_width + start + tile)
-                block = jnp.dot(
-                    gained_ref[...], weight_refs[part][:, columns], preferred_element_type=jnp.float32
-                )
-                if extra:
-                    block = block + refs[0][:, place].astype(jnp.float32)
-                out_ref[:, place] = block.astype(kind)
-        if flip and extra:
-            both = stats_ref[...].astype(jnp.float32) + refs[0][:, width:].astype(jnp.float32)
-            out_ref[:, width:] = in_three(jnp.sum(both, axis=1, keepdims=True))
-        elif flip:
-            out_ref[:, width:] = stats_ref[...]
-
-    return pl.pallas_call(
-        kernel,
-        out_shape=jax.ShapeDtypeStruct((rows, width + (LANES if flip else 0)), kind),
-        in_specs=whole(4 + len(extra)),
+                out_ref[:, part * own_width + start : part * own_width + start + tile] = jnp.dot(
+                    gained_ref[...], weight_ref[part, :, start : start + tile], preferred_element_type=jnp.float32
+                ).astype(kind)
+        if riders:
+            out_ref[:, width:] = refs[0][...]
+
+    return pl.pallas_call(
+        kernel,
+        out_shape=jax.ShapeDtypeStruct((rows, width + (LANES if riders else 0)), kind),
+        in_specs=whole(2 + len(riders)),
         out_specs=whole(1)[0],
         compiler_params=pltpu.CompilerParams(vmem_limit_bytes=4 * MIB),
         cost_estimate=cost(2 * rows * depth * width),
-    )(gained, stats, *weights, *extra)
-
-
-def convolve(own, received, squares, state, taps, bias, weight, features):
+    )(gained, weight, *riders)
+
+
+def relay(block, arrived, stats):
+    rows, width = block.shape
+
+    def kernel(block_ref, arrived_ref, stats_ref, out_ref):
+        out_ref[:, :width] = (block_ref[...] + arrived_ref[:, :width].astype(jnp.float32)).astype(jnp.bfloat16)
+        both = stats_ref[...].astype(jnp.float32) + arrived_ref[:, width:].astype(jnp.float32)
+        out_ref[:, width:] = in_three(jnp.sum(both, axis=1, keepdims=True))
+
+    return pl.pallas_call(
+        kernel,
+        out_shape=jax.ShapeDtypeStruct((rows, width + LANES), jnp.bfloat16),
+        in_specs=whole(3),
+        out_specs=whole(1)[0],
+        compiler_params=pltpu.CompilerParams(vmem_limit_bytes=4 * MIB),
+        cost_estimate=cost(rows * width * 8),
+    )(block, arrived, stats)
+
+
+def convolve(own, near, received, squares, state, taps, bias, weight, features):
     rows, width = own.shape
     own_width = width // 2
     requests = state.shape[1]
@@ -369,12 +420,12 @@
     mixed_width = weight.shape[0]
     count = len(squares)
 
-    def kernel(own_ref, received_ref, state_ref, taps_ref, bias_ref, weight_ref, *refs):
+    def kernel(own_ref, near_ref, received_ref, state_ref, taps_ref, bias_ref, weight_ref, *refs):
         squares_refs, (conv_ref, gate_ref, mixing_ref) = refs[:count], refs[count:]
         pieces = received_ref[:, width:].astype(jnp.float32)
         for ref in squares_refs:
             pieces = pieces + ref[:, ref.shape[1] - LANES :].astype(jnp.float32)
-        channels = own_ref[...] + received_ref[:, :width].astype(jnp.float32)
+        channels = (own_ref[...] + near_ref[...].astype(jnp.float32)) + received_ref[:, :width].astype(jnp.float32)
         squares = jnp.sum(pieces, axis=1, keepdims=True)
         channels = (channels * lax.rsqrt(squares / features + EPS)).astype(jnp.bfloat16)
         gate_ref[...] = channels[:, own_width:]
@@ -401,11 +452,11 @@
             jax.ShapeDtypeStruct((rows, own_width), jnp.bfloat16),
             jax.ShapeDtypeStruct((rows, mixed_width), jnp.float32),
         ),
-        in_specs=whole(6 + count),
+        in_specs=whole(7 + count),
         out_specs=tuple(whole(3)),
         compiler_params=pltpu.CompilerParams(vmem_limit_bytes=8 * MIB),
         cost_estimate=cost(FLOPS_AHEAD),
-    )(own, received, state, taps, bias, weight, *squares)
+    )(own, near, received, state, taps, bias, weight, *squares)
 
 
 def scan_states(mixing, conv, gate, dt_weight, dt_bias, decay, skip, state, brought):
@@ -460,40 +511,34 @@
     )(mixing, conv, gate, dt_weight, dt_bias, decay, skip, state, brought)
 
 
-def project_out(blocks, flips, weight, before):
+def project_out(blocks, weights, before):
     rows, own_width = blocks[0].shape
-    width = weight.shape[1]
+    width = weights[0].shape[2]
+    count = len(blocks)
+    end = count + len(weights)
     tile = tile_of(width, 512)
     kind = jnp.float32 if before is None else jnp.bfloat16
+    places = [(k, place) for k, weight in enumerate(weights) for place in range(weight.shape[0])]
 
     def kernel(*refs):
-        block_refs, weight_ref, out_ref = refs[: len(flips)], refs[len(flips)], refs[-1]
+        block_refs, weight_refs, out_ref = refs[:count], refs[count:end], refs[-1]
         for start in range(0, width, tile):
             columns = slice(start, start + tile)
-            terms = []
-            for ref, flip in zip(block_refs, flips):
-                base = pl.multiple_of((hs_position() ^ flip) * own_width, own_width)
-                terms.append(
-                    jnp.dot(
-                        ref[...], weight_ref[pl.ds(base, own_width), columns], preferred_element_type=jnp.float32
-                    )
-                )
-            total = terms[0]
-            for term in terms[1:]:
-                total = total + term
-            if before is not None:
-                total = total + refs[len(flips) + 1][:, columns]
+            total = None if before is None else refs[end][:, columns]
+            for ref, (k, place) in zip(block_refs, places):
+                term = jnp.dot(ref[...], weight_refs[k][place, :, columns], preferred_element_type=jnp.float32)
+                total = term if total is None else total + term
             out_ref[:, columns] = total.astype(kind)
 
     extra = () if before is None else (before,)
     return pl.pallas_call(
         kernel,
         out_shape=jax.ShapeDtypeStruct((rows, width), kind),
-        in_specs=whole(len(blocks) + 1 + len(extra)),
+        in_specs=whole(end + len(extra)),
         out_specs=whole(1)[0],
         compiler_params=pltpu.CompilerParams(vmem_limit_bytes=4 * MIB),
-        cost_estimate=cost(2 * rows * own_width * width * len(flips)),
-    )(*blocks, weight, *extra)
+        cost_estimate=cost(2 * rows * own_width * width * count),
+    )(*blocks, *weights, *extra)
 
 
 def finish(residual, parts, requests):
@@ -740,9 +785,10 @@
             mamba_out_weight,
         )
     part, out_rows = attention(
-        query, key_new, value_new, kv_cache, kv_scale, context_len, attn_out_weight
-    )
-    first_in = bring(in_weight, 0, part)
+        query, key_new, value_new, kv_cache, kv_scale, context_len, [whole_job(attn_out_weight)]
+    )
+    columns = lambda flip: block_job(in_weight, own_width, flip)
+    far_columns, chip_columns = bring([columns(3), columns(2)], part)
     place = range(hs_count)
     parts = [
         lax.ppermute(
@@ -756,19 +802,24 @@
         )
         for turn in range(2)
     ]
-    parts, first_in = lax.optimization_barrier((parts, first_in))
+    parts, far_columns, chip_columns = lax.optimization_barrier((parts, far_columns, chip_columns))
     parts = parts + [crossed(arrived, "sub", 1) for arrived in parts]
-    partial = merge_project(parts, out_rows, rows, heads, dim, first_in)
-    second_in = bring(in_weight, 1, partial)
-    residual, gained, stats = add_residual(hidden, crossed_all(partial, "seq"), norm_gain)
+    partial = merge_project(parts, out_rows, rows, heads, dim)
+    core_columns, own_columns = bring([columns(1), columns(0)], partial)
+    terms, core_columns, own_columns = lax.optimization_barrier(
+        (crossed_all(partial, "seq"), core_columns, own_columns)
+    )
+    residual, gained, stats = add_residual(hidden, terms, norm_gain)
     features = residual.shape[1] * hs_count
-    give = lambda flip, arrived=None: project_block(gained, (first_in, second_in), stats, own_width, flip, arrived)
-    for_far = crossed(give(3), "sub", 1)
-    for_near = crossed(give(1), "sub", 1)
-    received = crossed(give(2, for_far), "head", 1)
-    own = give(0, for_near)
+    for_far = crossed(project_block(gained, far_columns, own_width, jnp.bfloat16, stats), "sub", 1)
+    block = relay(project_block(gained, chip_columns, own_width, jnp.float32, None), for_far, stats)
+    received = crossed(block, "head", 1)
+    late, block = lax.optimization_barrier((gained, block))
+    near = crossed(project_block(late, core_columns, own_width, jnp.bfloat16, None), "sub", 1)
+    own = project_block(late, own_columns, own_width, jnp.float32, None)
     conv, gate, mixing = convolve(
         own,
+        near,
         received,
         [stats, for_far],
         conv_state.transpose(1, 0, 2),
@@ -778,7 +829,8 @@
         features,
     )
     mixing = mixing + crossed(mixing, "sub", 1)
-    mamba_rows = bring(mamba_out_weight, None, mixing)
+    mamba_rows = lambda flips: rows_job(mamba_out_weight, own_width, flips)
+    own_rows, other_rows = bring([mamba_rows([0]), mamba_rows([1, 2])], mixing)
     base = lambda s, x, c: s * hs_count + x * 2 + c
     arrived = [
         lax.ppermute(
@@ -789,7 +841,7 @@
         )
         for flip in range(seq_count - 1, -1, -1)
     ]
-    arrived, mamba_rows = lax.optimization_barrier((arrived, mamba_rows))
+    arrived, own_rows, other_rows = lax.optimization_barrier((arrived, own_rows, other_rows))
     line = jnp.where(lax.axis_index("sub") == 0, mixing, 0.0) + paired_sum(arrived)
     mixing = line + crossed(line, "sub", 1)
     gated, state = scan_states(
@@ -801,11 +853,12 @@
         decay_rate.T,
         skip_gain.reshape(1, -1),
         ssm_state.transpose(0, 2, 1),
-        mamba_rows,
-    )
-    blocks = crossed_all(gated, HS)
-    first = project_out(blocks[:1], [0], mamba_rows, None)
-    partial = project_out(blocks[1:], list(place)[1:], mamba_rows, first)
+        other_rows,
+    )
+    (last_rows,) = bring([mamba_rows([3])], gated)
+    first = project_out([gated], [own_rows], None)
+    blocks, last_rows, first = lax.optimization_barrier((crossed_all(gated, HS), last_rows, first))
+    partial = project_out(blocks[1:], [other_rows, last_rows], first)
     final = finish(residual, crossed_all(partial, "seq"), requests)
     return final, state.transpose(0, 2, 1)
 

time: 76 us -> 73.2 us (0.963)
  waiting for transfers between devices: 13 us -> 9.84 us
    ppermute x16, waiting for transfers between devices: 12.2 us -> 9.07 us  [crossed(): lax.ppermute(value, axes, [(i, i ^ flip) for i in range(lax.axis_size(axe...]
    pallas_call x4 -> x6, Pallas kernels: 22.4 us -> 23.1 us  [the longest x4 19 us: bring(): pl.pallas_call(kernel, out_shape=tuple(job_shapes(jobs)), in_specs=anywhe...]
  transfers between devices with their start and end apart: 22 -> 22, of which waited for: 10 -> 9; matrix products, arithmetic and copies ran while one was open for 0% -> 0% of each run, Pallas kernels for 29% -> 32%
where the time goes in v4:
time: 73.2 us; the launch traced here: 73 us
  Pallas kernels  35 us (48%)
  starting transfers between devices  27.2 us (37%)
  waiting for transfers between devices  9.84 us (13%)
  between operations  0.92 us (1%)
    pallas_call x4, Pallas kernels, bring(): pl.pallas_call(kernel, out_shape=tuple(job_shapes(jobs)), in_specs=anywhe...  19 us
    ppermute x16, starting transfers between devices, crossed(): lax.ppermute(value, axes, [(i, i ^ flip) for i in range(lax.axis_size(axe...  14.5 us
    ppermute x16, waiting for transfers between devices, crossed(): lax.ppermute(value, axes, [(i, i ^ flip) for i in range(lax.axis_size(axe...  9.07 us
    ppermute x2, starting transfers between devices, local(): lax.ppermute(part, ('seq',) + HS, [(s * hs_count + j, j * hs_count + (s /...  7.46 us
    ppermute x4, starting transfers between devices, local(): lax.ppermute(mixing, ('seq',) + HS, [(base(s, x, 1), base(s ^ flip, x ^ 1...  5.22 us
    pallas_call x4, Pallas kernels, project_block(): pl.pallas_call(kernel, out_shape=jax.ShapeDtypeStruct((rows, width + (LAN...  4.78 us
    pallas_call x1, Pallas kernels, attention(): pl.pallas_call(kernel, out_shape=tuple([jax.ShapeDtypeStruct((total_rows...  3.98 us
    pallas_call x2, Pallas kernels, project_out(): pl.pallas_call(kernel, out_shape=jax.ShapeDtypeStruct((rows, width), kind...  2.38 us
  transfers between devices with their start and end apart: 22, of which 9 were waited for; matrix products, arithmetic and copies ran while one was open for 0% of the time, Pallas kernels for 32%

profile of v4, /device:TPU:0, one launch (start us, length us, event | category | flops | bytes accessed | tf_op | source)
XLA Modules:
  0.0 73.0 jit_solution(9693281643498367457)
XLA Ops:
  0.6 4.0 %shard_map.203 = (bf16[272,128]{1,0:T(8,128)(2,1)S(1)}, bf16[2048,2048]{1,0:T(8,128)(2,1)S(1)}) custom-call(s32[1,4]{1,0:T(1,128)} %bitcast.30, f32[2,2,2,4]{3,2,1,0:T(2,128)} %bitcast.29, bf16[4,64,128]{2,1,0:T(8,128)(2,1)} %bitcast.26, bf16[4,8,128]{2,1,0:T(8,128)(2,1)} %bitcast.27, bf16[4,8,128]{2,1,0:T(8,128)(2,1)} %bitcast.28, ...), custom_call_target="tpu_custom_call" | custom-call | flops 1000000000 | tf_op jit(solution)/shard_map/pallas_call | solution.py:268
  5.3 6.8 %collective-permute-start.1 = (bf16[272,128]{1,0:T(8,128)(2,1)S(1)}, bf16[272,128]{1,0:T(8,128)(2,1)S(1)}, u32[]{:S(2)}, u32[]{:S(2)}) collective-permute-start(bf16[272,128]{1,0:T(8,128)(2,1)S(1)} %get-tuple-element.40.refs_2_), channel_id=1, source_target_pairs={{0,2},{1,6},{2,10},{3,14},{4,3},{5,7},{6,11},{7,15},{8,0},{9,4},{1... | collective-permute-start | bytes 208904 | tf_op jit(solution)/shard_map/ppermute | solution.py:794
  12.1 6.0 %shard_map.204 = (bf16[2,2048,1024]{2,1,0:T(8,128)(2,1)S(1)}, bf16[2,2048,1024]{2,1,0:T(8,128)(2,1)S(1)}) custom-call(bf16[2,2048,4096]{2,1,0:T(8,128)(2,1)} %refs_1_.4, bf16[2,2048,4096]{2,1,0:T(8,128)(2,1)} %refs_1_.4, bf16[272,128]{1,0:T(8,128)(2,1)S(1)} %get-tuple-element.40.refs_2_), custom_call_target="tpu_custom_call" | custom-call | bytes 33554432 | tf_op jit(solution)/shard_map/pallas_call | solution.py:145
  20.3 2.0 %shard_map.205.refs_2_.refs_0_ = bf16[16,2048]{1,0:T(8,128)(2,1)S(1)} custom-call(bf16[272,128]{1,0:T(8,128)(2,1)S(1)} %collective-permute-done.refs_0_, bf16[272,128]{1,0:T(8,128)(2,1)S(1)} %collective-permute-done.1.refs_1_, bf16[272,128]{1,0:T(8,128)(2,1)S(1)} %collective-permute-done.2.refs_2_, bf16[272,128]{1,0:T(8,128)(2,1)S(1)} %collective-permute-done.3.refs_3_, ...), custom_call_target="tpu_custom_call" | custom-call | flops 20000000000 | tf_op jit(solution)/shard_map/pallas_call | solution.py:320
  22.2 1.5 %collective-permute-start.4 = (bf16[16,2048]{1,0:T(8,128)(2,1)S(1)}, bf16[16,2048]{1,0:T(8,128)(2,1)S(1)}, u32[]{:S(2)}, u32[]{:S(2)}) collective-permute-start(bf16[16,2048]{1,0:T(8,128)(2,1)S(1)} %shard_map.205.refs_2_.refs_0_), channel_id=1, source_target_pairs={{0,4},{4,0},{8,12},{12,8},{1,5},{5,1},{9,13},{13,9},{2,6},{6,2},{1... | collective-permute-start | bytes 196616 | tf_op jit(solution)/shard_map/ppermute | solution.py:32
  23.8 2.9 %collective-permute-start.6 = (bf16[16,2048]{1,0:T(8,128)(2,1)S(1)}, bf16[16,2048]{1,0:T(8,128)(2,1)S(1)}, u32[]{:S(2)}, u32[]{:S(2)}) collective-permute-start(bf16[16,2048]{1,0:T(8,128)(2,1)S(1)} %shard_map.205.refs_2_.refs_0_), channel_id=1, source_target_pairs={{0,12},{4,8},{8,4},{12,0},{1,13},{5,9},{9,5},{13,1},{2,14},{6,10},... | collective-permute-start | bytes 196616 | tf_op jit(solution)/shard_map/ppermute | solution.py:32
  26.7 6.0 %shard_map.206 = (bf16[2,2048,1024]{2,1,0:T(8,128)(2,1)S(1)}, bf16[2,2048,1024]{2,1,0:T(8,128)(2,1)S(1)}) custom-call(bf16[2,2048,4096]{2,1,0:T(8,128)(2,1)} %refs_1_.4, bf16[2,2048,4096]{2,1,0:T(8,128)(2,1)} %refs_1_.4, bf16[16,2048]{1,0:T(8,128)(2,1)S(1)} %shard_map.205.refs_2_.refs_0_), custom_call_target="tpu_custom_call" | custom-call | bytes 33554432 | tf_op jit(solution)/shard_map/pallas_call | solution.py:145
  32.9 1.2 %shard_map.209 = bf16[16,2176]{1,0:T(8,128)(2,1)S(1)} custom-call(bf16[16,2048]{1,0:T(8,128)(2,1)S(1)} %get-tuple-element.57.gained_ref, bf16[2,2048,1024]{2,1,0:T(8,128)(2,1)S(1)} %get-tuple-element.55.weight_ref, bf16[16,128]{1,0:T(8,128)(2,1)S(1)} %get-tuple-element.56.refs_0_.stats_ref), custom_call_target="tpu_custom_call" | custom-call | flops 134217728 | tf_op jit(solution)/shard_map/pallas_call | solution.py:387
  34.1 1.2 %shard_map.208.block_ref = f32[16,2048]{1,0:T(8,128)S(1)} custom-call(bf16[16,2048]{1,0:T(8,128)(2,1)S(1)} %get-tuple-element.57.gained_ref, bf16[2,2048,1024]{2,1,0:T(8,128)(2,1)S(1)} %get-tuple-element.54.weight_ref), custom_call_target="tpu_custom_call" | custom-call | flops 134217728 | tf_op jit(solution)/shard_map/pallas_call | solution.py:387
  35.9 1.2 %shard_map.212 = bf16[16,2048]{1,0:T(8,128)(2,1)S(1)} custom-call(bf16[16,2048]{1,0:T(8,128)(2,1)S(1)} %get-tuple-element.57.gained_ref, bf16[2,2048,1024]{2,1,0:T(8,128)(2,1)S(1)} %get-tuple-element.59.weight_ref), custom_call_target="tpu_custom_call" | custom-call | flops 134217728 | tf_op jit(solution)/shard_map/pallas_call | solution.py:387
  37.3 1.2 %shard_map.211.own_ref = f32[16,2048]{1,0:T(8,128)S(1)} custom-call(bf16[16,2048]{1,0:T(8,128)(2,1)S(1)} %get-tuple-element.57.gained_ref, bf16[2,2048,1024]{2,1,0:T(8,128)(2,1)S(1)} %get-tuple-element.58.weight_ref), custom_call_target="tpu_custom_call" | custom-call | flops 134217728 | tf_op jit(solution)/shard_map/pallas_call | solution.py:387
  38.5 1.6 %collective-permute-done.9.received_ref = bf16[16,2176]{1,0:T(8,128)(2,1)S(1)} collective-permute-done((bf16[16,2176]{1,0:T(8,128)(2,1)S(1)}, bf16[16,2176]{1,0:T(8,128)(2,1)S(1)}, u32[]{:S(2)}, u32[]{:S(2)}) %collective-permute-start.9) | collective-permute-done | bytes 69664 | tf_op jit(solution)/shard_map/ppermute | solution.py:32
  40.6 1.2 %collective-permute-done.10 = f32[16,544]{1,0:T(8,128)S(1)} collective-permute-done((f32[16,544]{1,0:T(8,128)S(1)}, f32[16,544]{1,0:T(8,128)S(1)}, u32[]{:S(2)}, u32[]{:S(2)}) %collective-permute-start.10) | collective-permute-done | bytes 34848 | tf_op jit(solution)/shard_map/ppermute | solution.py:32
  42.8 1.3 %collective-permute-start.12 = (f32[16,544]{1,0:T(8,128)S(1)}, f32[16,544]{1,0:T(8,128)S(1)}, u32[]{:S(2)}, u32[]{:S(2)}) collective-permute-start(f32[16,544]{1,0:T(8,128)S(1)} %add.18.refs_2_), channel_id=1, source_target_pairs={{1,11},{3,9},{5,15},{7,13},{9,3},{11,1},{13,7},{15,5},{0,8},{2,10}... | collective-permute-start | bytes 104456 | tf_op jit(solution)/shard_map/ppermute | solution.py:836
  44.1 2.1 %collective-permute-start.13 = (f32[16,544]{1,0:T(8,128)S(1)}, f32[16,544]{1,0:T(8,128)S(1)}, u32[]{:S(2)}, u32[]{:S(2)}) collective-permute-start(f32[16,544]{1,0:T(8,128)S(1)} %add.18.refs_2_), channel_id=1, source_target_pairs={{1,7},{3,5},{5,3},{7,1},{9,15},{11,13},{13,11},{15,9},{0,4},{2,6},... | collective-permute-start | bytes 104456 | tf_op jit(solution)/shard_map/ppermute | solution.py:836
  47.1 4.8 %shard_map.214 = (bf16[1,1024,2048]{2,1,0:T(8,128)(2,1)S(1)}, bf16[2,1024,2048]{2,1,0:T(8,128)(2,1)S(1)}) custom-call(bf16[4096,2048]{1,0:T(8,128)(2,1)} %refs_0_.7, bf16[4096,2048]{1,0:T(8,128)(2,1)} %refs_0_.7, f32[16,544]{1,0:T(8,128)S(1)} %add.18.refs_2_), custom_call_target="tpu_custom_call" | custom-call | bytes 25165824 | tf_op jit(solution)/shard_map/pallas_call | solution.py:145
  52.0 2.7 %collective-permute-start.15 = (f32[16,544]{1,0:T(8,128)S(1)}, f32[16,544]{1,0:T(8,128)S(1)}, u32[]{:S(2)}, u32[]{:S(2)}) collective-permute-start(f32[16,544]{1,0:T(8,128)S(1)} %add_add_fusion), channel_id=1, source_target_pairs={{0,1},{1,0},{2,3},{3,2},{4,5},{5,4},{6,7},{7,6},{8,9},{9,8},{10,11... | collective-permute-start | bytes 104456 | tf_op jit(solution)/shard_map/ppermute | solution.py:32
  55.6 1.4 %shard_map.215 = (bf16[16,1024]{1,0:T(8,128)(2,1)S(1)}, f32[4,16,1024]{2,1,0:T(8,128)}) custom-call(f32[16,544]{1,0:T(8,128)S(1)} %add.23.mixing_ref, bf16[16,1024]{1,0:T(8,128)(2,1)S(1)} %get-tuple-element.67.conv_ref, bf16[16,1024]{1,0:T(8,128)(2,1)S(1)} %get-tuple-element.68.gate_ref, bf16[512,1024]{1,0:T(8,128)(2,1)S(1)} %copy-done.3, ...), custom_call_target="tpu_custom_call" | custom-call | flops 5000000000 | tf_op jit(solution)/shard_map/pallas_call | solution.py:500
  58.9 2.2 %shard_map.216.refs_4_ = bf16[1,1024,2048]{2,1,0:T(8,128)(2,1)S(1)} custom-call(bf16[4096,2048]{1,0:T(8,128)(2,1)} %refs_0_.7, bf16[16,1024]{1,0:T(8,128)(2,1)S(1)} %get-tuple-element.70.refs_1_.refs_0_), custom_call_target="tpu_custom_call" | custom-call | bytes 8388608 | tf_op jit(solution)/shard_map/pallas_call | solution.py:145
  61.8 1.7 %shard_map.218.refs_0_ = bf16[16,2048]{1,0:T(8,128)(2,1)S(1)} custom-call(bf16[16,1024]{1,0:T(8,128)(2,1)S(1)} %collective-permute-done.16.refs_0_, bf16[16,1024]{1,0:T(8,128)(2,1)S(1)} %collective-permute-done.17.refs_1_, bf16[16,1024]{1,0:T(8,128)(2,1)S(1)} %collective-permute-done.18.refs_2_, ...), custom_call_target="tpu_custom_call" | custom-call | flops 201326592 | tf_op jit(solution)/shard_map/pallas_call | solution.py:534
  63.6 2.3 %collective-permute-start.20 = (bf16[16,2048]{1,0:T(8,128)(2,1)S(1)}, bf16[16,2048]{1,0:T(8,128)(2,1)S(1)}, u32[]{:S(2)}, u32[]{:S(2)}) collective-permute-start(bf16[16,2048]{1,0:T(8,128)(2,1)S(1)} %shard_map.218.refs_0_), channel_id=1, source_target_pairs={{0,8},{4,12},{8,0},{12,4},{1,9},{5,13},{9,1},{13,5},{2,10},{6,14},... | collective-permute-start | bytes 196616 | tf_op jit(solution)/shard_map/ppermute | solution.py:32
  65.9 2.0 %collective-permute-start.21 = (bf16[16,2048]{1,0:T(8,128)(2,1)S(1)}, bf16[16,2048]{1,0:T(8,128)(2,1)S(1)}, u32[]{:S(2)}, u32[]{:S(2)}) collective-permute-start(bf16[16,2048]{1,0:T(8,128)(2,1)S(1)} %shard_map.218.refs_0_), channel_id=1, source_target_pairs={{0,12},{4,8},{8,4},{12,0},{1,13},{5,9},{9,5},{13,1},{2,14},{6,10},... | collective-permute-start | bytes 196616 | tf_op jit(solution)/shard_map/ppermute | solution.py:32
  68.0 1.4 %collective-permute-done.19.refs_1_ = bf16[16,2048]{1,0:T(8,128)(2,1)S(1)} collective-permute-done((bf16[16,2048]{1,0:T(8,128)(2,1)S(1)}, bf16[16,2048]{1,0:T(8,128)(2,1)S(1)}, u32[]{:S(2)}, u32[]{:S(2)}) %collective-permute-start.19) | collective-permute-done | bytes 65568 | tf_op jit(solution)/shard_map/ppermute | solution.py:32
  69.4 2.9 %collective-permute-done.20.refs_2_ = bf16[16,2048]{1,0:T(8,128)(2,1)S(1)} collective-permute-done((bf16[16,2048]{1,0:T(8,128)(2,1)S(1)}, bf16[16,2048]{1,0:T(8,128)(2,1)S(1)}, u32[]{:S(2)}, u32[]{:S(2)}) %collective-permute-start.20) | collective-permute-done | bytes 65568 | tf_op jit(solution)/shard_map/ppermute | solution.py:32
  (62 shorter events, 10.4 us)
Async XLA Ops:
  4.6 13.5 %collective-permute-start = (bf16[272,128]{1,0:T(8,128)(2,1)S(1)}, bf16[272,128]{1,0:T(8,128)(2,1)S(1)}, u32[]{:S(2)}, u32[]{:S(2)}) collective-permute-start(bf16[272,128]{1,0:T(8,128)(2,1)S(1)} %get-tuple-element.40.refs_2_), channel_id=1, source_target_pairs={{0,0},{1,4},{2,8},{3,12},{4,1},{5,5},{6,9},{7,13},{8,2},{9,6},{10,... | collective-permute-start | bytes 208904 | tf_op jit(solution)/shard_map/ppermute | solution.py:794
  5.3 13.6 %collective-permute-start.1 = (bf16[272,128]{1,0:T(8,128)(2,1)S(1)}, bf16[272,128]{1,0:T(8,128)(2,1)S(1)}, u32[]{:S(2)}, u32[]{:S(2)}) collective-permute-start(bf16[272,128]{1,0:T(8,128)(2,1)S(1)} %get-tuple-element.40.refs_2_), channel_id=1, source_target_pairs={{0,2},{1,6},{2,10},{3,14},{4,3},{5,7},{6,11},{7,15},{8,0},{9,4},{1... | collective-permute-start | bytes 208904 | tf_op jit(solution)/shard_map/ppermute | solution.py:794
  18.9 1.3 %collective-permute-start.2 = (bf16[272,128]{1,0:T(8,128)(2,1)S(1)}, bf16[272,128]{1,0:T(8,128)(2,1)S(1)}, u32[]{:S(2)}, u32[]{:S(2)}) collective-permute-start(bf16[272,128]{1,0:T(8,128)(2,1)S(1)} %collective-permute-done.refs_0_), channel_id=1, source_target_pairs={{0,1},{1,0},{2,3},{3,2},{4,5},{5,4},{6,7},{7,6},{8,9},{9,8},{10,11... | collective-permute-start | bytes 208904 | tf_op jit(solution)/shard_map/ppermute | solution.py:32
  18.9 1.4 %collective-permute-start.3 = (bf16[272,128]{1,0:T(8,128)(2,1)S(1)}, bf16[272,128]{1,0:T(8,128)(2,1)S(1)}, u32[]{:S(2)}, u32[]{:S(2)}) collective-permute-start(bf16[272,128]{1,0:T(8,128)(2,1)S(1)} %collective-permute-done.1.refs_1_), channel_id=1, source_target_pairs={{0,1},{1,0},{2,3},{3,2},{4,5},{5,4},{6,7},{7,6},{8,9},{9,8},{10,11... | collective-permute-start | bytes 208904 | tf_op jit(solution)/shard_map/ppermute | solution.py:32
  22.2 10.4 %copy-start = (bf16[4,4,2048]{2,1,0:T(4,128)(2,1)S(1)}, bf16[4,4,2048]{2,1,0:T(4,128)(2,1)}, u32[]{:S(2)}) copy-start(bf16[4,4,2048]{2,1,0:T(4,128)(2,1)} %hidden_ref.1) | copy-start | bytes 196612
  22.2 10.5 %copy-start.1 = (f32[2048]{0:T(1024)S(1)}, f32[2048]{0:T(1024)}, u32[]{:S(2)}) copy-start(f32[2048]{0:T(1024)} %param.28) | copy-start | bytes 24580
  22.2 10.4 %collective-permute-start.4 = (bf16[16,2048]{1,0:T(8,128)(2,1)S(1)}, bf16[16,2048]{1,0:T(8,128)(2,1)S(1)}, u32[]{:S(2)}, u32[]{:S(2)}) collective-permute-start(bf16[16,2048]{1,0:T(8,128)(2,1)S(1)} %shard_map.205.refs_2_.refs_0_), channel_id=1, source_target_pairs={{0,4},{4,0},{8,12},{12,8},{1,5},{5,1},{9,13},{13,9},{2,6},{6,2},{1... | collective-permute-start | bytes 196616 | tf_op jit(solution)/shard_map/ppermute | solution.py:32
  23.8 8.9 %collective-permute-start.5 = (bf16[16,2048]{1,0:T(8,128)(2,1)S(1)}, bf16[16,2048]{1,0:T(8,128)(2,1)S(1)}, u32[]{:S(2)}, u32[]{:S(2)}) collective-permute-start(bf16[16,2048]{1,0:T(8,128)(2,1)S(1)} %shard_map.205.refs_2_.refs_0_), channel_id=1, source_target_pairs={{0,8},{4,12},{8,0},{12,4},{1,9},{5,13},{9,1},{13,5},{2,10},{6,14},... | collective-permute-start | bytes 196616 | tf_op jit(solution)/shard_map/ppermute | solution.py:32
  23.8 8.9 %collective-permute-start.6 = (bf16[16,2048]{1,0:T(8,128)(2,1)S(1)}, bf16[16,2048]{1,0:T(8,128)(2,1)S(1)}, u32[]{:S(2)}, u32[]{:S(2)}) collective-permute-start(bf16[16,2048]{1,0:T(8,128)(2,1)S(1)} %shard_map.205.refs_2_.refs_0_), channel_id=1, source_target_pairs={{0,12},{4,8},{8,4},{12,0},{1,13},{5,9},{9,5},{13,1},{2,14},{6,10},... | collective-permute-start | bytes 196616 | tf_op jit(solution)/shard_map/ppermute | solution.py:32
  34.1 1.3 %collective-permute-start.7 = (bf16[16,2176]{1,0:T(8,128)(2,1)S(1)}, bf16[16,2176]{1,0:T(8,128)(2,1)S(1)}, u32[]{:S(2)}, u32[]{:S(2)}) collective-permute-start(bf16[16,2176]{1,0:T(8,128)(2,1)S(1)} %shard_map.209), channel_id=1, source_target_pairs={{0,1},{1,0},{2,3},{3,2},{4,5},{5,4},{6,7},{7,6},{8,9},{9,8},{10,11... | collective-permute-start | bytes 208904 | tf_op jit(solution)/shard_map/ppermute | solution.py:32
  35.5 4.6 %collective-permute-start.9 = (bf16[16,2176]{1,0:T(8,128)(2,1)S(1)}, bf16[16,2176]{1,0:T(8,128)(2,1)S(1)}, u32[]{:S(2)}, u32[]{:S(2)}) collective-permute-start(bf16[16,2176]{1,0:T(8,128)(2,1)S(1)} %shard_map.210), channel_id=1, source_target_pairs={{0,2},{2,0},{1,3},{3,1},{4,6},{6,4},{5,7},{7,5},{8,10},{10,8},{9,1... | collective-permute-start | bytes 208904 | tf_op jit(solution)/shard_map/ppermute | solution.py:32
  37.1 1.4 %collective-permute-start.8 = (bf16[16,2048]{1,0:T(8,128)(2,1)S(1)}, bf16[16,2048]{1,0:T(8,128)(2,1)S(1)}, u32[]{:S(2)}, u32[]{:S(2)}) collective-permute-start(bf16[16,2048]{1,0:T(8,128)(2,1)S(1)} %shard_map.212), channel_id=1, source_target_pairs={{0,1},{1,0},{2,3},{3,2},{4,5},{5,4},{6,7},{7,6},{8,9},{9,8},{10,11... | collective-permute-start | bytes 196616 | tf_op jit(solution)/shard_map/ppermute | solution.py:32
  40.6 1.2 %collective-permute-start.10 = (f32[16,544]{1,0:T(8,128)S(1)}, f32[16,544]{1,0:T(8,128)S(1)}, u32[]{:S(2)}, u32[]{:S(2)}) collective-permute-start(f32[16,544]{1,0:T(8,128)S(1)} %get-tuple-element.60), channel_id=1, source_target_pairs={{0,1},{1,0},{2,3},{3,2},{4,5},{5,4},{6,7},{7,6},{8,9},{9,8},{10,11... | collective-permute-start | bytes 104456 | tf_op jit(solution)/shard_map/ppermute | solution.py:32
  41.8 10.1 %collective-permute-start.11 = (f32[16,544]{1,0:T(8,128)S(1)}, f32[16,544]{1,0:T(8,128)S(1)}, u32[]{:S(2)}, u32[]{:S(2)}) collective-permute-start(f32[16,544]{1,0:T(8,128)S(1)} %add.18.refs_2_), channel_id=1, source_target_pairs={{1,15},{3,13},{5,11},{7,9},{9,7},{11,5},{13,3},{15,1},{0,12},{2,14... | collective-permute-start | bytes 104456 | tf_op jit(solution)/shard_map/ppermute | solution.py:836
  42.8 9.2 %collective-permute-start.12 = (f32[16,544]{1,0:T(8,128)S(1)}, f32[16,544]{1,0:T(8,128)S(1)}, u32[]{:S(2)}, u32[]{:S(2)}) collective-permute-start(f32[16,544]{1,0:T(8,128)S(1)} %add.18.refs_2_), channel_id=1, source_target_pairs={{1,11},{3,9},{5,15},{7,13},{9,3},{11,1},{13,7},{15,5},{0,8},{2,10}... | collective-permute-start | bytes 104456 | tf_op jit(solution)/shard_map/ppermute | solution.py:836
  44.1 7.9 %collective-permute-start.13 = (f32[16,544]{1,0:T(8,128)S(1)}, f32[16,544]{1,0:T(8,128)S(1)}, u32[]{:S(2)}, u32[]{:S(2)}) collective-permute-start(f32[16,544]{1,0:T(8,128)S(1)} %add.18.refs_2_), channel_id=1, source_target_pairs={{1,7},{3,5},{5,3},{7,1},{9,15},{11,13},{13,11},{15,9},{0,4},{2,6},... | collective-permute-start | bytes 104456 | tf_op jit(solution)/shard_map/ppermute | solution.py:836
  46.2 5.8 %collective-permute-start.14 = (f32[16,544]{1,0:T(8,128)S(1)}, f32[16,544]{1,0:T(8,128)S(1)}, u32[]{:S(2)}, u32[]{:S(2)}) collective-permute-start(f32[16,544]{1,0:T(8,128)S(1)} %add.18.refs_2_), channel_id=1, source_target_pairs={{1,3},{3,1},{5,7},{7,5},{9,11},{11,9},{13,15},{15,13},{17,19},{19,... | collective-permute-start | bytes 104456 | tf_op jit(solution)/shard_map/ppermute | solution.py:836
  52.0 3.6 %collective-permute-start.15 = (f32[16,544]{1,0:T(8,128)S(1)}, f32[16,544]{1,0:T(8,128)S(1)}, u32[]{:S(2)}, u32[]{:S(2)}) collective-permute-start(f32[16,544]{1,0:T(8,128)S(1)} %add_add_fusion), channel_id=1, source_target_pairs={{0,1},{1,0},{2,3},{3,2},{4,5},{5,4},{6,7},{7,6},{8,9},{9,8},{10,11... | collective-permute-start | bytes 104456 | tf_op jit(solution)/shard_map/ppermute | solution.py:32
  57.1 4.7 %collective-permute-start.16 = (bf16[16,1024]{1,0:T(8,128)(2,1)S(1)}, bf16[16,1024]{1,0:T(8,128)(2,1)S(1)}, u32[]{:S(2)}, u32[]{:S(2)}) collective-permute-start(bf16[16,1024]{1,0:T(8,128)(2,1)S(1)} %get-tuple-element.70.refs_1_.refs_0_), channel_id=1, source_target_pairs={{0,1},{1,0},{2,3},{3,2},{4,5},{5,4},{6,7},{7,6},{8,9},{9,8},{10,11... | collective-permute-start | bytes 98312 | tf_op jit(solution)/shard_map/ppermute | solution.py:32
  57.4 4.4 %collective-permute-start.17 = (bf16[16,1024]{1,0:T(8,128)(2,1)S(1)}, bf16[16,1024]{1,0:T(8,128)(2,1)S(1)}, u32[]{:S(2)}, u32[]{:S(2)}) collective-permute-start(bf16[16,1024]{1,0:T(8,128)(2,1)S(1)} %get-tuple-element.70.refs_1_.refs_0_), channel_id=1, source_target_pairs={{0,2},{1,3},{2,0},{3,1},{4,6},{5,7},{6,4},{7,5},{8,10},{9,11},{10,... | collective-permute-start | bytes 98312 | tf_op jit(solution)/shard_map/ppermute | solution.py:32
  57.8 4.1 %collective-permute-start.18 = (bf16[16,1024]{1,0:T(8,128)(2,1)S(1)}, bf16[16,1024]{1,0:T(8,128)(2,1)S(1)}, u32[]{:S(2)}, u32[]{:S(2)}) collective-permute-start(bf16[16,1024]{1,0:T(8,128)(2,1)S(1)} %get-tuple-element.70.refs_1_.refs_0_), channel_id=1, source_target_pairs={{0,3},{1,2},{2,1},{3,0},{4,7},{5,6},{6,5},{7,4},{8,11},{9,10},{10,... | collective-permute-start | bytes 98312 | tf_op jit(solution)/shard_map/ppermute | solution.py:32
  63.6 5.8 %collective-permute-start.19 = (bf16[16,2048]{1,0:T(8,128)(2,1)S(1)}, bf16[16,2048]{1,0:T(8,128)(2,1)S(1)}, u32[]{:S(2)}, u32[]{:S(2)}) collective-permute-start(bf16[16,2048]{1,0:T(8,128)(2,1)S(1)} %shard_map.218.refs_0_), channel_id=1, source_target_pairs={{0,4},{4,0},{8,12},{12,8},{1,5},{5,1},{9,13},{13,9},{2,6},{6,2},{1... | collective-permute-start | bytes 196616 | tf_op jit(solution)/shard_map/ppermute | solution.py:32
  63.6 8.6 %collective-permute-start.20 = (bf16[16,2048]{1,0:T(8,128)(2,1)S(1)}, bf16[16,2048]{1,0:T(8,128)(2,1)S(1)}, u32[]{:S(2)}, u32[]{:S(2)}) collective-permute-start(bf16[16,2048]{1,0:T(8,128)(2,1)S(1)} %shard_map.218.refs_0_), channel_id=1, source_target_pairs={{0,8},{4,12},{8,0},{12,4},{1,9},{5,13},{9,1},{13,5},{2,10},{6,14},... | collective-permute-start | bytes 196616 | tf_op jit(solution)/shard_map/ppermute | solution.py:32
  65.9 6.4 %collective-permute-start.21 = (bf16[16,2048]{1,0:T(8,128)(2,1)S(1)}, bf16[16,2048]{1,0:T(8,128)(2,1)S(1)}, u32[]{:S(2)}, u32[]{:S(2)}) collective-permute-start(bf16[16,2048]{1,0:T(8,128)(2,1)S(1)} %shard_map.218.refs_0_), channel_id=1, source_target_pairs={{0,12},{4,8},{8,4},{12,0},{1,13},{5,9},{9,5},{13,1},{2,14},{6,10},... | collective-permute-start | bytes 196616 | tf_op jit(solution)/shard_map/ppermute | solution.py:32
  (9 other events, 61.2 us)

commit v5 on v4

--- a/solution.py
+++ b/solution.py
@@ -91,17 +91,6 @@
         ]
 
     return weight, (2, weight.shape[1], own_width), views, 2 * PIECES
-
-
-def rows_job(weight, own_width, flips):
-    def views(source, target):
-        pairs = []
-        for place, flip in enumerate(flips):
-            base = pl.multiple_of((hs_position() ^ flip) * own_width, own_width)
-            pairs += in_pieces(source.at[pl.ds(base, own_width)], target.at[place])
-        return pairs
-
-    return weight, (len(flips), own_width, weight.shape[1]), views, len(flips) * PIECES
 
 
 def job_shapes(jobs):
@@ -455,16 +444,16 @@
         in_specs=whole(7 + count),
         out_specs=tuple(whole(3)),
         compiler_params=pltpu.CompilerParams(vmem_limit_bytes=8 * MIB),
-        cost_estimate=cost(FLOPS_AHEAD),
+        cost_estimate=cost(FLOPS_AHEAD//2),
     )(own, near, received, state, taps, bias, weight, *squares)
 
 
-def scan_states(mixing, conv, gate, dt_weight, dt_bias, decay, skip, state, brought):
+def scan_states(mixing, conv, gate, dt_weight, dt_bias, decay, skip, state):
     rows, own_width = conv.shape
     requests, state_width = state.shape[:2]
     low_width = dt_weight.shape[0]
 
-    def kernel(mixing_ref, conv_ref, gate_ref, dt_ref, bias_ref, decay_ref, skip_ref, state_ref, brought_ref, *refs):
+    def kernel(mixing_ref, conv_ref, gate_ref, dt_ref, bias_ref, decay_ref, skip_ref, state_ref, *refs):
         gated_ref, next_ref, out = refs
         low = mixing_ref[:, :low_width]
         low_rank = (low * lax.rsqrt(jnp.mean(low * low, axis=1, keepdims=True) + EPS)).astype(jnp.bfloat16)
@@ -503,30 +492,31 @@
             jax.ShapeDtypeStruct((rows, own_width), jnp.bfloat16),
             jax.ShapeDtypeStruct(state.shape, jnp.float32),
         ),
-        in_specs=whole(8) + [pl.BlockSpec(memory_space=pl.ANY)],
+        in_specs=whole(8),
         out_specs=tuple(whole(2)),
         scratch_shapes=[pltpu.VMEM((rows, own_width), jnp.float32)],
         compiler_params=pltpu.CompilerParams(vmem_limit_bytes=8 * MIB),
-        cost_estimate=cost(FLOPS_AHEAD // 4),
-    )(mixing, conv, gate, dt_weight, dt_bias, decay, skip, state, brought)
-
-
-def project_out(blocks, weights, before):
+        cost_estimate=cost(FLOPS_AHEAD//2),
+    )(mixing, conv, gate, dt_weight, dt_bias, decay, skip, state)
+
+
+def project_out(blocks, flips, weight, before):
     rows, own_width = blocks[0].shape
-    width = weights[0].shape[2]
+    width = weight.shape[1]
     count = len(blocks)
-    end = count + len(weights)
     tile = tile_of(width, 512)
     kind = jnp.float32 if before is None else jnp.bfloat16
-    places = [(k, place) for k, weight in enumerate(weights) for place in range(weight.shape[0])]
 
     def kernel(*refs):
-        block_refs, weight_refs, out_ref = refs[:count], refs[count:end], refs[-1]
+        block_refs, weight_ref, out_ref = refs[:count], refs[count], refs[-1]
         for start in range(0, width, tile):
             columns = slice(start, start + tile)
-            total = None if before is None else refs[end][:, columns]
-            for ref, (k, place) in zip(block_refs, places):
-                term = jnp.dot(ref[...], weight_refs[k][place, :, columns], preferred_element_type=jnp.float32)
+            total = None if before is None else refs[count + 1][:, columns]
+            for ref, flip in zip(block_refs, flips):
+                base = pl.multiple_of((hs_position() ^ flip) * own_width, own_width)
+                term = jnp.dot(
+                    ref[...], weight_ref[pl.ds(base, own_width), columns], preferred_element_type=jnp.float32
+                )
                 total = term if total is None else total + term
             out_ref[:, columns] = total.astype(kind)
 
@@ -534,11 +524,11 @@
     return pl.pallas_call(
         kernel,
         out_shape=jax.ShapeDtypeStruct((rows, width), kind),
-        in_specs=whole(end + len(extra)),
+        in_specs=whole(count + 1 + len(extra)),
         out_specs=whole(1)[0],
         compiler_params=pltpu.CompilerParams(vmem_limit_bytes=4 * MIB),
         cost_estimate=cost(2 * rows * own_width * width * count),
-    )(*blocks, *weights, *extra)
+    )(*blocks, weight, *extra)
 
 
 def finish(residual, parts, requests):
@@ -829,8 +819,6 @@
         features,
     )
     mixing = mixing + crossed(mixing, "sub", 1)
-    mamba_rows = lambda flips: rows_job(mamba_out_weight, own_width, flips)
-    own_rows, other_rows = bring([mamba_rows([0]), mamba_rows([1, 2])], mixing)
     base = lambda s, x, c: s * hs_count + x * 2 + c
     arrived = [
         lax.ppermute(
@@ -841,7 +829,6 @@
         )
         for flip in range(seq_count - 1, -1, -1)
     ]
-    arrived, own_rows, other_rows = lax.optimization_barrier((arrived, own_rows, other_rows))
     line = jnp.where(lax.axis_index("sub") == 0, mixing, 0.0) + paired_sum(arrived)
     mixing = line + crossed(line, "sub", 1)
     gated, state = scan_states(
@@ -853,12 +840,10 @@
         decay_rate.T,
         skip_gain.reshape(1, -1),
         ssm_state.transpose(0, 2, 1),
-        other_rows,
-    )
-    (last_rows,) = bring([mamba_rows([3])], gated)
-    first = project_out([gated], [own_rows], None)
-    blocks, last_rows, first = lax.optimization_barrier((crossed_all(gated, HS), last_rows, first))
-    partial = project_out(blocks[1:], [other_rows, last_rows], first)
+    )
+    first = project_out([gated], [0], mamba_out_weight, None)
+    blocks, first = lax.optimization_barrier((crossed_all(gated, HS), first))
+    partial = project_out(blocks[1:], list(place)[1:], mamba_out_weight, first)
     final = finish(residual, crossed_all(partial, "seq"), requests)
     return final, state.transpose(0, 2, 1)
 

time: 73.2 us -> 70.4 us (0.962)
  Pallas kernels: 35 us -> 28 us
  local copies, waits for them, and re-layouts: 0.06 us -> 2.45 us
  waiting for transfers between devices: 9.84 us -> 12 us
    pallas_call x4 -> x2, Pallas kernels: 19 us -> 12 us  [bring(): pl.pallas_call(kernel, out_shape=tuple(job_shapes(jobs)), in_specs=anywhe...]
    unnamed x22 -> x30, local copies, waits for them, and re-layouts: 0.06 us -> 2.45 us
    ppermute x4, waiting for transfers between devices: 0.01 us -> 1.72 us  [local(): lax.ppermute(mixing, ('seq',) + HS, [(base(s, x, 1), base(s ^ flip, x ^ 1...]
  transfers between devices with their start and end apart: 22 -> 22, of which waited for: 9 -> 12; matrix products, arithmetic and copies ran while one was open for 0% -> 0% of each run, Pallas kernels for 32% -> 23%
where the time goes in v5:
time: 70.4 us; the launch traced here: 70.2 us
  Pallas kernels  28 us (40%)
  starting transfers between devices  26.9 us (38%)
  waiting for transfers between devices  12 us (17%)
  local copies, waits for them, and re-layouts  2.45 us (3%)
  between operations  0.9 us (1%)
    ppermute x16, starting transfers between devices, crossed(): lax.ppermute(value, axes, [(i, i ^ flip) for i in range(lax.axis_size(axe...  14.2 us
    pallas_call x2, Pallas kernels, bring(): pl.pallas_call(kernel, out_shape=tuple(job_shapes(jobs)), in_specs=anywhe...  12 us
    ppermute x16, waiting for transfers between devices, crossed(): lax.ppermute(value, axes, [(i, i ^ flip) for i in range(lax.axis_size(axe...  9.52 us
    ppermute x2, starting transfers between devices, local(): lax.ppermute(part, ('seq',) + HS, [(s * hs_count + j, j * hs_count + (s /...  7.46 us
    ppermute x4, starting transfers between devices, local(): lax.ppermute(mixing, ('seq',) + HS, [(base(s, x, 1), base(s ^ flip, x ^ 1...  5.22 us
    pallas_call x4, Pallas kernels, project_block(): pl.pallas_call(kernel, out_shape=jax.ShapeDtypeStruct((rows, width + (LAN...  4.78 us
    pallas_call x1, Pallas kernels, attention(): pl.pallas_call(kernel, out_shape=tuple([jax.ShapeDtypeStruct((total_rows...  3.98 us
    unnamed x30, local copies, waits for them, and re-layouts  2.45 us
  transfers between devices with their start and end apart: 22, of which 12 were waited for; matrix products, arithmetic and copies ran while one was open for 0% of the time, Pallas kernels for 23%

profile of v5, /device:TPU:0, one launch (start us, length us, event | category | flops | bytes accessed | tf_op | source)
XLA Modules:
  0.0 70.2 jit_solution(6762608089725246829)
XLA Ops:
  0.6 4.0 %shard_map.203 = (bf16[272,128]{1,0:T(8,128)(2,1)S(1)}, bf16[2048,2048]{1,0:T(8,128)(2,1)S(1)}) custom-call(s32[1,4]{1,0:T(1,128)} %bitcast.32, f32[2,2,2,4]{3,2,1,0:T(2,128)} %bitcast.31, bf16[4,64,128]{2,1,0:T(8,128)(2,1)} %bitcast.28, bf16[4,8,128]{2,1,0:T(8,128)(2,1)} %bitcast.29, bf16[4,8,128]{2,1,0:T(8,128)(2,1)} %bitcast.30, ...), custom_call_target="tpu_custom_call" | custom-call | flops 1000000000 | tf_op jit(solution)/shard_map/pallas_call | solution.py:257
  5.3 6.8 %collective-permute-start.1 = (bf16[272,128]{1,0:T(8,128)(2,1)S(1)}, bf16[272,128]{1,0:T(8,128)(2,1)S(1)}, u32[]{:S(2)}, u32[]{:S(2)}) collective-permute-start(bf16[272,128]{1,0:T(8,128)(2,1)S(1)} %get-tuple-element.31.refs_2_), channel_id=1, source_target_pairs={{0,2},{1,6},{2,10},{3,14},{4,3},{5,7},{6,11},{7,15},{8,0},{9,4},{1... | collective-permute-start | bytes 208904 | tf_op jit(solution)/shard_map/ppermute | solution.py:784
  12.1 6.0 %shard_map.204 = (bf16[2,2048,1024]{2,1,0:T(8,128)(2,1)S(1)}, bf16[2,2048,1024]{2,1,0:T(8,128)(2,1)S(1)}) custom-call(bf16[2,2048,4096]{2,1,0:T(8,128)(2,1)} %refs_1_.4, bf16[2,2048,4096]{2,1,0:T(8,128)(2,1)} %refs_1_.4, bf16[272,128]{1,0:T(8,128)(2,1)S(1)} %get-tuple-element.31.refs_2_), custom_call_target="tpu_custom_call" | custom-call | bytes 33554432 | tf_op jit(solution)/shard_map/pallas_call | solution.py:134
  20.3 2.0 %shard_map.205.refs_2_.refs_0_ = bf16[16,2048]{1,0:T(8,128)(2,1)S(1)} custom-call(bf16[272,128]{1,0:T(8,128)(2,1)S(1)} %collective-permute-done.refs_0_, bf16[272,128]{1,0:T(8,128)(2,1)S(1)} %collective-permute-done.1.refs_1_, bf16[272,128]{1,0:T(8,128)(2,1)S(1)} %collective-permute-done.2.refs_2_, bf16[272,128]{1,0:T(8,128)(2,1)S(1)} %collective-permute-done.3.refs_3_, ...), custom_call_target="tpu_custom_call" | custom-call | flops 20000000000 | tf_op jit(solution)/shard_map/pallas_call | solution.py:309
  22.2 1.5 %collective-permute-start.4 = (bf16[16,2048]{1,0:T(8,128)(2,1)S(1)}, bf16[16,2048]{1,0:T(8,128)(2,1)S(1)}, u32[]{:S(2)}, u32[]{:S(2)}) collective-permute-start(bf16[16,2048]{1,0:T(8,128)(2,1)S(1)} %shard_map.205.refs_2_.refs_0_), channel_id=1, source_target_pairs={{0,4},{4,0},{8,12},{12,8},{1,5},{5,1},{9,13},{13,9},{2,6},{6,2},{1... | collective-permute-start | bytes 196616 | tf_op jit(solution)/shard_map/ppermute | solution.py:32
  23.8 2.9 %collective-permute-start.6 = (bf16[16,2048]{1,0:T(8,128)(2,1)S(1)}, bf16[16,2048]{1,0:T(8,128)(2,1)S(1)}, u32[]{:S(2)}, u32[]{:S(2)}) collective-permute-start(bf16[16,2048]{1,0:T(8,128)(2,1)S(1)} %shard_map.205.refs_2_.refs_0_), channel_id=1, source_target_pairs={{0,12},{4,8},{8,4},{12,0},{1,13},{5,9},{9,5},{13,1},{2,14},{6,10},... | collective-permute-start | bytes 196616 | tf_op jit(solution)/shard_map/ppermute | solution.py:32
  26.7 6.0 %shard_map.206 = (bf16[2,2048,1024]{2,1,0:T(8,128)(2,1)S(1)}, bf16[2,2048,1024]{2,1,0:T(8,128)(2,1)S(1)}) custom-call(bf16[2,2048,4096]{2,1,0:T(8,128)(2,1)} %refs_1_.4, bf16[2,2048,4096]{2,1,0:T(8,128)(2,1)} %refs_1_.4, bf16[16,2048]{1,0:T(8,128)(2,1)S(1)} %shard_map.205.refs_2_.refs_0_), custom_call_target="tpu_custom_call" | custom-call | bytes 33554432 | tf_op jit(solution)/shard_map/pallas_call | solution.py:134
  32.9 1.2 %shard_map.209 = bf16[16,2176]{1,0:T(8,128)(2,1)S(1)} custom-call(bf16[16,2048]{1,0:T(8,128)(2,1)S(1)} %get-tuple-element.48.gained_ref, bf16[2,2048,1024]{2,1,0:T(8,128)(2,1)S(1)} %get-tuple-element.46.weight_ref, bf16[16,128]{1,0:T(8,128)(2,1)S(1)} %get-tuple-element.47.refs_0_.stats_ref), custom_call_target="tpu_custom_call" | custom-call | flops 134217728 | tf_op jit(solution)/shard_map/pallas_call | solution.py:376
  34.1 1.2 %shard_map.208.block_ref = f32[16,2048]{1,0:T(8,128)S(1)} custom-call(bf16[16,2048]{1,0:T(8,128)(2,1)S(1)} %get-tuple-element.48.gained_ref, bf16[2,2048,1024]{2,1,0:T(8,128)(2,1)S(1)} %get-tuple-element.45.weight_ref), custom_call_target="tpu_custom_call" | custom-call | flops 134217728 | tf_op jit(solution)/shard_map/pallas_call | solution.py:376
  35.9 1.2 %shard_map.212 = bf16[16,2048]{1,0:T(8,128)(2,1)S(1)} custom-call(bf16[16,2048]{1,0:T(8,128)(2,1)S(1)} %get-tuple-element.48.gained_ref, bf16[2,2048,1024]{2,1,0:T(8,128)(2,1)S(1)} %get-tuple-element.50.weight_ref), custom_call_target="tpu_custom_call" | custom-call | flops 134217728 | tf_op jit(solution)/shard_map/pallas_call | solution.py:376
  37.3 1.2 %shard_map.211.own_ref = f32[16,2048]{1,0:T(8,128)S(1)} custom-call(bf16[16,2048]{1,0:T(8,128)(2,1)S(1)} %get-tuple-element.48.gained_ref, bf16[2,2048,1024]{2,1,0:T(8,128)(2,1)S(1)} %get-tuple-element.49.weight_ref), custom_call_target="tpu_custom_call" | custom-call | flops 134217728 | tf_op jit(solution)/shard_map/pallas_call | solution.py:376
  38.5 1.6 %collective-permute-done.9.received_ref = bf16[16,2176]{1,0:T(8,128)(2,1)S(1)} collective-permute-done((bf16[16,2176]{1,0:T(8,128)(2,1)S(1)}, bf16[16,2176]{1,0:T(8,128)(2,1)S(1)}, u32[]{:S(2)}, u32[]{:S(2)}) %collective-permute-start.9) | collective-permute-done | bytes 69664 | tf_op jit(solution)/shard_map/ppermute | solution.py:32
  40.6 1.2 %collective-permute-done.10 = f32[16,544]{1,0:T(8,128)S(1)} collective-permute-done((f32[16,544]{1,0:T(8,128)S(1)}, f32[16,544]{1,0:T(8,128)S(1)}, u32[]{:S(2)}, u32[]{:S(2)}) %collective-permute-start.10) | collective-permute-done | bytes 34848 | tf_op jit(solution)/shard_map/ppermute | solution.py:32
  41.9 0.9 %collective-permute-start.11 = (f32[16,544]{1,0:T(8,128)S(1)}, f32[16,544]{1,0:T(8,128)S(1)}, u32[]{:S(2)}, u32[]{:S(2)}) collective-permute-start(f32[16,544]{1,0:T(8,128)S(1)} %add.18), channel_id=1, source_target_pairs={{1,15},{3,13},{5,11},{7,9},{9,7},{11,5},{13,3},{15,1},{0,12},{2,14... | collective-permute-start | bytes 104456 | tf_op jit(solution)/shard_map/ppermute | solution.py:824
  42.8 3.4 %collective-permute-start.13 = (f32[16,544]{1,0:T(8,128)S(1)}, f32[16,544]{1,0:T(8,128)S(1)}, u32[]{:S(2)}, u32[]{:S(2)}) collective-permute-start(f32[16,544]{1,0:T(8,128)S(1)} %add.18), channel_id=1, source_target_pairs={{1,11},{3,9},{5,15},{7,13},{9,3},{11,1},{13,7},{15,5},{0,8},{2,10}... | collective-permute-start | bytes 104456 | tf_op jit(solution)/shard_map/ppermute | solution.py:824
  48.9 2.2 %collective-permute-start.15 = (f32[16,544]{1,0:T(8,128)S(1)}, f32[16,544]{1,0:T(8,128)S(1)}, u32[]{:S(2)}, u32[]{:S(2)}) collective-permute-start(f32[16,544]{1,0:T(8,128)S(1)} %add_add_fusion), channel_id=1, source_target_pairs={{0,1},{1,0},{2,3},{3,2},{4,5},{5,4},{6,7},{7,6},{8,9},{9,8},{10,11... | collective-permute-start | bytes 104456 | tf_op jit(solution)/shard_map/ppermute | solution.py:32
  52.0 1.4 %shard_map.214 = (bf16[16,1024]{1,0:T(8,128)(2,1)S(1)}, f32[4,16,1024]{2,1,0:T(8,128)}) custom-call(f32[16,544]{1,0:T(8,128)S(1)} %add.23.mixing_ref, bf16[16,1024]{1,0:T(8,128)(2,1)S(1)} %get-tuple-element.52.conv_ref, bf16[16,1024]{1,0:T(8,128)(2,1)S(1)} %get-tuple-element.53.gate_ref, bf16[512,1024]{1,0:T(8,128)(2,1)S(1)} %copy-done.3, ...), custom_call_target="tpu_custom_call" | custom-call | flops 10000000000 | tf_op jit(solution)/shard_map/pallas_call | solution.py:489
  53.8 1.7 %collective-permute-start.17 = (bf16[16,1024]{1,0:T(8,128)(2,1)S(1)}, bf16[16,1024]{1,0:T(8,128)(2,1)S(1)}, u32[]{:S(2)}, u32[]{:S(2)}) collective-permute-start(bf16[16,1024]{1,0:T(8,128)(2,1)S(1)} %get-tuple-element.54.refs_0_), channel_id=1, source_target_pairs={{0,2},{1,3},{2,0},{3,1},{4,6},{5,7},{6,4},{7,5},{8,10},{9,11},{10,... | collective-permute-start | bytes 98312 | tf_op jit(solution)/shard_map/ppermute | solution.py:32
  55.5 1.2 %slice-done.2 = s8[4194304]{0:T(1024)(128)(4,1)S(1)} async-done(((s8[16777216]{0:T(1024)(128)(4,1)}), s8[4194304]{0:T(1024)(128)(4,1)S(1)}, s32[]{:S(2)}) %slice-start.2) | async-done | bytes 4194328
  56.7 1.2 %slice-done.3 = s8[4194304]{0:T(1024)(128)(4,1)S(1)} async-done(((s8[16777216]{0:T(1024)(128)(4,1)}), s8[4194304]{0:T(1024)(128)(4,1)S(1)}, s32[]{:S(2)}) %slice-start.3) | async-done | bytes 4194328
  59.2 1.7 %shard_map.216.refs_0_ = bf16[16,2048]{1,0:T(8,128)(2,1)S(1)} custom-call(bf16[16,1024]{1,0:T(8,128)(2,1)S(1)} %collective-permute-done.16.refs_0_, bf16[16,1024]{1,0:T(8,128)(2,1)S(1)} %collective-permute-done.17.refs_1_, bf16[16,1024]{1,0:T(8,128)(2,1)S(1)} %collective-permute-done.18.refs_2_, bf16[4096,2048]{1,0:T(8,128)(2,1)S(1)} %bitcast.17, ...), custom_call_target="tpu_custom_call" | custom-call | flops 201326592 | tf_op jit(solution)/shard_map/pallas_call | solution.py:524
  60.9 2.2 %collective-permute-start.20 = (bf16[16,2048]{1,0:T(8,128)(2,1)S(1)}, bf16[16,2048]{1,0:T(8,128)(2,1)S(1)}, u32[]{:S(2)}, u32[]{:S(2)}) collective-permute-start(bf16[16,2048]{1,0:T(8,128)(2,1)S(1)} %shard_map.216.refs_0_), channel_id=1, source_target_pairs={{0,8},{4,12},{8,0},{12,4},{1,9},{5,13},{9,1},{13,5},{2,10},{6,14},... | collective-permute-start | bytes 196616 | tf_op jit(solution)/shard_map/ppermute | solution.py:32
  63.1 2.2 %collective-permute-start.21 = (bf16[16,2048]{1,0:T(8,128)(2,1)S(1)}, bf16[16,2048]{1,0:T(8,128)(2,1)S(1)}, u32[]{:S(2)}, u32[]{:S(2)}) collective-permute-start(bf16[16,2048]{1,0:T(8,128)(2,1)S(1)} %shard_map.216.refs_0_), channel_id=1, source_target_pairs={{0,12},{4,8},{8,4},{12,0},{1,13},{5,9},{9,5},{13,1},{2,14},{6,10},... | collective-permute-start | bytes 196616 | tf_op jit(solution)/shard_map/ppermute | solution.py:32
  66.1 3.4 %collective-permute-done.20.refs_2_ = bf16[16,2048]{1,0:T(8,128)(2,1)S(1)} collective-permute-done((bf16[16,2048]{1,0:T(8,128)(2,1)S(1)}, bf16[16,2048]{1,0:T(8,128)(2,1)S(1)}, u32[]{:S(2)}, u32[]{:S(2)}) %collective-permute-start.20) | collective-permute-done | bytes 65568 | tf_op jit(solution)/shard_map/ppermute | solution.py:32
  (69 shorter events, 10.9 us)
Async XLA Ops:
  4.6 13.5 %collective-permute-start = (bf16[272,128]{1,0:T(8,128)(2,1)S(1)}, bf16[272,128]{1,0:T(8,128)(2,1)S(1)}, u32[]{:S(2)}, u32[]{:S(2)}) collective-permute-start(bf16[272,128]{1,0:T(8,128)(2,1)S(1)} %get-tuple-element.31.refs_2_), channel_id=1, source_target_pairs={{0,0},{1,4},{2,8},{3,12},{4,1},{5,5},{6,9},{7,13},{8,2},{9,6},{10,... | collective-permute-start | bytes 208904 | tf_op jit(solution)/shard_map/ppermute | solution.py:784
  5.3 13.6 %collective-permute-start.1 = (bf16[272,128]{1,0:T(8,128)(2,1)S(1)}, bf16[272,128]{1,0:T(8,128)(2,1)S(1)}, u32[]{:S(2)}, u32[]{:S(2)}) collective-permute-start(bf16[272,128]{1,0:T(8,128)(2,1)S(1)} %get-tuple-element.31.refs_2_), channel_id=1, source_target_pairs={{0,2},{1,6},{2,10},{3,14},{4,3},{5,7},{6,11},{7,15},{8,0},{9,4},{1... | collective-permute-start | bytes 208904 | tf_op jit(solution)/shard_map/ppermute | solution.py:784
  18.9 1.3 %collective-permute-start.2 = (bf16[272,128]{1,0:T(8,128)(2,1)S(1)}, bf16[272,128]{1,0:T(8,128)(2,1)S(1)}, u32[]{:S(2)}, u32[]{:S(2)}) collective-permute-start(bf16[272,128]{1,0:T(8,128)(2,1)S(1)} %collective-permute-done.refs_0_), channel_id=1, source_target_pairs={{0,1},{1,0},{2,3},{3,2},{4,5},{5,4},{6,7},{7,6},{8,9},{9,8},{10,11... | collective-permute-start | bytes 208904 | tf_op jit(solution)/shard_map/ppermute | solution.py:32
  18.9 1.4 %collective-permute-start.3 = (bf16[272,128]{1,0:T(8,128)(2,1)S(1)}, bf16[272,128]{1,0:T(8,128)(2,1)S(1)}, u32[]{:S(2)}, u32[]{:S(2)}) collective-permute-start(bf16[272,128]{1,0:T(8,128)(2,1)S(1)} %collective-permute-done.1.refs_1_), channel_id=1, source_target_pairs={{0,1},{1,0},{2,3},{3,2},{4,5},{5,4},{6,7},{7,6},{8,9},{9,8},{10,11... | collective-permute-start | bytes 208904 | tf_op jit(solution)/shard_map/ppermute | solution.py:32
  22.2 10.4 %collective-permute-start.4 = (bf16[16,2048]{1,0:T(8,128)(2,1)S(1)}, bf16[16,2048]{1,0:T(8,128)(2,1)S(1)}, u32[]{:S(2)}, u32[]{:S(2)}) collective-permute-start(bf16[16,2048]{1,0:T(8,128)(2,1)S(1)} %shard_map.205.refs_2_.refs_0_), channel_id=1, source_target_pairs={{0,4},{4,0},{8,12},{12,8},{1,5},{5,1},{9,13},{13,9},{2,6},{6,2},{1... | collective-permute-start | bytes 196616 | tf_op jit(solution)/shard_map/ppermute | solution.py:32
  23.8 8.9 %collective-permute-start.5 = (bf16[16,2048]{1,0:T(8,128)(2,1)S(1)}, bf16[16,2048]{1,0:T(8,128)(2,1)S(1)}, u32[]{:S(2)}, u32[]{:S(2)}) collective-permute-start(bf16[16,2048]{1,0:T(8,128)(2,1)S(1)} %shard_map.205.refs_2_.refs_0_), channel_id=1, source_target_pairs={{0,8},{4,12},{8,0},{12,4},{1,9},{5,13},{9,1},{13,5},{2,10},{6,14},... | collective-permute-start | bytes 196616 | tf_op jit(solution)/shard_map/ppermute | solution.py:32
  23.8 8.9 %collective-permute-start.6 = (bf16[16,2048]{1,0:T(8,128)(2,1)S(1)}, bf16[16,2048]{1,0:T(8,128)(2,1)S(1)}, u32[]{:S(2)}, u32[]{:S(2)}) collective-permute-start(bf16[16,2048]{1,0:T(8,128)(2,1)S(1)} %shard_map.205.refs_2_.refs_0_), channel_id=1, source_target_pairs={{0,12},{4,8},{8,4},{12,0},{1,13},{5,9},{9,5},{13,1},{2,14},{6,10},... | collective-permute-start | bytes 196616 | tf_op jit(solution)/shard_map/ppermute | solution.py:32
  34.1 1.3 %collective-permute-start.7 = (bf16[16,2176]{1,0:T(8,128)(2,1)S(1)}, bf16[16,2176]{1,0:T(8,128)(2,1)S(1)}, u32[]{:S(2)}, u32[]{:S(2)}) collective-permute-start(bf16[16,2176]{1,0:T(8,128)(2,1)S(1)} %shard_map.209), channel_id=1, source_target_pairs={{0,1},{1,0},{2,3},{3,2},{4,5},{5,4},{6,7},{7,6},{8,9},{9,8},{10,11... | collective-permute-start | bytes 208904 | tf_op jit(solution)/shard_map/ppermute | solution.py:32
  35.5 4.6 %collective-permute-start.9 = (bf16[16,2176]{1,0:T(8,128)(2,1)S(1)}, bf16[16,2176]{1,0:T(8,128)(2,1)S(1)}, u32[]{:S(2)}, u32[]{:S(2)}) collective-permute-start(bf16[16,2176]{1,0:T(8,128)(2,1)S(1)} %shard_map.210), channel_id=1, source_target_pairs={{0,2},{2,0},{1,3},{3,1},{4,6},{6,4},{5,7},{7,5},{8,10},{10,8},{9,1... | collective-permute-start | bytes 208904 | tf_op jit(solution)/shard_map/ppermute | solution.py:32
  37.1 1.4 %collective-permute-start.8 = (bf16[16,2048]{1,0:T(8,128)(2,1)S(1)}, bf16[16,2048]{1,0:T(8,128)(2,1)S(1)}, u32[]{:S(2)}, u32[]{:S(2)}) collective-permute-start(bf16[16,2048]{1,0:T(8,128)(2,1)S(1)} %shard_map.212), channel_id=1, source_target_pairs={{0,1},{1,0},{2,3},{3,2},{4,5},{5,4},{6,7},{7,6},{8,9},{9,8},{10,11... | collective-permute-start | bytes 196616 | tf_op jit(solution)/shard_map/ppermute | solution.py:32
  40.1 11.8 %copy-start.3 = (bf16[512,1024]{1,0:T(8,128)(2,1)S(1)}, bf16[512,1024]{1,0:T(8,128)(2,1)}, u32[]{:S(2)}) copy-start(bf16[512,1024]{1,0:T(8,128)(2,1)} %dt_ref.1) | copy-start | bytes 3145732
  40.1 11.8 %copy-start.4 = (f32[4,1024,16]{1,2,0:T(8,128)S(1)}, f32[4,1024,16]{1,2,0:T(8,128)}, u32[]{:S(2)}) copy-start(f32[4,1024,16]{1,2,0:T(8,128)} %param.38) | copy-start | bytes 786436
  40.6 1.2 %collective-permute-start.10 = (f32[16,544]{1,0:T(8,128)S(1)}, f32[16,544]{1,0:T(8,128)S(1)}, u32[]{:S(2)}, u32[]{:S(2)}) collective-permute-start(f32[16,544]{1,0:T(8,128)S(1)} %get-tuple-element.51), channel_id=1, source_target_pairs={{0,1},{1,0},{2,3},{3,2},{4,5},{5,4},{6,7},{7,6},{8,9},{9,8},{10,11... | collective-permute-start | bytes 104456 | tf_op jit(solution)/shard_map/ppermute | solution.py:32
  41.9 6.0 %collective-permute-start.11 = (f32[16,544]{1,0:T(8,128)S(1)}, f32[16,544]{1,0:T(8,128)S(1)}, u32[]{:S(2)}, u32[]{:S(2)}) collective-permute-start(f32[16,544]{1,0:T(8,128)S(1)} %add.18), channel_id=1, source_target_pairs={{1,15},{3,13},{5,11},{7,9},{9,7},{11,5},{13,3},{15,1},{0,12},{2,14... | collective-permute-start | bytes 104456 | tf_op jit(solution)/shard_map/ppermute | solution.py:824
  42.8 6.0 %collective-permute-start.12 = (f32[16,544]{1,0:T(8,128)S(1)}, f32[16,544]{1,0:T(8,128)S(1)}, u32[]{:S(2)}, u32[]{:S(2)}) collective-permute-start(f32[16,544]{1,0:T(8,128)S(1)} %add.18), channel_id=1, source_target_pairs={{1,7},{3,5},{5,3},{7,1},{9,15},{11,13},{13,11},{15,9},{0,4},{2,6},... | collective-permute-start | bytes 104456 | tf_op jit(solution)/shard_map/ppermute | solution.py:824
  42.8 6.0 %collective-permute-start.13 = (f32[16,544]{1,0:T(8,128)S(1)}, f32[16,544]{1,0:T(8,128)S(1)}, u32[]{:S(2)}, u32[]{:S(2)}) collective-permute-start(f32[16,544]{1,0:T(8,128)S(1)} %add.18), channel_id=1, source_target_pairs={{1,11},{3,9},{5,15},{7,13},{9,3},{11,1},{13,7},{15,5},{0,8},{2,10}... | collective-permute-start | bytes 104456 | tf_op jit(solution)/shard_map/ppermute | solution.py:824
  46.3 2.6 %collective-permute-start.14 = (f32[16,544]{1,0:T(8,128)S(1)}, f32[16,544]{1,0:T(8,128)S(1)}, u32[]{:S(2)}, u32[]{:S(2)}) collective-permute-start(f32[16,544]{1,0:T(8,128)S(1)} %add.18), channel_id=1, source_target_pairs={{1,3},{3,1},{5,7},{7,5},{9,11},{11,9},{13,15},{15,13},{17,19},{19,... | collective-permute-start | bytes 104456 | tf_op jit(solution)/shard_map/ppermute | solution.py:824
  48.9 3.1 %collective-permute-start.15 = (f32[16,544]{1,0:T(8,128)S(1)}, f32[16,544]{1,0:T(8,128)S(1)}, u32[]{:S(2)}, u32[]{:S(2)}) collective-permute-start(f32[16,544]{1,0:T(8,128)S(1)} %add_add_fusion), channel_id=1, source_target_pairs={{0,1},{1,0},{2,3},{3,2},{4,5},{5,4},{6,7},{7,6},{8,9},{9,8},{10,11... | collective-permute-start | bytes 104456 | tf_op jit(solution)/shard_map/ppermute | solution.py:32
  53.5 5.1 %collective-permute-start.16 = (bf16[16,1024]{1,0:T(8,128)(2,1)S(1)}, bf16[16,1024]{1,0:T(8,128)(2,1)S(1)}, u32[]{:S(2)}, u32[]{:S(2)}) collective-permute-start(bf16[16,1024]{1,0:T(8,128)(2,1)S(1)} %get-tuple-element.54.refs_0_), channel_id=1, source_target_pairs={{0,1},{1,0},{2,3},{3,2},{4,5},{5,4},{6,7},{7,6},{8,9},{9,8},{10,11... | collective-permute-start | bytes 98312 | tf_op jit(solution)/shard_map/ppermute | solution.py:32
  53.8 4.7 %collective-permute-start.17 = (bf16[16,1024]{1,0:T(8,128)(2,1)S(1)}, bf16[16,1024]{1,0:T(8,128)(2,1)S(1)}, u32[]{:S(2)}, u32[]{:S(2)}) collective-permute-start(bf16[16,1024]{1,0:T(8,128)(2,1)S(1)} %get-tuple-element.54.refs_0_), channel_id=1, source_target_pairs={{0,2},{1,3},{2,0},{3,1},{4,6},{5,7},{6,4},{7,5},{8,10},{9,11},{10,... | collective-permute-start | bytes 98312 | tf_op jit(solution)/shard_map/ppermute | solution.py:32
  55.5 3.6 %collective-permute-start.18 = (bf16[16,1024]{1,0:T(8,128)(2,1)S(1)}, bf16[16,1024]{1,0:T(8,128)(2,1)S(1)}, u32[]{:S(2)}, u32[]{:S(2)}) collective-permute-start(bf16[16,1024]{1,0:T(8,128)(2,1)S(1)} %get-tuple-element.54.refs_0_), channel_id=1, source_target_pairs={{0,3},{1,2},{2,1},{3,0},{4,7},{5,6},{6,5},{7,4},{8,11},{9,10},{10,... | collective-permute-start | bytes 98312 | tf_op jit(solution)/shard_map/ppermute | solution.py:32
  60.9 5.2 %collective-permute-start.19 = (bf16[16,2048]{1,0:T(8,128)(2,1)S(1)}, bf16[16,2048]{1,0:T(8,128)(2,1)S(1)}, u32[]{:S(2)}, u32[]{:S(2)}) collective-permute-start(bf16[16,2048]{1,0:T(8,128)(2,1)S(1)} %shard_map.216.refs_0_), channel_id=1, source_target_pairs={{0,4},{4,0},{8,12},{12,8},{1,5},{5,1},{9,13},{13,9},{2,6},{6,2},{1... | collective-permute-start | bytes 196616 | tf_op jit(solution)/shard_map/ppermute | solution.py:32
  60.9 8.6 %collective-permute-start.20 = (bf16[16,2048]{1,0:T(8,128)(2,1)S(1)}, bf16[16,2048]{1,0:T(8,128)(2,1)S(1)}, u32[]{:S(2)}, u32[]{:S(2)}) collective-permute-start(bf16[16,2048]{1,0:T(8,128)(2,1)S(1)} %shard_map.216.refs_0_), channel_id=1, source_target_pairs={{0,8},{4,12},{8,0},{12,4},{1,9},{5,13},{9,1},{13,5},{2,10},{6,14},... | collective-permute-start | bytes 196616 | tf_op jit(solution)/shard_map/ppermute | solution.py:32
  63.1 6.3 %collective-permute-start.21 = (bf16[16,2048]{1,0:T(8,128)(2,1)S(1)}, bf16[16,2048]{1,0:T(8,128)(2,1)S(1)}, u32[]{:S(2)}, u32[]{:S(2)}) collective-permute-start(bf16[16,2048]{1,0:T(8,128)(2,1)S(1)} %shard_map.216.refs_0_), channel_id=1, source_target_pairs={{0,12},{4,8},{8,4},{12,0},{1,13},{5,9},{9,5},{13,1},{2,14},{6,10},... | collective-permute-start | bytes 196616 | tf_op jit(solution)/shard_map/ppermute | solution.py:32
  (13 other events, 92.7 us)

commit v6 on v5

--- a/solution.py
+++ b/solution.py
@@ -496,8 +496,25 @@
         out_specs=tuple(whole(2)),
         scratch_shapes=[pltpu.VMEM((rows, own_width), jnp.float32)],
         compiler_params=pltpu.CompilerParams(vmem_limit_bytes=8 * MIB),
-        cost_estimate=cost(FLOPS_AHEAD//2),
+        cost_estimate=cost(FLOPS_AHEAD//4),
     )(mixing, conv, gate, dt_weight, dt_bias, decay, skip, state)
+
+
+def add_up(terms, flops):
+    def kernel(*refs):
+        total = refs[0][...]
+        for ref in refs[1:-1]:
+            total = total + ref[...]
+        refs[-1][...] = total
+
+    return pl.pallas_call(
+        kernel,
+        out_shape=jax.ShapeDtypeStruct(terms[0].shape, terms[0].dtype),
+        in_specs=whole(len(terms)),
+        out_specs=whole(1)[0],
+        compiler_params=pltpu.CompilerParams(vmem_limit_bytes=4 * MIB),
+        cost_estimate=cost(flops),
+    )(*terms)
 
 
 def project_out(blocks, flips, weight, before):
@@ -818,7 +835,7 @@
         xproj_weight.T,
         features,
     )
-    mixing = mixing + crossed(mixing, "sub", 1)
+    mixing = add_up([mixing, crossed(mixing, "sub", 1)], 1_000_000)
     base = lambda s, x, c: s * hs_count + x * 2 + c
     arrived = [
         lax.ppermute(
@@ -829,8 +846,8 @@
         )
         for flip in range(seq_count - 1, -1, -1)
     ]
-    line = jnp.where(lax.axis_index("sub") == 0, mixing, 0.0) + paired_sum(arrived)
-    mixing = line + crossed(line, "sub", 1)
+    line = add_up([jnp.where(lax.axis_index("sub") == 0, mixing, 0.0)] + arrived, FLOPS_AHEAD//4)
+    mixing = add_up([line, crossed(line, "sub", 1)], 1_000_000)
     gated, state = scan_states(
         mixing,
         conv,

time: 70.4 us -> 70.3 us (level)
  waiting for transfers between devices: 12 us -> 14.6 us
  local copies, waits for them, and re-layouts: 2.45 us -> 0.08 us
    unnamed x30, local copies, waits for them, and re-layouts: 2.45 us -> 0.08 us
    ppermute x16, waiting for transfers between devices: 9.52 us -> 11.8 us  [crossed(): lax.ppermute(value, axes, [(i, i ^ flip) for i in range(lax.axis_size(axe...]
  transfers between devices with their start and end apart: 22 -> 22, of which waited for: 12 -> 14; matrix products, arithmetic and copies ran while one was open for 0% -> 0% of each run, Pallas kernels for 23% -> 23%
where the time goes in v6:
time: 70.3 us; the launch traced here: 70.2 us
  Pallas kernels  28 us (40%)
  starting transfers between devices  26.5 us (38%)
  waiting for transfers between devices  14.6 us (21%)
  between operations  0.91 us (1%)
    ppermute x16, starting transfers between devices, crossed(): lax.ppermute(value, axes, [(i, i ^ flip) for i in range(lax.axis_size(axe...  13.7 us
    pallas_call x2, Pallas kernels, bring(): pl.pallas_call(kernel, out_shape=tuple(job_shapes(jobs)), in_specs=anywhe...  12 us
    ppermute x16, waiting for transfers between devices, crossed(): lax.ppermute(value, axes, [(i, i ^ flip) for i in range(lax.axis_size(axe...  11.8 us
    ppermute x2, starting transfers between devices, local(): lax.ppermute(part, ('seq',) + HS, [(s * hs_count + j, j * hs_count + (s /...  7.46 us
    ppermute x4, starting transfers between devices, local(): lax.ppermute(mixing, ('seq',) + HS, [(base(s, x, 1), base(s ^ flip, x ^ 1...  5.28 us
    pallas_call x4, Pallas kernels, project_block(): pl.pallas_call(kernel, out_shape=jax.ShapeDtypeStruct((rows, width + (LAN...  4.78 us
    pallas_call x1, Pallas kernels, attention(): pl.pallas_call(kernel, out_shape=tuple([jax.ShapeDtypeStruct((total_rows...  3.98 us
    pallas_call x2, Pallas kernels, project_out(): pl.pallas_call(kernel, out_shape=jax.ShapeDtypeStruct((rows, width), kind...  2.39 us
  transfers between devices with their start and end apart: 22, of which 14 were waited for; matrix products, arithmetic and copies ran while one was open for 0% of the time, Pallas kernels for 23%

profile of v6, /device:TPU:0, one launch (start us, length us, event | category | flops | bytes accessed | tf_op | source)
XLA Modules:
  0.0 70.2 jit_solution(6563223734894550683)
XLA Ops:
  0.6 4.0 %shard_map.203 = (bf16[272,128]{1,0:T(8,128)(2,1)S(1)}, bf16[2048,2048]{1,0:T(8,128)(2,1)S(1)}) custom-call(s32[1,4]{1,0:T(1,128)} %bitcast.32, f32[2,2,2,4]{3,2,1,0:T(2,128)} %bitcast.31, bf16[4,64,128]{2,1,0:T(8,128)(2,1)} %bitcast.28, bf16[4,8,128]{2,1,0:T(8,128)(2,1)} %bitcast.29, bf16[4,8,128]{2,1,0:T(8,128)(2,1)} %bitcast.30, ...), custom_call_target="tpu_custom_call" | custom-call | flops 1000000000 | tf_op jit(solution)/shard_map/pallas_call | solution.py:257
  5.3 6.8 %collective-permute-start.1 = (bf16[272,128]{1,0:T(8,128)(2,1)S(1)}, bf16[272,128]{1,0:T(8,128)(2,1)S(1)}, u32[]{:S(2)}, u32[]{:S(2)}) collective-permute-start(bf16[272,128]{1,0:T(8,128)(2,1)S(1)} %get-tuple-element.31.refs_2_), channel_id=1, source_target_pairs={{0,2},{1,6},{2,10},{3,14},{4,3},{5,7},{6,11},{7,15},{8,0},{9,4},{1... | collective-permute-start | bytes 208904 | tf_op jit(solution)/shard_map/ppermute | solution.py:801
  12.1 6.0 %shard_map.204 = (bf16[2,2048,1024]{2,1,0:T(8,128)(2,1)S(1)}, bf16[2,2048,1024]{2,1,0:T(8,128)(2,1)S(1)}) custom-call(bf16[2,2048,4096]{2,1,0:T(8,128)(2,1)} %refs_1_.4, bf16[2,2048,4096]{2,1,0:T(8,128)(2,1)} %refs_1_.4, bf16[272,128]{1,0:T(8,128)(2,1)S(1)} %get-tuple-element.31.refs_2_), custom_call_target="tpu_custom_call" | custom-call | bytes 33554432 | tf_op jit(solution)/shard_map/pallas_call | solution.py:134
  20.3 2.0 %shard_map.205.refs_2_.refs_0_ = bf16[16,2048]{1,0:T(8,128)(2,1)S(1)} custom-call(bf16[272,128]{1,0:T(8,128)(2,1)S(1)} %collective-permute-done.refs_0_, bf16[272,128]{1,0:T(8,128)(2,1)S(1)} %collective-permute-done.1.refs_1_, bf16[272,128]{1,0:T(8,128)(2,1)S(1)} %collective-permute-done.2.refs_2_, bf16[272,128]{1,0:T(8,128)(2,1)S(1)} %collective-permute-done.3.refs_3_, ...), custom_call_target="tpu_custom_call" | custom-call | flops 20000000000 | tf_op jit(solution)/shard_map/pallas_call | solution.py:309
  22.2 1.5 %collective-permute-start.4 = (bf16[16,2048]{1,0:T(8,128)(2,1)S(1)}, bf16[16,2048]{1,0:T(8,128)(2,1)S(1)}, u32[]{:S(2)}, u32[]{:S(2)}) collective-permute-start(bf16[16,2048]{1,0:T(8,128)(2,1)S(1)} %shard_map.205.refs_2_.refs_0_), channel_id=1, source_target_pairs={{0,4},{4,0},{8,12},{12,8},{1,5},{5,1},{9,13},{13,9},{2,6},{6,2},{1... | collective-permute-start | bytes 196616 | tf_op jit(solution)/shard_map/ppermute | solution.py:32
  23.8 2.9 %collective-permute-start.6 = (bf16[16,2048]{1,0:T(8,128)(2,1)S(1)}, bf16[16,2048]{1,0:T(8,128)(2,1)S(1)}, u32[]{:S(2)}, u32[]{:S(2)}) collective-permute-start(bf16[16,2048]{1,0:T(8,128)(2,1)S(1)} %shard_map.205.refs_2_.refs_0_), channel_id=1, source_target_pairs={{0,12},{4,8},{8,4},{12,0},{1,13},{5,9},{9,5},{13,1},{2,14},{6,10},... | collective-permute-start | bytes 196616 | tf_op jit(solution)/shard_map/ppermute | solution.py:32
  26.7 6.0 %shard_map.206 = (bf16[2,2048,1024]{2,1,0:T(8,128)(2,1)S(1)}, bf16[2,2048,1024]{2,1,0:T(8,128)(2,1)S(1)}) custom-call(bf16[2,2048,4096]{2,1,0:T(8,128)(2,1)} %refs_1_.4, bf16[2,2048,4096]{2,1,0:T(8,128)(2,1)} %refs_1_.4, bf16[16,2048]{1,0:T(8,128)(2,1)S(1)} %shard_map.205.refs_2_.refs_0_), custom_call_target="tpu_custom_call" | custom-call | bytes 33554432 | tf_op jit(solution)/shard_map/pallas_call | solution.py:134
  32.9 1.2 %shard_map.209 = bf16[16,2176]{1,0:T(8,128)(2,1)S(1)} custom-call(bf16[16,2048]{1,0:T(8,128)(2,1)S(1)} %get-tuple-element.48.gained_ref, bf16[2,2048,1024]{2,1,0:T(8,128)(2,1)S(1)} %get-tuple-element.46.weight_ref, bf16[16,128]{1,0:T(8,128)(2,1)S(1)} %get-tuple-element.47.refs_0_.stats_ref), custom_call_target="tpu_custom_call" | custom-call | flops 134217728 | tf_op jit(solution)/shard_map/pallas_call | solution.py:376
  34.1 1.2 %shard_map.208.block_ref = f32[16,2048]{1,0:T(8,128)S(1)} custom-call(bf16[16,2048]{1,0:T(8,128)(2,1)S(1)} %get-tuple-element.48.gained_ref, bf16[2,2048,1024]{2,1,0:T(8,128)(2,1)S(1)} %get-tuple-element.45.weight_ref), custom_call_target="tpu_custom_call" | custom-call | flops 134217728 | tf_op jit(solution)/shard_map/pallas_call | solution.py:376
  35.9 1.2 %shard_map.212 = bf16[16,2048]{1,0:T(8,128)(2,1)S(1)} custom-call(bf16[16,2048]{1,0:T(8,128)(2,1)S(1)} %get-tuple-element.48.gained_ref, bf16[2,2048,1024]{2,1,0:T(8,128)(2,1)S(1)} %get-tuple-element.50.weight_ref), custom_call_target="tpu_custom_call" | custom-call | flops 134217728 | tf_op jit(solution)/shard_map/pallas_call | solution.py:376
  37.3 1.2 %shard_map.211.own_ref = f32[16,2048]{1,0:T(8,128)S(1)} custom-call(bf16[16,2048]{1,0:T(8,128)(2,1)S(1)} %get-tuple-element.48.gained_ref, bf16[2,2048,1024]{2,1,0:T(8,128)(2,1)S(1)} %get-tuple-element.49.weight_ref), custom_call_target="tpu_custom_call" | custom-call | flops 134217728 | tf_op jit(solution)/shard_map/pallas_call | solution.py:376
  38.5 1.6 %collective-permute-done.9.received_ref = bf16[16,2176]{1,0:T(8,128)(2,1)S(1)} collective-permute-done((bf16[16,2176]{1,0:T(8,128)(2,1)S(1)}, bf16[16,2176]{1,0:T(8,128)(2,1)S(1)}, u32[]{:S(2)}, u32[]{:S(2)}) %collective-permute-start.9) | collective-permute-done | bytes 69664 | tf_op jit(solution)/shard_map/ppermute | solution.py:32
  40.6 1.2 %collective-permute-done.10.refs_1_ = f32[16,544]{1,0:T(8,128)S(1)} collective-permute-done((f32[16,544]{1,0:T(8,128)S(1)}, f32[16,544]{1,0:T(8,128)S(1)}, u32[]{:S(2)}, u32[]{:S(2)}) %collective-permute-start.10) | collective-permute-done | bytes 34848 | tf_op jit(solution)/shard_map/ppermute | solution.py:32
  42.8 1.3 %collective-permute-start.12 = (f32[16,544]{1,0:T(8,128)S(1)}, f32[16,544]{1,0:T(8,128)S(1)}, u32[]{:S(2)}, u32[]{:S(2)}) collective-permute-start(f32[16,544]{1,0:T(8,128)S(1)} %shard_map.214), channel_id=1, source_target_pairs={{1,11},{3,9},{5,15},{7,13},{9,3},{11,1},{13,7},{15,5},{0,8},{2,10}... | collective-permute-start | bytes 104456 | tf_op jit(solution)/shard_map/ppermute | solution.py:841
  44.1 2.1 %collective-permute-start.13 = (f32[16,544]{1,0:T(8,128)S(1)}, f32[16,544]{1,0:T(8,128)S(1)}, u32[]{:S(2)}, u32[]{:S(2)}) collective-permute-start(f32[16,544]{1,0:T(8,128)S(1)} %shard_map.214), channel_id=1, source_target_pairs={{1,7},{3,5},{5,3},{7,1},{9,15},{11,13},{13,11},{15,9},{0,4},{2,6},... | collective-permute-start | bytes 104456 | tf_op jit(solution)/shard_map/ppermute | solution.py:841
  49.3 1.8 %collective-permute-start.15 = (f32[16,544]{1,0:T(8,128)S(1)}, f32[16,544]{1,0:T(8,128)S(1)}, u32[]{:S(2)}, u32[]{:S(2)}) collective-permute-start(f32[16,544]{1,0:T(8,128)S(1)} %shard_map.215.refs_0_), channel_id=1, source_target_pairs={{0,1},{1,0},{2,3},{3,2},{4,5},{5,4},{6,7},{7,6},{8,9},{9,8},{10,11... | collective-permute-start | bytes 104456 | tf_op jit(solution)/shard_map/ppermute | solution.py:32
  52.0 1.4 %shard_map.217 = (bf16[16,1024]{1,0:T(8,128)(2,1)S(1)}, f32[4,16,1024]{2,1,0:T(8,128)}) custom-call(f32[16,544]{1,0:T(8,128)S(1)} %shard_map.216.mixing_ref, bf16[16,1024]{1,0:T(8,128)(2,1)S(1)} %get-tuple-element.52.conv_ref, bf16[16,1024]{1,0:T(8,128)(2,1)S(1)} %get-tuple-element.53.gate_ref, bf16[512,1024]{1,0:T(8,128)(2,1)S(1)} %copy-done.3, ...), custom_call_target="tpu_custom_call" | custom-call | flops 5000000000 | tf_op jit(solution)/shard_map/pallas_call | solution.py:489
  53.8 1.7 %collective-permute-start.17 = (bf16[16,1024]{1,0:T(8,128)(2,1)S(1)}, bf16[16,1024]{1,0:T(8,128)(2,1)S(1)}, u32[]{:S(2)}, u32[]{:S(2)}) collective-permute-start(bf16[16,1024]{1,0:T(8,128)(2,1)S(1)} %get-tuple-element.54.refs_0_), channel_id=1, source_target_pairs={{0,2},{1,3},{2,0},{3,1},{4,6},{5,7},{6,4},{7,5},{8,10},{9,11},{10,... | collective-permute-start | bytes 98312 | tf_op jit(solution)/shard_map/ppermute | solution.py:32
  56.2 1.5 %collective-permute-done.17.refs_1_ = bf16[16,1024]{1,0:T(8,128)(2,1)S(1)} collective-permute-done((bf16[16,1024]{1,0:T(8,128)(2,1)S(1)}, bf16[16,1024]{1,0:T(8,128)(2,1)S(1)}, u32[]{:S(2)}, u32[]{:S(2)}) %collective-permute-start.17) | collective-permute-done | bytes 32800 | tf_op jit(solution)/shard_map/ppermute | solution.py:32
  57.7 1.4 %collective-permute-done.18.refs_2_ = bf16[16,1024]{1,0:T(8,128)(2,1)S(1)} collective-permute-done((bf16[16,1024]{1,0:T(8,128)(2,1)S(1)}, bf16[16,1024]{1,0:T(8,128)(2,1)S(1)}, u32[]{:S(2)}, u32[]{:S(2)}) %collective-permute-start.18) | collective-permute-done | bytes 32800 | tf_op jit(solution)/shard_map/ppermute | solution.py:32
  59.1 1.7 %shard_map.219.refs_0_ = bf16[16,2048]{1,0:T(8,128)(2,1)S(1)} custom-call(bf16[16,1024]{1,0:T(8,128)(2,1)S(1)} %collective-permute-done.16.refs_0_, bf16[16,1024]{1,0:T(8,128)(2,1)S(1)} %collective-permute-done.17.refs_1_, bf16[16,1024]{1,0:T(8,128)(2,1)S(1)} %collective-permute-done.18.refs_2_, bf16[4096,2048]{1,0:T(8,128)(2,1)S(1)} %bitcast.17, ...), custom_call_target="tpu_custom_call" | custom-call | flops 201326592 | tf_op jit(solution)/shard_map/pallas_call | solution.py:541
  60.8 1.6 %collective-permute-start.20 = (bf16[16,2048]{1,0:T(8,128)(2,1)S(1)}, bf16[16,2048]{1,0:T(8,128)(2,1)S(1)}, u32[]{:S(2)}, u32[]{:S(2)}) collective-permute-start(bf16[16,2048]{1,0:T(8,128)(2,1)S(1)} %shard_map.219.refs_0_), channel_id=1, source_target_pairs={{0,8},{4,12},{8,0},{12,4},{1,9},{5,13},{9,1},{13,5},{2,10},{6,14},... | collective-permute-start | bytes 196616 | tf_op jit(solution)/shard_map/ppermute | solution.py:32
  62.4 2.8 %collective-permute-start.21 = (bf16[16,2048]{1,0:T(8,128)(2,1)S(1)}, bf16[16,2048]{1,0:T(8,128)(2,1)S(1)}, u32[]{:S(2)}, u32[]{:S(2)}) collective-permute-start(bf16[16,2048]{1,0:T(8,128)(2,1)S(1)} %shard_map.219.refs_0_), channel_id=1, source_target_pairs={{0,12},{4,8},{8,4},{12,0},{1,13},{5,9},{9,5},{13,1},{2,14},{6,10},... | collective-permute-start | bytes 196616 | tf_op jit(solution)/shard_map/ppermute | solution.py:32
  66.0 3.4 %collective-permute-done.20.refs_2_ = bf16[16,2048]{1,0:T(8,128)(2,1)S(1)} collective-permute-done((bf16[16,2048]{1,0:T(8,128)(2,1)S(1)}, bf16[16,2048]{1,0:T(8,128)(2,1)S(1)}, u32[]{:S(2)}, u32[]{:S(2)}) %collective-permute-start.20) | collective-permute-done | bytes 65568 | tf_op jit(solution)/shard_map/ppermute | solution.py:32
  (70 shorter events, 11.7 us)
Async XLA Ops:
  4.6 13.5 %collective-permute-start = (bf16[272,128]{1,0:T(8,128)(2,1)S(1)}, bf16[272,128]{1,0:T(8,128)(2,1)S(1)}, u32[]{:S(2)}, u32[]{:S(2)}) collective-permute-start(bf16[272,128]{1,0:T(8,128)(2,1)S(1)} %get-tuple-element.31.refs_2_), channel_id=1, source_target_pairs={{0,0},{1,4},{2,8},{3,12},{4,1},{5,5},{6,9},{7,13},{8,2},{9,6},{10,... | collective-permute-start | bytes 208904 | tf_op jit(solution)/shard_map/ppermute | solution.py:801
  5.3 13.6 %collective-permute-start.1 = (bf16[272,128]{1,0:T(8,128)(2,1)S(1)}, bf16[272,128]{1,0:T(8,128)(2,1)S(1)}, u32[]{:S(2)}, u32[]{:S(2)}) collective-permute-start(bf16[272,128]{1,0:T(8,128)(2,1)S(1)} %get-tuple-element.31.refs_2_), channel_id=1, source_target_pairs={{0,2},{1,6},{2,10},{3,14},{4,3},{5,7},{6,11},{7,15},{8,0},{9,4},{1... | collective-permute-start | bytes 208904 | tf_op jit(solution)/shard_map/ppermute | solution.py:801
  18.9 1.3 %collective-permute-start.2 = (bf16[272,128]{1,0:T(8,128)(2,1)S(1)}, bf16[272,128]{1,0:T(8,128)(2,1)S(1)}, u32[]{:S(2)}, u32[]{:S(2)}) collective-permute-start(bf16[272,128]{1,0:T(8,128)(2,1)S(1)} %collective-permute-done.refs_0_), channel_id=1, source_target_pairs={{0,1},{1,0},{2,3},{3,2},{4,5},{5,4},{6,7},{7,6},{8,9},{9,8},{10,11... | collective-permute-start | bytes 208904 | tf_op jit(solution)/shard_map/ppermute | solution.py:32
  18.9 1.4 %collective-permute-start.3 = (bf16[272,128]{1,0:T(8,128)(2,1)S(1)}, bf16[272,128]{1,0:T(8,128)(2,1)S(1)}, u32[]{:S(2)}, u32[]{:S(2)}) collective-permute-start(bf16[272,128]{1,0:T(8,128)(2,1)S(1)} %collective-permute-done.1.refs_1_), channel_id=1, source_target_pairs={{0,1},{1,0},{2,3},{3,2},{4,5},{5,4},{6,7},{7,6},{8,9},{9,8},{10,11... | collective-permute-start | bytes 208904 | tf_op jit(solution)/shard_map/ppermute | solution.py:32
  22.2 10.4 %copy-start = (bf16[4,4,2048]{2,1,0:T(4,128)(2,1)S(1)}, bf16[4,4,2048]{2,1,0:T(4,128)(2,1)}, u32[]{:S(2)}) copy-start(bf16[4,4,2048]{2,1,0:T(4,128)(2,1)} %hidden_ref.1) | copy-start | bytes 196612
  22.2 10.5 %copy-start.1 = (f32[2048]{0:T(1024)S(1)}, f32[2048]{0:T(1024)}, u32[]{:S(2)}) copy-start(f32[2048]{0:T(1024)} %param.28) | copy-start | bytes 24580
  22.2 10.4 %collective-permute-start.4 = (bf16[16,2048]{1,0:T(8,128)(2,1)S(1)}, bf16[16,2048]{1,0:T(8,128)(2,1)S(1)}, u32[]{:S(2)}, u32[]{:S(2)}) collective-permute-start(bf16[16,2048]{1,0:T(8,128)(2,1)S(1)} %shard_map.205.refs_2_.refs_0_), channel_id=1, source_target_pairs={{0,4},{4,0},{8,12},{12,8},{1,5},{5,1},{9,13},{13,9},{2,6},{6,2},{1... | collective-permute-start | bytes 196616 | tf_op jit(solution)/shard_map/ppermute | solution.py:32
  23.8 8.9 %collective-permute-start.5 = (bf16[16,2048]{1,0:T(8,128)(2,1)S(1)}, bf16[16,2048]{1,0:T(8,128)(2,1)S(1)}, u32[]{:S(2)}, u32[]{:S(2)}) collective-permute-start(bf16[16,2048]{1,0:T(8,128)(2,1)S(1)} %shard_map.205.refs_2_.refs_0_), channel_id=1, source_target_pairs={{0,8},{4,12},{8,0},{12,4},{1,9},{5,13},{9,1},{13,5},{2,10},{6,14},... | collective-permute-start | bytes 196616 | tf_op jit(solution)/shard_map/ppermute | solution.py:32
  23.8 8.9 %collective-permute-start.6 = (bf16[16,2048]{1,0:T(8,128)(2,1)S(1)}, bf16[16,2048]{1,0:T(8,128)(2,1)S(1)}, u32[]{:S(2)}, u32[]{:S(2)}) collective-permute-start(bf16[16,2048]{1,0:T(8,128)(2,1)S(1)} %shard_map.205.refs_2_.refs_0_), channel_id=1, source_target_pairs={{0,12},{4,8},{8,4},{12,0},{1,13},{5,9},{9,5},{13,1},{2,14},{6,10},... | collective-permute-start | bytes 196616 | tf_op jit(solution)/shard_map/ppermute | solution.py:32
  34.1 1.3 %collective-permute-start.7 = (bf16[16,2176]{1,0:T(8,128)(2,1)S(1)}, bf16[16,2176]{1,0:T(8,128)(2,1)S(1)}, u32[]{:S(2)}, u32[]{:S(2)}) collective-permute-start(bf16[16,2176]{1,0:T(8,128)(2,1)S(1)} %shard_map.209), channel_id=1, source_target_pairs={{0,1},{1,0},{2,3},{3,2},{4,5},{5,4},{6,7},{7,6},{8,9},{9,8},{10,11... | collective-permute-start | bytes 208904 | tf_op jit(solution)/shard_map/ppermute | solution.py:32
  35.5 4.6 %collective-permute-start.9 = (bf16[16,2176]{1,0:T(8,128)(2,1)S(1)}, bf16[16,2176]{1,0:T(8,128)(2,1)S(1)}, u32[]{:S(2)}, u32[]{:S(2)}) collective-permute-start(bf16[16,2176]{1,0:T(8,128)(2,1)S(1)} %shard_map.210), channel_id=1, source_target_pairs={{0,2},{2,0},{1,3},{3,1},{4,6},{6,4},{5,7},{7,5},{8,10},{10,8},{9,1... | collective-permute-start | bytes 208904 | tf_op jit(solution)/shard_map/ppermute | solution.py:32
  37.1 1.4 %collective-permute-start.8 = (bf16[16,2048]{1,0:T(8,128)(2,1)S(1)}, bf16[16,2048]{1,0:T(8,128)(2,1)S(1)}, u32[]{:S(2)}, u32[]{:S(2)}) collective-permute-start(bf16[16,2048]{1,0:T(8,128)(2,1)S(1)} %shard_map.212), channel_id=1, source_target_pairs={{0,1},{1,0},{2,3},{3,2},{4,5},{5,4},{6,7},{7,6},{8,9},{9,8},{10,11... | collective-permute-start | bytes 196616 | tf_op jit(solution)/shard_map/ppermute | solution.py:32
  40.6 1.2 %collective-permute-start.10 = (f32[16,544]{1,0:T(8,128)S(1)}, f32[16,544]{1,0:T(8,128)S(1)}, u32[]{:S(2)}, u32[]{:S(2)}) collective-permute-start(f32[16,544]{1,0:T(8,128)S(1)} %get-tuple-element.51.refs_0_), channel_id=1, source_target_pairs={{0,1},{1,0},{2,3},{3,2},{4,5},{5,4},{6,7},{7,6},{8,9},{9,8},{10,11... | collective-permute-start | bytes 104456 | tf_op jit(solution)/shard_map/ppermute | solution.py:32
  41.8 6.0 %collective-permute-start.11 = (f32[16,544]{1,0:T(8,128)S(1)}, f32[16,544]{1,0:T(8,128)S(1)}, u32[]{:S(2)}, u32[]{:S(2)}) collective-permute-start(f32[16,544]{1,0:T(8,128)S(1)} %shard_map.214), channel_id=1, source_target_pairs={{1,15},{3,13},{5,11},{7,9},{9,7},{11,5},{13,3},{15,1},{0,12},{2,14... | collective-permute-start | bytes 104456 | tf_op jit(solution)/shard_map/ppermute | solution.py:841
  42.8 6.0 %collective-permute-start.12 = (f32[16,544]{1,0:T(8,128)S(1)}, f32[16,544]{1,0:T(8,128)S(1)}, u32[]{:S(2)}, u32[]{:S(2)}) collective-permute-start(f32[16,544]{1,0:T(8,128)S(1)} %shard_map.214), channel_id=1, source_target_pairs={{1,11},{3,9},{5,15},{7,13},{9,3},{11,1},{13,7},{15,5},{0,8},{2,10}... | collective-permute-start | bytes 104456 | tf_op jit(solution)/shard_map/ppermute | solution.py:841
  44.1 5.1 %collective-permute-start.13 = (f32[16,544]{1,0:T(8,128)S(1)}, f32[16,544]{1,0:T(8,128)S(1)}, u32[]{:S(2)}, u32[]{:S(2)}) collective-permute-start(f32[16,544]{1,0:T(8,128)S(1)} %shard_map.214), channel_id=1, source_target_pairs={{1,7},{3,5},{5,3},{7,1},{9,15},{11,13},{13,11},{15,9},{0,4},{2,6},... | collective-permute-start | bytes 104456 | tf_op jit(solution)/shard_map/ppermute | solution.py:841
  46.3 3.0 %collective-permute-start.14 = (f32[16,544]{1,0:T(8,128)S(1)}, f32[16,544]{1,0:T(8,128)S(1)}, u32[]{:S(2)}, u32[]{:S(2)}) collective-permute-start(f32[16,544]{1,0:T(8,128)S(1)} %shard_map.214), channel_id=1, source_target_pairs={{1,3},{3,1},{5,7},{7,5},{9,11},{11,9},{13,15},{15,13},{17,19},{19,... | collective-permute-start | bytes 104456 | tf_op jit(solution)/shard_map/ppermute | solution.py:841
  49.3 2.6 %collective-permute-start.15 = (f32[16,544]{1,0:T(8,128)S(1)}, f32[16,544]{1,0:T(8,128)S(1)}, u32[]{:S(2)}, u32[]{:S(2)}) collective-permute-start(f32[16,544]{1,0:T(8,128)S(1)} %shard_map.215.refs_0_), channel_id=1, source_target_pairs={{0,1},{1,0},{2,3},{3,2},{4,5},{5,4},{6,7},{7,6},{8,9},{9,8},{10,11... | collective-permute-start | bytes 104456 | tf_op jit(solution)/shard_map/ppermute | solution.py:32
  53.4 2.7 %collective-permute-start.16 = (bf16[16,1024]{1,0:T(8,128)(2,1)S(1)}, bf16[16,1024]{1,0:T(8,128)(2,1)S(1)}, u32[]{:S(2)}, u32[]{:S(2)}) collective-permute-start(bf16[16,1024]{1,0:T(8,128)(2,1)S(1)} %get-tuple-element.54.refs_0_), channel_id=1, source_target_pairs={{0,1},{1,0},{2,3},{3,2},{4,5},{5,4},{6,7},{7,6},{8,9},{9,8},{10,11... | collective-permute-start | bytes 98312 | tf_op jit(solution)/shard_map/ppermute | solution.py:32
  53.8 3.9 %collective-permute-start.17 = (bf16[16,1024]{1,0:T(8,128)(2,1)S(1)}, bf16[16,1024]{1,0:T(8,128)(2,1)S(1)}, u32[]{:S(2)}, u32[]{:S(2)}) collective-permute-start(bf16[16,1024]{1,0:T(8,128)(2,1)S(1)} %get-tuple-element.54.refs_0_), channel_id=1, source_target_pairs={{0,2},{1,3},{2,0},{3,1},{4,6},{5,7},{6,4},{7,5},{8,10},{9,11},{10,... | collective-permute-start | bytes 98312 | tf_op jit(solution)/shard_map/ppermute | solution.py:32
  55.5 3.6 %collective-permute-start.18 = (bf16[16,1024]{1,0:T(8,128)(2,1)S(1)}, bf16[16,1024]{1,0:T(8,128)(2,1)S(1)}, u32[]{:S(2)}, u32[]{:S(2)}) collective-permute-start(bf16[16,1024]{1,0:T(8,128)(2,1)S(1)} %get-tuple-element.54.refs_0_), channel_id=1, source_target_pairs={{0,3},{1,2},{2,1},{3,0},{4,7},{5,6},{6,5},{7,4},{8,11},{9,10},{10,... | collective-permute-start | bytes 98312 | tf_op jit(solution)/shard_map/ppermute | solution.py:32
  60.8 5.2 %collective-permute-start.19 = (bf16[16,2048]{1,0:T(8,128)(2,1)S(1)}, bf16[16,2048]{1,0:T(8,128)(2,1)S(1)}, u32[]{:S(2)}, u32[]{:S(2)}) collective-permute-start(bf16[16,2048]{1,0:T(8,128)(2,1)S(1)} %shard_map.219.refs_0_), channel_id=1, source_target_pairs={{0,4},{4,0},{8,12},{12,8},{1,5},{5,1},{9,13},{13,9},{2,6},{6,2},{1... | collective-permute-start | bytes 196616 | tf_op jit(solution)/shard_map/ppermute | solution.py:32
  60.8 8.6 %collective-permute-start.20 = (bf16[16,2048]{1,0:T(8,128)(2,1)S(1)}, bf16[16,2048]{1,0:T(8,128)(2,1)S(1)}, u32[]{:S(2)}, u32[]{:S(2)}) collective-permute-start(bf16[16,2048]{1,0:T(8,128)(2,1)S(1)} %shard_map.219.refs_0_), channel_id=1, source_target_pairs={{0,8},{4,12},{8,0},{12,4},{1,9},{5,13},{9,1},{13,5},{2,10},{6,14},... | collective-permute-start | bytes 196616 | tf_op jit(solution)/shard_map/ppermute | solution.py:32
  62.4 7.0 %collective-permute-start.21 = (bf16[16,2048]{1,0:T(8,128)(2,1)S(1)}, bf16[16,2048]{1,0:T(8,128)(2,1)S(1)}, u32[]{:S(2)}, u32[]{:S(2)}) collective-permute-start(bf16[16,2048]{1,0:T(8,128)(2,1)S(1)} %shard_map.219.refs_0_), channel_id=1, source_target_pairs={{0,12},{4,8},{8,4},{12,0},{1,13},{5,9},{9,5},{13,1},{2,14},{6,10},... | collective-permute-start | bytes 196616 | tf_op jit(solution)/shard_map/ppermute | solution.py:32
  (13 other events, 64.8 us)
